TPU v7x, 32 devices: a whole 2x2x4 slice. The times are simulated.
32 devices in a mesh: dp: 8 (over z, x), fsdp: 4 (over y, core).
Axes of the slice: x: 2, y: 2, z: 4, core: 2. Of those that a mesh axis runs over, the one named last changes fastest.
Arguments:
- patches: bfloat16 [128, 153, 768], P(('dp', 'fsdp')), may hold values from -6 to 6
- counts: int32 [128], P(('dp', 'fsdp')), may hold values from 26 to 153, as said below
- positions: int32 [128, 153], P(('dp', 'fsdp')), may hold values from 0 to 255, as said below
- ln1_gain: bfloat16 [768], P(('dp', 'fsdp')), may hold values from 0.5 to 1.5
- ln1_bias: bfloat16 [768], P(('dp', 'fsdp')), may hold values from -1 to 1
- qkv_weight: bfloat16 [768, 2304], P(('dp', 'fsdp')), may hold values from -0.21875 to 0.21875
- qv_bias: bfloat16 [1536], P(('dp', 'fsdp')), may hold values from -1.5 to 1.5
- out_weight: bfloat16 [768, 768], P(('dp', 'fsdp')), may hold values from -0.625 to 0.625
- out_bias: bfloat16 [768], P(('dp', 'fsdp')), may hold values from -1 to 1
- ln2_gain: bfloat16 [768], P(('dp', 'fsdp')), may hold values from 0.5 to 1.5
- ln2_bias: bfloat16 [768], P(('dp', 'fsdp')), may hold values from -1 to 1
- fc1_weight: bfloat16 [768, 3072], P(('dp', 'fsdp')), may hold values from -0.21875 to 0.21875
- fc1_bias: bfloat16 [3072], P(('dp', 'fsdp')), may hold values from -1.5 to 1.5
- fc2_weight: bfloat16 [3072, 768], P(('dp', 'fsdp')), may hold values from -0.109375 to 0.109375
- fc2_bias: bfloat16 [768], P(('dp', 'fsdp')), may hold values from -1 to 1
- cotangent: bfloat16 [128, 153, 768], P(('dp', 'fsdp')), may hold values from -6 to 6
Outputs:
- output: bfloat16 [128, 153, 768], P(('dp', 'fsdp'))
- input_grad: bfloat16 [128, 153, 768], P(('dp', 'fsdp'))
- ln1_gain_grad: float32 [768], P(('dp', 'fsdp'))
- ln1_bias_grad: float32 [768], P(('dp', 'fsdp'))
- qkv_weight_grad: float32 [768, 2304], P(('dp', 'fsdp'))
- qv_bias_grad: float32 [1536], P(('dp', 'fsdp'))
- out_weight_grad: float32 [768, 768], P(('dp', 'fsdp'))
- out_bias_grad: float32 [768], P(('dp', 'fsdp'))
- ln2_gain_grad: float32 [768], P(('dp', 'fsdp'))
- ln2_bias_grad: float32 [768], P(('dp', 'fsdp'))
- fc1_weight_grad: float32 [768, 3072], P(('dp', 'fsdp'))
- fc1_bias_grad: float32 [3072], P(('dp', 'fsdp'))
- fc2_weight_grad: float32 [3072, 768], P(('dp', 'fsdp'))
- fc2_bias_grad: float32 [768], P(('dp', 'fsdp'))
Inputs may be any that keep to these rules, and one draw needn't show every extreme that they name: `counts`: rows at and beyond an image's count are padding; some image has exactly 153. `positions`: row index times 16 plus column index of the patch on the image's grid, distinct within an image; padding rows hold some grid index too.
All inputs are finite; a program needn't handle non-finite values.
Results may differ from a plain program's by a relative error of at most 0.012.
Values may be sent and summed in bfloat16 or wider, within the bound.
No kernel may reach another device: no remote copies, remote signals or barrier semaphores. Data moves between devices by JAX's collectives and lax.ppermute only.
A program may use at most 192 MiB of HBM per device.

v0:
```python
import math

import jax
import jax.numpy as jnp
from jax import lax
from jax.sharding import PartitionSpec as P

HEADS = 12
SIDE = 16


EPSILON = 1e-06


def power_slopes(number):
    first_slope = 2.0 ** (-8.0 / number)
    return [first_slope ** (index + 1) for index in range(number)]


def slope_list(heads_total):
    lower_power = 2 ** int(math.floor(math.log2(heads_total)))
    return (
        power_slopes(lower_power) + power_slopes(2 * lower_power)[0::2][: heads_total - lower_power]
    )


def alibi_table(positions, heads_total, side_count):
    grid_rows = (positions // side_count).astype(jnp.float32)
    grid_cols = (positions % side_count).astype(jnp.float32)
    row_delta = grid_rows[:, :, None] - grid_rows[:, None, :]
    col_delta = grid_cols[:, :, None] - grid_cols[:, None, :]
    distance = jnp.sqrt(row_delta * row_delta + col_delta * col_delta)
    slopes = jnp.array(slope_list(heads_total), jnp.float32)
    return -slopes[None, :, None, None] * distance[:, None, :, :]


def gelu_exact(values):
    return jax.nn.gelu(values, approximate=False)


def norm_parts(values, gain, shift):
    center = jnp.mean(values, axis=-1, keepdims=True)
    centered = values - center
    scale = lax.rsqrt(jnp.mean(centered * centered, axis=-1, keepdims=True) + EPSILON)
    normed = centered * scale
    return (normed * gain + shift, normed, scale)


def norm_back(grad_out, normed, scale, gain):
    grad_normed = grad_out * gain
    centered_mean = jnp.mean(grad_normed, axis=-1, keepdims=True)
    projected_mean = jnp.mean(grad_normed * normed, axis=-1, keepdims=True)
    return scale * (grad_normed - centered_mean - normed * projected_mean)


def run_forward(patches, valid_rows, key_mask, alibi_bias, attn_set, mlp_set):
    ln1_gain, ln1_bias, qkv_weight, qv_bias, out_weight, out_bias = attn_set
    ln2_gain, ln2_bias, fc1_weight, fc1_bias, fc2_weight, fc2_bias = mlp_set
    images, length, width = patches.shape
    head_dim = width // HEADS
    inputs = patches.astype(jnp.float32).reshape(images * length, width)
    first_norm, normed_one, scale_one = norm_parts(
        inputs, ln1_gain.astype(jnp.float32), ln1_bias.astype(jnp.float32)
    )
    first_low = first_norm.astype(jnp.bfloat16)
    qv_full = qv_bias.astype(jnp.float32)
    bias_row = jnp.concatenate([qv_full[:width], jnp.zeros((width,), jnp.float32), qv_full[width:]])
    projected = jnp.dot(first_low, qkv_weight, preferred_element_type=jnp.float32) + bias_row
    qkv_low = projected.astype(jnp.bfloat16).reshape(images, length, 3, HEADS, head_dim)
    queries = qkv_low[:, :, 0]
    key_rows = qkv_low[:, :, 1]
    values = qkv_low[:, :, 2]
    scores = jnp.einsum(
        "nqhe,nkhe->nhqk", queries, key_rows, preferred_element_type=jnp.float32
    ) * head_dim ** (-0.5)
    scores = scores + alibi_bias + key_mask[:, None, None, :]
    top_score = jnp.max(scores, axis=-1, keepdims=True)
    shifted = jnp.exp(scores - top_score)
    probs = shifted / jnp.sum(shifted, axis=-1, keepdims=True)
    probs_low = probs.astype(jnp.bfloat16)
    attended = jnp.einsum("nhqk,nkhe->nqhe", probs_low, values, preferred_element_type=jnp.float32)
    att_low = attended.reshape(images * length, width).astype(jnp.bfloat16)
    residual = (
        inputs
        + jnp.dot(att_low, out_weight, preferred_element_type=jnp.float32)
        + out_bias.astype(jnp.float32)
    )
    second_norm, normed_two, scale_two = norm_parts(
        residual, ln2_gain.astype(jnp.float32), ln2_bias.astype(jnp.float32)
    )
    second_low = second_norm.astype(jnp.bfloat16)
    hidden = jnp.dot(second_low, fc1_weight, preferred_element_type=jnp.float32) + fc1_bias.astype(
        jnp.float32
    )
    act_low = gelu_exact(hidden).astype(jnp.bfloat16)
    branch = jnp.dot(act_low, fc2_weight, preferred_element_type=jnp.float32) + fc2_bias.astype(
        jnp.float32
    )
    output = valid_rows.reshape(images * length, 1) * (residual + branch)
    saved = (
        normed_one,
        scale_one,
        first_low,
        queries,
        key_rows,
        values,
        probs,
        probs_low,
        att_low,
        normed_two,
        scale_two,
        second_low,
        hidden,
        act_low,
    )
    return (output.reshape(images, length, width), saved)


def run_backward(saved, grad_out, attn_set, mlp_set):
    (
        normed_one,
        scale_one,
        first_low,
        queries,
        key_rows,
        values,
        probs,
        probs_low,
        att_low,
        normed_two,
        scale_two,
        second_low,
        hidden,
        act_low,
    ) = saved
    gain_one = attn_set[0].astype(jnp.float32)
    qkv_weight = attn_set[2]
    out_weight = attn_set[4]
    gain_two = mlp_set[0].astype(jnp.float32)
    fc1_weight = mlp_set[2]
    fc2_weight = mlp_set[4]
    images, length, heads_count, head_dim = queries.shape
    width = heads_count * head_dim
    branch_low = grad_out.astype(jnp.bfloat16)
    fc2_grad = jnp.einsum("rf,rd->fd", act_low, branch_low, preferred_element_type=jnp.float32)
    fc2_bias_grad = jnp.sum(branch_low, axis=0, dtype=jnp.float32)
    grad_act = jnp.einsum("rd,fd->rf", branch_low, fc2_weight, preferred_element_type=jnp.float32)
    grad_hidden = jax.vjp(gelu_exact, hidden)[1](grad_act)[0]
    hidden_low = grad_hidden.astype(jnp.bfloat16)
    fc1_grad = jnp.einsum("rd,rf->df", second_low, hidden_low, preferred_element_type=jnp.float32)
    fc1_bias_grad = jnp.sum(hidden_low, axis=0, dtype=jnp.float32)
    grad_second = jnp.einsum(
        "rf,df->rd", hidden_low, fc1_weight, preferred_element_type=jnp.float32
    )
    gain_two_grad = jnp.sum(grad_second * normed_two, axis=0)
    bias_two_grad = jnp.sum(grad_second, axis=0)
    grad_resid = grad_out + norm_back(grad_second, normed_two, scale_two, gain_two)
    mlp_terms = (gain_two_grad, bias_two_grad, fc1_grad, fc1_bias_grad, fc2_grad, fc2_bias_grad)
    mlp_grads = (
        lax.psum_scatter(mlp_terms[0], ("dp", "fsdp"), scatter_dimension=0, tiled=True),
        lax.psum_scatter(mlp_terms[1], ("dp", "fsdp"), scatter_dimension=0, tiled=True),
        lax.psum_scatter(mlp_terms[2], ("dp", "fsdp"), scatter_dimension=0, tiled=True),
        lax.psum_scatter(mlp_terms[3], ("dp", "fsdp"), scatter_dimension=0, tiled=True),
        lax.psum_scatter(mlp_terms[4], ("dp", "fsdp"), scatter_dimension=0, tiled=True),
        lax.psum_scatter(mlp_terms[5], ("dp", "fsdp"), scatter_dimension=0, tiled=True),
    )
    resid_low = grad_resid.astype(jnp.bfloat16)
    out_grad = jnp.einsum("rd,re->de", att_low, resid_low, preferred_element_type=jnp.float32)
    out_bias_grad = jnp.sum(resid_low, axis=0, dtype=jnp.float32)
    grad_att = jnp.einsum("re,de->rd", resid_low, out_weight, preferred_element_type=jnp.float32)
    grad_att = grad_att.astype(jnp.bfloat16).reshape(images, length, heads_count, head_dim)
    values_grad = jnp.einsum(
        "nhqk,nqhe->nkhe", probs_low, grad_att, preferred_element_type=jnp.float32
    )
    probs_grad = jnp.einsum("nqhe,nkhe->nhqk", grad_att, values, preferred_element_type=jnp.float32)
    inner_sum = jnp.sum(probs * probs_grad, axis=-1, keepdims=True)
    score_low = (probs * (probs_grad - inner_sum)).astype(jnp.bfloat16)
    scale_factor = head_dim ** (-0.5)
    queries_grad = (
        jnp.einsum("nhqk,nkhe->nqhe", score_low, key_rows, preferred_element_type=jnp.float32)
        * scale_factor
    )
    keys_grad = (
        jnp.einsum("nhqk,nqhe->nkhe", score_low, queries, preferred_element_type=jnp.float32)
        * scale_factor
    )
    qkv_grad = jnp.stack([queries_grad, keys_grad, values_grad], axis=2).astype(jnp.bfloat16)
    qkv_grad = qkv_grad.reshape(images * length, 3 * width)
    qkv_weight_grad = jnp.einsum(
        "rd,re->de", first_low, qkv_grad, preferred_element_type=jnp.float32
    )
    column_sums = jnp.sum(qkv_grad, axis=0, dtype=jnp.float32)
    qv_bias_grad = jnp.concatenate([column_sums[:width], column_sums[2 * width :]])
    grad_first = jnp.einsum("re,de->rd", qkv_grad, qkv_weight, preferred_element_type=jnp.float32)
    gain_one_grad = jnp.sum(grad_first * normed_one, axis=0)
    bias_one_grad = jnp.sum(grad_first, axis=0)
    grad_input = grad_resid + norm_back(grad_first, normed_one, scale_one, gain_one)
    attn_terms = (
        gain_one_grad,
        bias_one_grad,
        qkv_weight_grad,
        qv_bias_grad,
        out_grad,
        out_bias_grad,
    )
    attn_grads = (
        lax.psum_scatter(attn_terms[0], ("dp", "fsdp"), scatter_dimension=0, tiled=True),
        lax.psum_scatter(attn_terms[1], ("dp", "fsdp"), scatter_dimension=0, tiled=True),
        lax.psum_scatter(attn_terms[2], ("dp", "fsdp"), scatter_dimension=0, tiled=True),
        lax.psum_scatter(attn_terms[3], ("dp", "fsdp"), scatter_dimension=0, tiled=True),
        lax.psum_scatter(attn_terms[4], ("dp", "fsdp"), scatter_dimension=0, tiled=True),
        lax.psum_scatter(attn_terms[5], ("dp", "fsdp"), scatter_dimension=0, tiled=True),
    )
    return (grad_input.reshape(images, length, width), attn_grads, mlp_grads)


def shards(
    patches,
    counts,
    positions,
    ln1_gain,
    ln1_bias,
    qkv_weight,
    qv_bias,
    out_weight,
    out_bias,
    ln2_gain,
    ln2_bias,
    fc1_weight,
    fc1_bias,
    fc2_weight,
    fc2_bias,
    cotangent,
):
    images, length, width = patches.shape
    attn_set = (
        lax.all_gather(ln1_gain, ("dp", "fsdp"), axis=0, tiled=True),
        lax.all_gather(ln1_bias, ("dp", "fsdp"), axis=0, tiled=True),
        lax.all_gather(qkv_weight, ("dp", "fsdp"), axis=0, tiled=True),
        lax.all_gather(qv_bias, ("dp", "fsdp"), axis=0, tiled=True),
        lax.all_gather(out_weight, ("dp", "fsdp"), axis=0, tiled=True),
        lax.all_gather(out_bias, ("dp", "fsdp"), axis=0, tiled=True),
    )
    mlp_set = (
        lax.all_gather(ln2_gain, ("dp", "fsdp"), axis=0, tiled=True),
        lax.all_gather(ln2_bias, ("dp", "fsdp"), axis=0, tiled=True),
        lax.all_gather(fc1_weight, ("dp", "fsdp"), axis=0, tiled=True),
        lax.all_gather(fc1_bias, ("dp", "fsdp"), axis=0, tiled=True),
        lax.all_gather(fc2_weight, ("dp", "fsdp"), axis=0, tiled=True),
        lax.all_gather(fc2_bias, ("dp", "fsdp"), axis=0, tiled=True),
    )
    row_index = jnp.arange(length, dtype=jnp.int32)
    is_live = row_index[None, :] < counts[:, None]
    valid_rows = is_live.astype(jnp.float32)
    key_mask = jnp.where(is_live, 0.0, -1000000000.0).astype(jnp.float32)
    alibi_bias = alibi_table(positions, HEADS, SIDE)
    output, saved = run_forward(patches, valid_rows, key_mask, alibi_bias, attn_set, mlp_set)
    back_attn = (
        lax.all_gather(ln1_gain, ("dp", "fsdp"), axis=0, tiled=True),
        lax.all_gather(ln1_bias, ("dp", "fsdp"), axis=0, tiled=True),
        lax.all_gather(qkv_weight, ("dp", "fsdp"), axis=0, tiled=True),
        lax.all_gather(qv_bias, ("dp", "fsdp"), axis=0, tiled=True),
        lax.all_gather(out_weight, ("dp", "fsdp"), axis=0, tiled=True),
        lax.all_gather(out_bias, ("dp", "fsdp"), axis=0, tiled=True),
    )
    back_mlp = (
        lax.all_gather(ln2_gain, ("dp", "fsdp"), axis=0, tiled=True),
        lax.all_gather(ln2_bias, ("dp", "fsdp"), axis=0, tiled=True),
        lax.all_gather(fc1_weight, ("dp", "fsdp"), axis=0, tiled=True),
        lax.all_gather(fc1_bias, ("dp", "fsdp"), axis=0, tiled=True),
        lax.all_gather(fc2_weight, ("dp", "fsdp"), axis=0, tiled=True),
        lax.all_gather(fc2_bias, ("dp", "fsdp"), axis=0, tiled=True),
    )
    kept = run_forward(patches, valid_rows, key_mask, alibi_bias, back_attn, back_mlp)[1]
    grad_out = (valid_rows[:, :, None] * cotangent.astype(jnp.float32)).reshape(
        images * length, width
    )
    grad_input, attn_grads, mlp_grads = run_backward(kept, grad_out, back_attn, back_mlp)
    return (
        output.astype(jnp.bfloat16),
        grad_input.astype(jnp.bfloat16),
        attn_grads[0],
        attn_grads[1],
        attn_grads[2],
        attn_grads[3],
        attn_grads[4],
        attn_grads[5],
        mlp_grads[0],
        mlp_grads[1],
        mlp_grads[2],
        mlp_grads[3],
        mlp_grads[4],
        mlp_grads[5],
    )


def solution(mesh):
    in_specs = (
        P(("dp", "fsdp"), None, None),
        P(("dp", "fsdp")),
        P(("dp", "fsdp"), None),
        P(("dp", "fsdp")),
        P(("dp", "fsdp")),
        P(("dp", "fsdp"), None),
        P(("dp", "fsdp")),
        P(("dp", "fsdp"), None),
        P(("dp", "fsdp")),
        P(("dp", "fsdp")),
        P(("dp", "fsdp")),
        P(("dp", "fsdp"), None),
        P(("dp", "fsdp")),
        P(("dp", "fsdp"), None),
        P(("dp", "fsdp")),
        P(("dp", "fsdp"), None, None),
    )
    out_specs = (
        P(("dp", "fsdp"), None, None),
        P(("dp", "fsdp"), None, None),
        P(("dp", "fsdp")),
        P(("dp", "fsdp")),
        P(("dp", "fsdp"), None),
        P(("dp", "fsdp")),
        P(("dp", "fsdp"), None),
        P(("dp", "fsdp")),
        P(("dp", "fsdp")),
        P(("dp", "fsdp")),
        P(("dp", "fsdp"), None),
        P(("dp", "fsdp")),
        P(("dp", "fsdp"), None),
        P(("dp", "fsdp")),
    )
    return jax.shard_map(shards, mesh=mesh, in_specs=in_specs, out_specs=out_specs, check_vma=False)
```

profile of v0, /device:TPU:0, one launch (start us, length us, event | category | flops | bytes accessed | tf_op | source)
XLA Modules:
  0.0 794.6 jit_solution(11204251976484448130)
XLA Ops:
  7.3 0.7 all-gather.5.cloned.1.call-update
  8.1 0.7 all-gather.7.cloned.1.call-update
  8.8 0.7 all-gather.9.cloned.1.call-update
  10.1 1.6 convert_reduce_fusion.4
  11.8 2.1 multiply_reduce_fusion.6
  14.0 1.4 copy.87
  17.5 42.9 %all-reduce.17 = (bf16[1536]{0:T(1024)(128)(2,1)S(1)}, bf16[768]{0:T(1024)(128)(2,1)S(1)}, bf16[768]{0:T(1024)(128)(2,1)S(1)}, bf16[768]{0:T(1024)(128)(2,1)S(1)...) all-reduce(bf16[1536]{0:T(1024)(128)(2,1)S(1)} %dynamic-update-slic, ...), channel_id=1, replica_groups=mesh['dp'=8,'fsdp'=4] {'dp','fsdp'}, use_global_device_ids=true, to_apply=%add.2 | all-reduce | flops 9216 | bytes 36864
  60.7 1.5 reshape.219
  62.3 0.6 convert_element_type.174
  63.0 1.2 convert_reduce_fusion.3
  64.5 1.5 reshape.221
  66.1 0.8 add_convert_fusion.5
  66.9 1.1 copy.107
  68.0 2.4 convert_element_type.191
  70.4 1.2 add_sqrt_fusion
  71.6 2.4 all-gather.5.cloned.1.call-done
  73.9 6.2 add_convert_fusion.1
  80.1 9.6 %reshape.240 = bf16[4,153,3,12,64]{4,3,2,1,0:T(8,128)(2,1)} reshape(bf16[612,2304]{1,0:T(8,128)(2,1)} %add_convert_fusion.1) | data formatting | bytes 5640192 | tf_op jit(solution)/shard_map/reshape | solution.py:69
  89.7 5.5 fusion.57
  95.2 3.5 copy.119
  98.7 4.0 copy.120
  102.7 4.8 copy.118
  107.6 1.3 fusion.23
  108.8 4.2 fusion.60
  113.1 0.8 fusion.30
  113.9 2.3 copy-done.5
  116.2 1.2 copy.96
  117.4 1.8 convert_element_type.169
  119.2 10.7 %all-gather.7.cloned.1.call-done = bf16[768,768]{1,0:T(8,128)(2,1)} async-done(((bf16[24,768]{1,0:T(8,128)(2,1)}), bf16[768,768]{1,0:T(8,128)(2,1)}) %all-gather.7.cloned.1.call-update) | async-done | bytes 1179664 | tf_op jit(solution)/shard_map/all_gather | solution.py:241
  129.9 3.2 fusion.61
  133.5 61.9 %all-gather.9.cloned.1.call-done = bf16[768,3072]{1,0:T(8,128)(2,1)} async-done(((bf16[24,3072]{1,0:T(8,128)(2,1)}), bf16[768,3072]{1,0:T(8,128)(2,1)}) %all-gather.9.cloned.1.call-update) | async-done | bytes 4718608 | tf_op jit(solution)/shard_map/all_gather | solution.py:247
  195.4 23.8 %multiply_convert_fusion.1 = (bf16[612,3072]{1,0:T(8,128)(2,1)}, f32[612,3072]{1,0:T(8,128)}, f32[612,3072]{1,0:T(8,128)}) fusion(f32[3072]{0:T(1024)} %convert_element_type.174, bf16[768,3072]{1,0:T(8,128)(2,1)} %all-gather.9.cloned.1.call-done, f32[612,768]{1,0:T(8,128)S(1)} %get-tuple-element.114, f32[768]{0:T(1024)S(1)} %convert_element_type.172, ...), kind=kOutput, calls=%fused_computation.11 | convolution fusion | flops 3014212608 | bytes 25422624 | tf_op jit(solution)/shard_map/dot_general | solution.py:92
  219.2 41.4 %all-gather.11.cloned.1.call-done = bf16[3072,768]{1,0:T(8,128)(2,1)} async-done(((bf16[96,768]{1,0:T(8,128)(2,1)}), bf16[3072,768]{1,0:T(8,128)(2,1)}) %all-gather.11.cloned.1.call-update) | async-done | bytes 4718608 | tf_op jit(solution)/shard_map/all_gather | solution.py:249
  260.6 10.9 %convert_reduce_fusion.1 = (f32[3072]{0:T(1024)}, bf16[612,3072]{1,0:T(8,128)(2,1)S(1)}) fusion(f32[612,3072]{1,0:T(8,128)} %get-tuple-element.99, bf16[3072,768]{1,0:T(8,128)(2,1)} %all-gather.11.cloned.1.call-done, f32[612,768]{1,0:T(8,128)} %reshape.221, f32[612,3072]{1,0:T(8,128)} %get-tuple-element.115, f32[3072]{0:T(1024)} %convert_element_type.174), kind=kOutput, calls=%fused_computation.9 | convolution fusion | flops 2920206336 | bytes 25423872 | tf_op jit(solution)/shard_map/rd,fd->rf/dot_general | solution.py:147
  271.5 4.0 multiply_reduce_fusion.1
  275.6 2.3 convert_reduce_fusion.2
  277.9 2.5 fusion.50
  280.6 3.2 convolution_convert_fusion
  283.8 4.1 reshape.241
  287.9 4.6 copy.100
  292.5 9.0 %multiply_reduce_fusion = (f32[4,12,153]{2,1,0:T(8,128)S(1)}, f32[4,12,153,153]{2,3,1,0:T(8,128)}) fusion(f32[4,12,153,153]{2,3,1,0:T(8,128)} %copy-done.5, f32[4,12,153]{2,1,0:T(8,128)S(1)} %get-tuple-element.111, bf16[4,153,12,64]{1,3,2,0:T(8,128)(2,1)} %copy.100, bf16[4,153,1,12,64]{1,4,3,0,2:T(8,128)(2,1)} %copy.118), kind=kOutput, calls=%fused_computation.5 | convolution fusion | flops 147188448 | bytes 10927872 | tf_op jit(solution)/shard_map/nqhe,nkhe->nhqk/dot_general | solution.py:175
  301.5 8.2 %multiply_convert_fusion = bf16[4,12,153,153]{2,3,1,0:T(8,128)(2,1)S(1)} fusion(f32[4,12,153,153]{2,3,1,0:T(8,128)} %get-tuple-element.118, f32[4,12,153]{2,1,0:T(8,128)S(1)} %get-tuple-element.117, f32[4,12,153,153]{2,3,1,0:T(8,128)} %copy-done.5, f32[4,12,153]{2,1,0:T(8,128)S(1)} %get-tuple-element.111), kind=kLoop, calls=%fused_computation.4 | loop fusion | flops 4494528 | bytes 11295072 | tf_op jit(solution)/shard_map/convert_element_type | solution.py:177
  309.7 0.7 multiply_bitcast_fusion.1
  310.4 0.7 copy-done.4
  311.2 1.4 multiply_bitcast_fusion
  312.6 4.8 fusion.16
  317.4 1.4 convert_reduce_fusion
  318.9 6.6 copy.105
  325.5 8.8 %convert_element_type.187 = bf16[612,2304]{0,1:T(8,128)(2,1)} reshape(bf16[4,153,3,12,64]{1,0,4,3,2:T(4,128)(2,1)} %copy.105) | data formatting | bytes 5640192 | tf_op jit(solution)/shard_map/convert_element_type | solution.py:187
  334.3 6.9 fusion.62
  341.3 10.4 %fusion.54 = f32[768,3072]{1,0:T(8,128)} fusion(bf16[612,3072]{1,0:T(8,128)(2,1)} %copy-done.9, f32[612,768]{1,0:T(8,128)} %copy-done, f32[768]{0:T(1024)S(1)} %convert_element_type.172, f32[768]{0:T(1024)S(1)} %convert_element_type.171, f32[612]{0:T(1024)S(1)} %add_rsqrt_fusion.1, f32[612]{0:T(1024)S(1)} %broadcast_multiply_fusion.5), kind=kOutput, calls=%fused_computation.107 | convolution fusion | flops 2890128384 | bytes 15088416 | tf_op jit(solution)/shard_map/rd,rf->df/dot_general | solution.py:150
  352.0 10.3 %fusion.39 = f32[3072,768]{1,0:T(8,128)} fusion(bf16[612,3072]{1,0:T(8,128)(2,1)} %get-tuple-element.98, f32[612,768]{1,0:T(8,128)} %reshape.221), kind=kOutput, calls=%fused_computation.76 | convolution fusion | flops 2888248320 | bytes 15077376 | tf_op jit(solution)/shard_map/rf,rd->fd/dot_general | solution.py:145
  362.3 0.6 copy-done.18
  363.3 7.5 multiply_reduce_fusion.2
  370.8 40.9 %all-reduce.16 = (f32[768]{0:T(1024)S(1)}, f32[768]{0:T(1024)S(1)}, f32[1536]{0:T(1024)S(1)}, f32[768]{0:T(1024)S(1)}, f32[768]{0:T(1024)S(1)}, /*index=5*/f32[7...) all-reduce(f32[768]{0:T(1024)S(1)} %get-tuple-element.72, ...), channel_id=2, replica_groups=mesh['dp'=8,'fsdp'=4] {'dp','fsdp'}, use_global_device_ids=true, to_apply=%region_12.13.clone | all-reduce | flops 9216 | bytes 73728
  411.7 0.6 dynamic-slice
  415.2 3.7 add_convert_fusion.2
  419.0 1.6 convert_element_type.189
  420.6 1.7 copy.109
  422.2 6.9 multiply_convert_fusion.2
  429.4 1.7 copy.108
  432.2 71.5 %reduce-scatter.5.cloned.1.call-done = f32[24,2304]{1,0:T(8,128)} async-done(((f32[768,2304]{1,0:T(8,128)}), f32[24,2304]{1,0:T(8,128)}) %reduce-scatter.5.cloned.1.call-update) | async-done | bytes 221200 | tf_op jit(solution)/shard_map/reduce_scatter | solution.py:209
  503.7 141.3 %reduce-scatter.9.cloned.1.call-done = f32[24,3072]{1,0:T(8,128)} async-done(((f32[768,3072]{1,0:T(8,128)}), f32[24,3072]{1,0:T(8,128)}) %reduce-scatter.9.cloned.1.call-update) | async-done | bytes 294928 | tf_op jit(solution)/shard_map/reduce_scatter | solution.py:162
  645.0 142.3 %reduce-scatter.11.cloned.1.call-done = f32[96,768]{1,0:T(8,128)} async-done(((f32[3072,768]{1,0:T(8,128)}), f32[96,768]{1,0:T(8,128)}) %reduce-scatter.11.cloned.1.call-update) | async-done | bytes 294928 | tf_op jit(solution)/shard_map/reduce_scatter | solution.py:164
  (144 shorter events, 9.4 us)
Async XLA Ops:
  7.2 8.2 %copy-start.28 = (s32[4]{0:T(128)S(1)}, s32[4]{0:T(128)}, u32[]{:S(2)}) copy-start(s32[4]{0:T(128)} %param.18) | copy-start | bytes 52
  7.2 8.4 %copy-start.30 = (bf16[24]{0:T(256)(128)(2,1)S(1)}, bf16[24]{0:T(256)(128)(2,1)}, u32[]{:S(2)}) copy-start(bf16[24]{0:T(256)(128)(2,1)} %param.20) | copy-start | bytes 148
  7.2 8.6 %copy-start.31 = (bf16[24]{0:T(256)(128)(2,1)S(1)}, bf16[24]{0:T(256)(128)(2,1)}, u32[]{:S(2)}) copy-start(bf16[24]{0:T(256)(128)(2,1)} %param.21) | copy-start | bytes 148
  7.2 8.8 %copy-start.32 = (bf16[24]{0:T(256)(128)(2,1)S(1)}, bf16[24]{0:T(256)(128)(2,1)}, u32[]{:S(2)}) copy-start(bf16[24]{0:T(256)(128)(2,1)} %param.25) | copy-start | bytes 148
  7.2 9.1 %copy-start.33 = (bf16[24]{0:T(256)(128)(2,1)S(1)}, bf16[24]{0:T(256)(128)(2,1)}, u32[]{:S(2)}) copy-start(bf16[24]{0:T(256)(128)(2,1)} %param.26) | copy-start | bytes 148
  7.2 9.3 %copy-start.34 = (bf16[24]{0:T(256)(128)(2,1)S(1)}, bf16[24]{0:T(256)(128)(2,1)}, u32[]{:S(2)}) copy-start(bf16[24]{0:T(256)(128)(2,1)} %param.27) | copy-start | bytes 148
  7.2 9.5 %copy-start.35 = (bf16[24]{0:T(256)(128)(2,1)S(1)}, bf16[24]{0:T(256)(128)(2,1)}, u32[]{:S(2)}) copy-start(bf16[24]{0:T(256)(128)(2,1)} %param.31) | copy-start | bytes 148
  7.3 9.7 %copy-start.36 = (bf16[96]{0:T(256)(128)(2,1)S(1)}, bf16[96]{0:T(256)(128)(2,1)}, u32[]{:S(2)}) copy-start(bf16[96]{0:T(256)(128)(2,1)} %param.29) | copy-start | bytes 580
  7.3 10.0 %copy-start.37 = (bf16[48]{0:T(256)(128)(2,1)S(1)}, bf16[48]{0:T(256)(128)(2,1)}, u32[]{:S(2)}) copy-start(bf16[48]{0:T(256)(128)(2,1)} %param.23) | copy-start | bytes 292
  7.3 66.7 %all-gather.5.cloned.1.call-start = ((), (), s32[]{:S(2)}) async-start(), calls=%async_computation.4 | async-start | bytes 3649536 | tf_op jit(solution)/shard_map/all_gather | solution.py:239
  8.0 121.9 %all-gather.7.cloned.1.call-start = ((), (), s32[]{:S(2)}) async-start(), calls=%async_computation.5 | async-start | bytes 1216512 | tf_op jit(solution)/shard_map/all_gather | solution.py:241
  8.8 186.6 %all-gather.9.cloned.1.call-start = ((), (), s32[]{:S(2)}) async-start(), calls=%async_computation.6 | async-start | bytes 4866048 | tf_op jit(solution)/shard_map/all_gather | solution.py:247
  9.5 251.1 %all-gather.11.cloned.1.call-start = ((), (), s32[]{:S(2)}) async-start(), calls=%async_computation.7 | async-start | bytes 4866048 | tf_op jit(solution)/shard_map/all_gather | solution.py:249
  10.1 422.2 %reduce-scatter.7.cloned.1.call-start = ((), (), s32[]{:S(2)}) async-start(), calls=%async_computation.9 | async-start | bytes 2433024 | tf_op jit(solution)/shard_map/reduce_scatter | solution.py:211
  13.9 48.3 %copy-start.25 = (s32[4,153]{1,0:T(4,128)S(1)}, s32[4,153]{1,0:T(4,128)}, u32[]{:S(2)}) copy-start(s32[4,153]{1,0:T(4,128)} %param.19) | copy-start | bytes 7348
  13.9 49.1 %copy-start.13 = (bf16[4,153,768]{2,0,1:T(4,128)(2,1)S(1)}, bf16[4,153,768]{2,0,1:T(4,128)(2,1)}, u32[]{:S(2)}) copy-start(bf16[4,153,768]{2,0,1:T(4,128)(2,1)} %param.32) | copy-start | bytes 2820100
  15.6 49.0 %copy-start.17 = (f32[4,153]{1,0:T(4,128)}, f32[4,153]{1,0:T(4,128)S(1)}, u32[]{:S(2)}) copy-start(f32[4,153]{1,0:T(4,128)S(1)} %fusion.48) | copy-start | bytes 7348
  60.4 13.5 %copy-start.15 = (f32[768]{0:T(1024)}, f32[768]{0:T(1024)S(1)}, u32[]{:S(2)}) copy-start(f32[768]{0:T(1024)S(1)} %convert_element_type.159) | copy-start | bytes 9220
  60.6 13.3 %copy-start.19 = (f32[612]{0:T(1024)}, f32[612]{0:T(1024)S(1)}, u32[]{:S(2)}) copy-start(f32[612]{0:T(1024)S(1)} %rsqrt.23) | copy-start | bytes 7348
  60.7 13.2 %copy-start.21 = (f32[612]{0:T(1024)}, f32[612]{0:T(1024)S(1)}, u32[]{:S(2)}) copy-start(f32[612]{0:T(1024)S(1)} %div.55) | copy-start | bytes 7348
  64.2 1.9 copy-start.2
  66.1 7.9 copy-start.6
  98.7 8.8 %copy-start.3 = (bf16[4,153,1,12,64]{1,4,3,0,2:T(8,128)(2,1)}, bf16[4,153,1,12,64]{1,4,3,0,2:T(8,128)(2,1)S(1)}, u32[]{:S(2)}) copy-start(bf16[4,153,1,12,64]{1,4,3,0,2:T(8,128)(2,1)S(1)} %copy.119) | copy-start | bytes 2820100
  107.5 1.3 copy-start.14
  107.5 1.3 copy-start.38
  108.8 4.3 copy-start.10
  113.1 3.1 copy-start.5
  133.1 138.4 %copy-start = (f32[612,768]{1,0:T(8,128)}, f32[612,768]{1,0:T(8,128)S(1)}, u32[]{:S(2)}) copy-start(f32[612,768]{1,0:T(8,128)S(1)} %get-tuple-element.114) | copy-start | bytes 5640196
  260.6 10.9 %copy-start.29 = (bf16[768,3072]{1,0:T(8,128)(2,1)S(1)}, bf16[768,3072]{1,0:T(8,128)(2,1)}, u32[]{:S(2)}) copy-start(bf16[768,3072]{1,0:T(8,128)(2,1)} %all-gather.9.cloned.1.call-done) | copy-start | bytes 14155780
  271.5 4.0 copy-start.9
  271.5 4.0 copy-start.7
  275.5 2.3 copy-start.8
  280.4 223.3 %reduce-scatter.5.cloned.1.call-start = ((), (), s32[]{:S(2)}) async-start(), calls=%async_computation.8 | async-start | bytes 7299072 | tf_op jit(solution)/shard_map/reduce_scatter | solution.py:209
  309.7 1.4 copy-start.4
  311.2 1.4 copy-start.11
  325.5 8.8 %copy-start.12 = (bf16[612,768]{1,0:T(8,128)(2,1)S(1)}, bf16[612,768]{1,0:T(8,128)(2,1)}, u32[]{:S(2)}) copy-start(bf16[612,768]{1,0:T(8,128)(2,1)} %convert_element_type.191) | copy-start | bytes 2820100
  341.2 303.7 %reduce-scatter.9.cloned.1.call-start = ((), (), s32[]{:S(2)}) async-start(), calls=%async_computation.10 | async-start | bytes 9732096 | tf_op jit(solution)/shard_map/reduce_scatter | solution.py:162
  351.7 435.5 %reduce-scatter.11.cloned.1.call-start = ((), (), s32[]{:S(2)}) async-start(), calls=%async_computation.11 | async-start | bytes 9732096 | tf_op jit(solution)/shard_map/reduce_scatter | solution.py:164
  362.3 0.7 copy-start.18
  362.3 0.8 copy-start.27
  362.3 0.9 copy-start.16
  362.3 0.9 copy-start.20
  362.3 0.9 copy-start.22
  363.3 7.6 copy-start.23
  363.3 7.6 copy-start.24
  363.3 7.5 copy-start.26
  419.0 3.3 copy-start.1
Sparse Core Ops, SparseCore 0:
  11.0 62.8 all-gather.4
  76.8 53.0 all-gather.6
  132.8 62.5 all-gather.8
  198.1 62.3 all-gather.10
  280.5 97.7 reduce-scatter.6
  385.4 118.2 reduce-scatter.4
  510.1 134.7 reduce-scatter.8
  652.4 134.7 reduce-scatter.10
where the time goes:
time: 800 us; the launch traced here: 795 us
  waiting for transfers between devices  474 us (59%)
  matrix products  114 us (14%)
  blocking collectives  83.8 us (10%)
  local copies, waits for them, and re-layouts  79.1 us (10%)
  other arithmetic  28 us (4%)
  between operations  15.2 us (2%)
    reduce_scatter x1, waiting for transfers between devices, run_backward(): lax.psum_scatter(mlp_terms[4], ('dp', 'fsdp'), scatter_dimension=0, tiled...  142 us
    reduce_scatter x1, waiting for transfers between devices, run_backward(): lax.psum_scatter(mlp_terms[2], ('dp', 'fsdp'), scatter_dimension=0, tiled...  141 us
    unnamed x2, blocking collectives  83.8 us
    reduce_scatter x1, waiting for transfers between devices, run_backward(): lax.psum_scatter(attn_terms[2], ('dp', 'fsdp'), scatter_dimension=0, tile...  71.5 us
    all_gather x1, waiting for transfers between devices, shards(): lax.all_gather(fc1_weight, ('dp', 'fsdp'), axis=0, tiled=True)  61.9 us
    all_gather x1, waiting for transfers between devices, shards(): lax.all_gather(fc2_weight, ('dp', 'fsdp'), axis=0, tiled=True)  41.4 us
    unnamed x109, local copies, waits for them, and re-layouts  26.2 us
    dot_general x1, matrix products, run_forward(): jnp.dot(second_low, fc1_weight, preferred_element_type=jnp.float32)  23.8 us
  transfers between devices with their start and end apart: 8, of which 7 were waited for; matrix products, arithmetic and copies ran while one was open for 25% of the time, Pallas kernels for 0%

commit v1 on v0

v1 whole, which is shorter than its diff:
```python
import math

import jax
import jax.numpy as jnp
import numpy as np
from jax import lax
from jax.experimental import pallas as pl
from jax.experimental.pallas import tpu as pltpu
from jax.sharding import PartitionSpec as P

HEADS = 12
SIDE = 16
EPSILON = 1e-06
AXES = ("dp", "fsdp")
FAR = 1e30
CHIPS = 16
BLOCK = 384
MIB = 1024 * 1024

BF = jnp.bfloat16
F32 = jnp.float32


def power_slopes(number):
    first_slope = 2.0 ** (-8.0 / number)
    return [first_slope ** (index + 1) for index in range(number)]


def slope_list(heads_total):
    lower_power = 2 ** int(math.floor(math.log2(heads_total)))
    return (
        power_slopes(lower_power) + power_slopes(2 * lower_power)[0::2][: heads_total - lower_power]
    )


SLOPES = [float(np.float32(slope)) for slope in slope_list(HEADS)]


def dot(left, right, left_dim=1, right_dim=0):
    return lax.dot_general(
        left, right, (((left_dim,), (right_dim,)), ((), ())), preferred_element_type=F32
    )


def normed_rows(values):
    centered = values - jnp.mean(values, axis=-1, keepdims=True)
    scale = lax.rsqrt(jnp.mean(centered * centered, axis=-1, keepdims=True) + EPSILON)
    return centered * scale, scale


def norm_back(grad_normed, normed, scale):
    centered_mean = jnp.mean(grad_normed, axis=-1, keepdims=True)
    projected_mean = jnp.mean(grad_normed * normed, axis=-1, keepdims=True)
    return scale * (grad_normed - centered_mean - normed * projected_mean)


def row_of(vectors_ref, index):
    return jnp.concatenate(
        [vectors_ref[0, index : index + 1, :], vectors_ref[1, index : index + 1, :]], axis=1
    )


def gelu_parts(hidden):
    cumulative = 0.5 + 0.5 * lax.erf(hidden * math.sqrt(0.5))
    bell = jnp.exp(-0.5 * hidden * hidden)
    return cumulative, cumulative + hidden * bell * (1.0 / math.sqrt(2.0 * math.pi))


def share_kernel(place, qkv_ref, out_ref, fc1_ref, *refs):
    smalls, (mine_ref, theirs_ref, lines_ref) = refs[:-3], refs[-3:]
    for target, core in ((mine_ref, place[48]), (theirs_ref, 1 - place[48])):
        starts = [(qkv_ref, 2 * BLOCK * part + BLOCK * core) for part in range(3)]
        starts.append((out_ref, BLOCK * core))
        starts += [(fc1_ref, 4 * BLOCK * core + BLOCK * part) for part in range(4)]
        for block, (source, start) in enumerate(starts):
            target[block] = source[:, pl.ds(pl.multiple_of(start, 128), BLOCK)]
    device = place[49]
    lines = []
    for small in smalls:
        count = small.shape[0]
        line = small[...].astype(F32).reshape(1, count)
        line = jnp.concatenate([line, jnp.zeros((1, BLOCK - count), F32)], axis=1)
        lines.append(pltpu.roll(line, lax.rem(device, BLOCK // count) * count, 1))
    lines_ref[...] = jnp.concatenate(lines + [jnp.zeros((8, BLOCK), F32)], axis=0).astype(BF)


def pair_kernel(place, mine_ref, got_ref, lines_ref, fc2_ref, a_ref, b1_ref, b2_ref):
    swap = place[48] == 1
    for block in range(8):
        mine, got = mine_ref[block].astype(F32), got_ref[block].astype(F32)
        rows = jnp.concatenate([jnp.where(swap, got, mine), jnp.where(swap, mine, got)], axis=0)
        if block < 3:
            a_ref[48 * block : 48 * (block + 1), :] = rows.astype(BF)
        elif block == 3:
            b2_ref[192:240, :] = rows.astype(BF)
        else:
            b1_ref[48 * (block - 4) : 48 * (block - 3), :] = rows.astype(BF)
    b2_ref[0:96, :] = fc2_ref[:, :BLOCK]
    b2_ref[96:192, :] = fc2_ref[:, BLOCK:]
    a_ref[144:160, :] = lines_ref[...]


def each_piece(place, table, sources, work):
    core = place[48]
    for number, source in enumerate(sources):
        half = core if number < 2 else 1 - core

        def bring(index, _, source=source, number=number, half=half):
            work(source, index, place[table + number * 8 + index], half)
            return 0

        lax.fori_loop(0, 8, bring, 0)


def bring_out_weight(place, sources, wo, sem):
    def work(source, index, chip, half):
        spot = pl.ds(pl.multiple_of(chip * 48, 16), 48)
        pltpu.make_async_copy(source.at[index, pl.ds(192, 48)], wo.at[half, spot], sem).start()

    each_piece(place, 0, sources, work)


def bring_qkv_weight(place, sources, side, wq, sem, part_of=None):
    for first, here in ((0, place[48] == side), (2, place[48] != side)):

        @pl.when(here)
        def _(first=first):
            for number in (first, first + 1):

                def bring(index, _, source=sources[number], number=number):
                    spot = pl.ds(pl.multiple_of(place[number * 8 + index] * 48, 16), 48)
                    for part in range(3):
                        pltpu.make_async_copy(
                            source.at[index, pl.ds(48 * part, 48)],
                            wq.at[spot, pl.ds(BLOCK * part, BLOCK)] if part_of is None else wq.at[part, spot],
                            sem if part_of is None else part_of.at[part],
                        ).start()
                    return 0

                lax.fori_loop(0, 8, bring, 0)


def wait_all(buffer, sem):
    pltpu.make_async_copy(buffer, buffer, sem).wait()


def qkv_kernel(
    place, own0, own1, other0, other1, rows_ref,
    vec_ref, fcb_ref, h1_turned, qkv_ref,
    wq, h1, qvb, small, sems,
):
    sources = (own0, own1, other0, other1)
    side = pl.program_id(0)

    @pl.when(side == 0)
    def _():
        def work(source, index, chip, half):
            pltpu.make_async_copy(
                source.at[index, pl.ds(144, 16)], small.at[2 * chip + half], sems.at[2]
            ).start()

        each_piece(place, 0, sources, work)
        for half in range(2):
            bring_qkv_weight(place, sources, half, wq.at[half], sems.at[half])
        normed, _ = normed_rows(rows_ref[...].astype(F32))
        wait_all(small, sems.at[2])
        spread = small[...].astype(F32)
        vec_ref[...] = jnp.sum(spread.reshape(2, 16, 16, BLOCK), axis=1)
        qvb[...] = jnp.sum(spread.reshape(4, 8, 16, BLOCK), axis=1)
        lines = jnp.sum(spread.reshape(8, 4, 16, BLOCK), axis=1)
        for block in range(4):
            fcb_ref[block] = jnp.concatenate([lines[2 * block, 7:8], lines[2 * block + 1, 7:8]], axis=1)
        low = (normed * row_of(vec_ref, 0) + row_of(vec_ref, 1)).astype(BF)
        h1[...] = low
        h1_turned[...] = low.T

    wait_all(wq.at[side], sems.at[side])
    bias = jnp.concatenate(
        [qvb[side, 6:7, :], jnp.zeros((1, BLOCK), F32), qvb[2 + side, 6:7, :]], axis=1
    )
    qkv_ref[0] = (dot(h1[...], wq[side]) + bias).astype(BF)


def two_heads(pair_rows, low_half):
    nothing = jnp.zeros_like(pair_rows)
    return jnp.concatenate(
        [jnp.where(low_half, pair_rows, nothing), jnp.where(low_half, nothing, pair_rows)], axis=0
    )


def attention_kernel(qkv_ref, far_ref, att_ref):
    length = att_ref.shape[0]
    low_half = lax.broadcasted_iota(jnp.int32, (length, 128), 1) < 64
    far = far_ref[0]
    for pair in range(HEADS // 2):
        side, at = pair // 3, 128 * (pair % 3)
        queries = two_heads(qkv_ref[side, :, at : at + 128] * jnp.asarray(0.125, BF), low_half)
        key_rows = qkv_ref[side, :, BLOCK + at : BLOCK + at + 128]
        values = qkv_ref[side, :, 2 * BLOCK + at : 2 * BLOCK + at + 128]
        both = dot(queries, key_rows, 1, 1)
        probs = []
        for head in range(2):
            scores = both[length * head : length * (head + 1)] - SLOPES[2 * pair + head] * far
            shifted = jnp.exp(scores - jnp.max(scores, axis=-1, keepdims=True))
            share = shifted * (1.0 / jnp.sum(shifted, axis=-1, keepdims=True))
            probs.append(share.astype(BF))
        result = dot(jnp.concatenate(probs, axis=0), values)
        att_ref[:, 128 * pair : 128 * (pair + 1)] = jnp.where(
            low_half, result[:length], result[length:]
        ).astype(BF)


def give_rows(place, total, keep_ref, send_ref, extra=None):
    for chip in range(CHIPS):
        below = None if extra is None else extra(chip)
        for which, target in enumerate((keep_ref, send_ref)):
            slot = place[32 + 64 * which + chip]
            owner = place[48] if which == 0 else 1 - place[48]
            share = total[pl.ds(pl.multiple_of(48 * chip + 24 * owner, 8), 24), :]
            if below is not None:
                share = jnp.concatenate([share, below], axis=0)
            target[slot] = share.astype(BF)


def stack_rows(rows):
    blank = jnp.zeros_like(next(row for row in rows if row is not None))
    rows = [blank if row is None else row for row in rows]
    return jnp.concatenate(rows + [blank] * (8 - len(rows)), axis=0)


def sum_rows(values):
    return jnp.sum(values.astype(F32), axis=0, keepdims=True)


def mlp_kernel(
    place, counts, a0, a1, a2, a3, b0, b1, b2, b3, att_ref, rows_ref, gout_ref, vec_ref, fcb_ref,
    out_ref, gresid_ref, glow_ref, keep1_ref, send1_ref, keep2, send2,
    w1, w2, wo, h2, h2_turned, normed, total, gh2, product1, product2, stage, stage_end, fcg, scales,
    sems1, sems2, sems,
):
    block = pl.program_id(0)
    wide = 2 * BLOCK
    gain = row_of(vec_ref, 3)

    @pl.when(block == 0)
    def _():
        def work1(source, index, chip, half):
            spot = pl.ds(pl.multiple_of(chip * 48, 16), 48)
            for part in range(4):
                column = 2 * half + part // 2
                pltpu.make_async_copy(
                    source.at[index, pl.ds(48 * part, 48)],
                    w1.at[column, spot, pl.ds(BLOCK * (part % 2), BLOCK)],
                    sems1.at[column],
                ).start()

        def work2(source, index, chip, half):
            spot = pl.ds(pl.multiple_of(chip * 192 + half * 96, 16), 96)
            for part in range(2):
                pltpu.make_async_copy(
                    source.at[index, pl.ds(96 * part, 96)],
                    w2.at[spot, pl.ds(BLOCK * part, BLOCK)],
                    sems2.at[chip // 4],
                ).start()

        bring_out_weight(place, (b0, b1, b2, b3), wo, sems.at[2])
        each_piece(place, 64, (a0, a1, a2, a3), work1)
        each_piece(place, 0, (b0, b1, b2, b3), work2)
        wait_all(wo, sems.at[2])
        bias = row_of(vec_ref, 2)
        for part in range(2):
            lanes = slice(BLOCK * part, BLOCK * (part + 1))
            total[:, lanes] = rows_ref[:, lanes].astype(F32) + dot(att_ref[...], wo[part]) + bias[:, lanes]
        normal, scale = normed_rows(total[...])
        normed[...] = normal
        scales[...] = jnp.broadcast_to(scale, scales.shape)
        low = (normal * gain + row_of(vec_ref, 4)).astype(BF)
        h2[...] = low
        h2_turned[...] = low.T
        gh2[...] = jnp.zeros_like(gh2)

    wait_all(w1.at[block], sems1.at[block])
    hidden = dot(h2[...], w1[block]) + fcb_ref[block]
    rows_of = pl.ds(pl.multiple_of(block * wide, wide), wide)
    wait_all(w2.at[rows_of], sems2.at[block])
    gactivated = dot(gout_ref[...], w2[rows_of, :], 1, 1)
    cumulative, slope = gelu_parts(hidden)
    activated = (hidden * cumulative).astype(BF)
    ghidden = (gactivated * slope).astype(BF)
    product1[...] = dot(h2_turned[...], ghidden)
    product2[...] = dot(activated, gout_ref[...], 0, 0)
    branch = dot(activated, w2[rows_of, :])
    gradient = dot(ghidden, w1[block], 1, 1)
    fcg[block] = stack_rows([None, None, None, sum_rows(ghidden)])
    give_rows(place, product1, keep1_ref, send1_ref)
    for pair in range(4):
        for which, target in enumerate((keep2, send2)):
            chip = 4 * block + pair
            owner = place[48] if which == 0 else 1 - place[48]
            start = pl.multiple_of(192 * pair + 96 * owner, 8)
            stage[which, chip] = product2[pl.ds(start, 96), :].astype(BF)
            slot = place[32 + 64 * which + chip]
            pltpu.make_async_copy(stage.at[which, chip], target.at[slot, pl.ds(0, 96)], sems.at[which]).start()

    @pl.when(block < pl.num_programs(0) - 1)
    def _():
        @pl.when(block == 0)
        def _():
            total[...] = total[...] + row_of(vec_ref, 5)

        total[...] += branch
        gh2[...] += gradient

    @pl.when(block == pl.num_programs(0) - 1)
    def _():
        length = out_ref.shape[0] // 4
        row_index = lax.broadcasted_iota(jnp.int32, (length, 1), 0)
        for image in range(4):
            rows = slice(length * image, length * (image + 1))
            value = total[rows, :] + branch[rows]
            out_ref[rows, :] = jnp.where(row_index < counts[image], value, 0.0).astype(BF)
        whole = gh2[...] + gradient
        gout = gout_ref[...].astype(F32)
        gresid = gout + norm_back(whole * gain, normed[...], scales[:, 0:1])
        gresid_ref[...] = gresid
        low = gresid.astype(BF)
        glow_ref[...] = low
        sums = stack_rows(
            [sum_rows(whole * normed[...]), sum_rows(whole), sum_rows(gout), None, sum_rows(low)]
        )
        product1[...] = dot(att_ref[...], low, 0, 0)
        for chip in range(CHIPS):
            below = sums + fcg[chip // 4]
            for which, target in enumerate((keep2, send2)):
                owner = place[48] if which == 0 else 1 - place[48]
                share = product1[pl.ds(pl.multiple_of(48 * chip + 24 * owner, 8), 24), :]
                stage_end[which, chip] = jnp.concatenate([share, below], axis=0).astype(BF)
                slot = place[32 + 64 * which + chip]
                pltpu.make_async_copy(
                    stage_end.at[which, chip], target.at[slot, pl.ds(96, 32)], sems.at[which]
                ).start()
        wait_all(keep2, sems.at[0])
        wait_all(send2, sems.at[1])


def attention_back_kernel(
    side, place, own0, own1, other0, other1, qkv_ref, far_ref, glow_ref, gqkv_ref, wo, sem
):
    @pl.when(pl.program_id(0) == 0)
    def _():
        bring_out_weight(place, (own0, own1, other0, other1), wo, sem)
        wait_all(wo, sem)

    low = glow_ref[...]
    mine = slice(BLOCK * side, BLOCK * (side + 1))
    gatt = (
        dot(low[:, :BLOCK], wo[0, mine, :], 1, 1) + dot(low[:, BLOCK:], wo[1, mine, :], 1, 1)
    ).astype(BF)
    length = low.shape[0]
    low_half = lax.broadcasted_iota(jnp.int32, (length, 128), 1) < 64
    far = far_ref[0]
    for pair in range(3):
        at = 128 * pair
        queries = qkv_ref[0, :, at : at + 128] * jnp.asarray(0.125, BF)
        key_rows = two_heads(qkv_ref[0, :, BLOCK + at : BLOCK + at + 128], low_half)
        values = two_heads(qkv_ref[0, :, 2 * BLOCK + at : 2 * BLOCK + at + 128], low_half)
        grads = gatt[:, at : at + 128]
        both = dot(key_rows, queries, 1, 1)
        gboth = dot(values, grads, 1, 1)
        probs, gscores = [], []
        for head in range(2):
            rows = slice(length * head, length * (head + 1))
            scores = both[rows] - SLOPES[6 * side + 2 * pair + head] * far
            shifted = jnp.exp(scores - jnp.max(scores, axis=0, keepdims=True))
            share = shifted * (1.0 / jnp.sum(shifted, axis=0, keepdims=True))
            weighted = share * gboth[rows]
            probs.append(share.astype(BF))
            inner = jnp.sum(weighted, axis=0, keepdims=True)
            gscores.append((weighted - share * inner).astype(BF))
        probs, gscores = jnp.concatenate(probs, axis=0), jnp.concatenate(gscores, axis=0)
        gvalues = dot(probs, grads)
        gkeys = dot(gscores, queries)
        gqkv_ref[:, at : at + 128] = (dot(gscores, key_rows, 0, 0) * 0.125).astype(BF)
        for which, result in ((1, gkeys), (2, gvalues)):
            gqkv_ref[:, which * BLOCK + at : which * BLOCK + at + 128] = jnp.where(
                low_half, result[:length], result[length:]
            ).astype(BF)


def qkv_grad_step(side, place, sources, h1_turned, gqkv_ref, product, wq, sems):
    part = pl.program_id(0)

    @pl.when(part == 0)
    def _():
        bring_qkv_weight(place, sources, side, wq, None, sems)

    product[...] = dot(h1_turned[...], gqkv_ref[...])
    wait_all(wq.at[part], sems.at[part])
    return part, dot(gqkv_ref[...], wq[part], 1, 1)


def qkv_grad_kernel(
    place, own0, own1, other0, other1, h1_turned, gqkv_ref, gh1_ref, sums_ref, keep_ref, send_ref, product, wq, sems
):
    part, gradient = qkv_grad_step(
        0, place, (own0, own1, other0, other1), h1_turned, gqkv_ref, product, wq, sems
    )
    gh1_ref[...] = jnp.where(part == 0, gradient, gh1_ref[...] + gradient)
    sums_ref[part] = stack_rows([None, None, sum_rows(gqkv_ref[...])])
    give_rows(place, product, keep_ref, send_ref)


def input_kernel(
    place, own0, own1, other0, other1, h1_turned, gqkv_ref, before_ref, rows_ref, vec_ref, gresid, gh1,
    ginput_ref, keep_ref, send_ref,
    product, wq, sums, gresid_here, total, sems, sems_in,
):
    loads = [
        pltpu.make_async_copy(gh1, total, sems_in.at[0]),
        pltpu.make_async_copy(gresid, gresid_here, sems_in.at[1]),
    ]

    @pl.when(pl.program_id(0) == 0)
    def _():
        for load in loads:
            load.start()

    part, gradient = qkv_grad_step(
        1, place, (own0, own1, other0, other1), h1_turned, gqkv_ref, product, wq, sems
    )

    @pl.when(part == 0)
    def _():
        loads[0].wait()

    total[...] += gradient
    sums[part] = stack_rows([None, None, sum_rows(gqkv_ref[...])])

    @pl.when(part < 2)
    def _():
        give_rows(place, product, keep_ref, send_ref, lambda chip: jnp.zeros((8, BLOCK), F32))

    @pl.when(part == 2)
    def _():
        loads[1].wait()
        gradient = total[...]
        normed, scale = normed_rows(rows_ref[...].astype(F32))
        ginput_ref[...] = (
            gresid_here[...] + norm_back(gradient * row_of(vec_ref, 0), normed, scale)
        ).astype(BF)
        gain, shift = sum_rows(gradient * normed), sum_rows(gradient)

        def below(chip):
            lanes = slice(BLOCK * (chip // 8), BLOCK * (chip // 8 + 1))
            biases = (before_ref[0], sums[0], before_ref[2], sums[2])[chip // 4]
            return stack_rows([gain[:, lanes], shift[:, lanes]]) + biases

        give_rows(place, product, keep_ref, send_ref, below)


def after(value, *others):
    return lax.optimization_barrier((value,) + others)[0]


class Links:
    def __init__(self, depth):
        self.depth = depth

        def table(move):
            pairs = []
            for z in range(depth):
                for x in range(2):
                    for y in range(2):
                        for c in range(2):
                            nz, nx, ny, nc = move(z, x, y, c)
                            source = (z * 2 + x) * 4 + y * 2 + c
                            pairs.append((source, ((nz % depth) * 2 + nx) * 4 + ny * 2 + nc))
            return pairs

        self.ups = {step: table(lambda z, x, y, c: (z + step, x, y, c)) for step in (1, 2, 3)}
        self.first = table(lambda z, x, y, c: (z, x, 1 - y, c) if c else (z, 1 - x, y, c))
        self.second = table(lambda z, x, y, c: (z, 1 - x, y, c) if c else (z, x, 1 - y, c))
        self.cores = table(lambda z, x, y, c: (z, x, y, 1 - c))

    def move(self, value, pairs):
        return lax.ppermute(value, AXES, pairs)

    def spots(self):
        dp, fsdp = lax.axis_index("dp"), lax.axis_index("fsdp")
        z, x, y, core = dp // 2, dp % 2, fsdp // 2, fsdp % 2

        def chip(c, flip1, flip2, step):
            flip_x = jnp.where(c == 0, flip1, flip2)
            flip_y = jnp.where(c == 0, flip2, flip1)
            return (((z - step) % self.depth) * 2 + (x ^ flip_x)) * 2 + (y ^ flip_y)

        index = jnp.arange(32, dtype=jnp.int32)
        whose = jnp.where(index < 16, core, 1 - core)
        flip2 = (index // 8) % 2
        z_first = chip(whose, (index // 4) % 2, flip2, index % 4)
        x_first = chip(whose, index % 2, (index // 2) % 2, (index // 4) % 4)
        chips = jnp.arange(16, dtype=jnp.int32)
        turn_x, turn_y = ((chips // 2) % 2) ^ x, (chips % 2) ^ y
        step = (chips // 4 - z) % self.depth
        slots0 = turn_y * 8 + turn_x * 4 + step
        slots1 = turn_x * 8 + turn_y * 4 + step
        own_slots = jnp.where(core == 0, slots0, slots1)
        other_slots = jnp.where(core == 0, slots1, slots0)
        rest = jnp.where(jnp.arange(16) == 1, dp * 4 + fsdp, core).astype(jnp.int32)
        return jnp.concatenate([z_first, own_slots, rest, x_first, other_slots]).astype(jnp.int32)

    def gather(self, piece_a, piece_b1, piece_b2):
        hold = lax.optimization_barrier
        up = lambda value, step: self.move(value, self.ups[step])
        a_one, a_three, b1_two = hold((up(piece_a, 1), up(piece_a, 3), self.move(piece_b1, self.first)))
        b1_two = jnp.stack([piece_b1, b1_two])
        a_two, b1_four = hold((up(a_one, 1), self.move(b1_two, self.second)))
        a_four = jnp.stack([piece_a, a_one, a_two, a_three])
        b1_four = jnp.concatenate([b1_two, b1_four])
        piece_b2 = after(piece_b2, a_two)
        a_rest, b2_one, b2_three = hold((self.move(a_four, self.first), up(piece_b2, 1), up(piece_b2, 3)))
        a_eight = jnp.concatenate([a_four, a_rest])
        a_other, b2_two, b1_one = hold((self.move(a_eight, self.second), up(b2_one, 1), up(b1_four, 1)))
        b2_four = jnp.stack([piece_b2, b2_one, b2_two, b2_three])
        a = self.finish(a_eight, a_other)
        return a, (b1_four, b1_one, up(b1_four, 3)), (b2_four, self.move(b2_four, self.first))

    def gather_on(self, b1, b2):
        b1_four, b1_one, b1_three = b1
        b1_two = self.move(b1_one, self.ups[1])
        b2_eight = jnp.concatenate(b2)
        b2_other = self.move(b2_eight, self.second)
        b1_mine = jnp.concatenate([b1_four, b1_one])
        return (b1_mine, b1_two, b1_three, self.move(b1_mine, self.cores)), (b2_eight, b2_other)

    def gather_end(self, b1, b2):
        mine, b1_two, b1_three, other = b1
        rest = jnp.concatenate([b1_two, b1_three])
        return (mine, rest, other, self.move(rest, self.cores)), self.finish(*b2)

    def finish(self, eight, rest):
        return (eight, rest, self.move(eight, self.cores), self.move(rest, self.cores))

    def reduce(self, stage, state):
        keep = state[0]
        wide = lambda *terms: sum(term.astype(F32) for term in terms)
        if stage == 0:
            return keep, self.move(state[1], self.cores)
        got = state[1]
        if stage == 1:
            return keep, got, self.move(wide(keep[8:], got[8:]).astype(BF), self.second)
        got1 = state[2]
        if stage == 2:
            part = wide(keep[4:8], got[4:8], got1[4:]).astype(BF)
            return keep, got, got1, self.move(part, self.first)
        got2 = state[3]
        if stage == 3:
            parts = [
                wide(keep[step], got[step], got1[step], got2[step]).astype(BF) for step in (1, 2, 3)
            ]
            return state + tuple(
                self.move(part, self.ups[step]) for part, step in zip(parts, (1, 2, 3))
            )
        return wide(keep[0], got[0], got1[0], got2[0], *state[4:])


def full_pieces(full, blocks):
    split = full.reshape((CHIPS, 48) + full.shape[1:])
    split = split.transpose(3, 0, 2, 1, 4) if full.shape[1] == blocks else split.transpose(2, 0, 3, 1, 4)
    return split.reshape(2 * CHIPS, blocks * 48, BLOCK)


def eights(pieces):
    return tuple(pieces[8 * index : 8 * (index + 1)] for index in range(4))


def placed(vector, device, per_row):
    start = (device % per_row) * vector.shape[0]
    return lax.dynamic_update_slice(jnp.zeros((BLOCK,), vector.dtype), vector, (start,))


def shards(
    mesh_shape,
    patches,
    counts,
    positions,
    ln1_gain,
    ln1_bias,
    qkv_weight,
    qv_bias,
    out_weight,
    out_bias,
    ln2_gain,
    ln2_bias,
    fc1_weight,
    fc1_bias,
    fc2_weight,
    fc2_bias,
    cotangent,
):
    images, length, width = patches.shape
    padded = (length + 31) // 32 * 32
    rows = images * padded
    hidden_width = fc1_weight.shape[1]
    devices = mesh_shape["dp"] * mesh_shape["fsdp"]
    by_hand = devices == 2 * CHIPS and mesh_shape["fsdp"] == 4
    small_parts = (ln1_gain, ln1_bias, out_bias, ln2_gain, ln2_bias, fc2_bias, qv_bias, fc1_bias)

    smem = pl.BlockSpec(memory_space=pltpu.SMEM)
    vmem = pl.BlockSpec(memory_space=pltpu.VMEM)
    anywhere = pl.BlockSpec(memory_space=pltpu.HBM)
    struct = jax.ShapeDtypeStruct

    row_index = jnp.arange(padded, dtype=jnp.int32)
    is_live = row_index[None, :] < counts[:, None]
    pad_rows = ((0, 0), (0, padded - length), (0, 0))
    rows_in = jnp.pad(patches, pad_rows).reshape(rows, width)
    gout = jnp.where(is_live[:, :, None], jnp.pad(cotangent, pad_rows), 0).reshape(rows, width)
    spots = jnp.pad(positions, pad_rows[:2])
    grid_rows = (spots // SIDE).astype(F32)
    grid_cols = (spots % SIDE).astype(F32)
    row_delta = grid_rows[:, :, None] - grid_rows[:, None, :]
    col_delta = grid_cols[:, :, None] - grid_cols[:, None, :]
    distance = jnp.sqrt(row_delta * row_delta + col_delta * col_delta)
    far = jnp.where(is_live[:, None, :], distance, FAR)
    far_turned = jnp.where(is_live[:, :, None], distance, FAR)

    if by_hand:
        links = Links(mesh_shape["dp"] // 2)
        place = links.spots()
        core = place[48]
        share = struct((8, 24, BLOCK), BF)
        mine, theirs, lines = pl.pallas_call(
            share_kernel,
            out_shape=(share, share, struct((16, BLOCK), BF)),
            in_specs=[smem] + [vmem] * 11,
            out_specs=(vmem,) * 3,
            name="share",
        )(place, qkv_weight, out_weight, fc1_weight, *small_parts)
        got = links.move(theirs, links.cores)
        pieces = pl.pallas_call(
            pair_kernel,
            out_shape=tuple(struct((height, BLOCK), BF) for height in (160, 192, 240)),
            in_specs=[smem] + [vmem] * 4,
            out_specs=(vmem,) * 3,
            name="pair",
        )(place, mine, got, lines, fc2_weight)
    else:
        links = None
        place = jnp.concatenate(
            [
                jnp.arange(32, dtype=jnp.int32) % 16,
                jnp.arange(16, dtype=jnp.int32),
                jnp.zeros((16,), jnp.int32),
                jnp.arange(32, dtype=jnp.int32) % 16,
                jnp.arange(16, dtype=jnp.int32),
            ]
        )
        whole = [lax.all_gather(part, AXES, axis=0, tiled=True) for part in small_parts]
        lines = []
        for part in whole:
            share = part.shape[0] // 32
            chunks = part.reshape(32, share)
            lines.append(
                jnp.stack([placed(chunks[index], index, BLOCK // share) for index in range(32)])
            )
        lines = jnp.concatenate([jnp.stack(lines, axis=1), jnp.zeros((32, 8, BLOCK), BF)], axis=1)
        lines = lines.reshape(CHIPS, 2, 16, BLOCK).transpose(1, 0, 2, 3).reshape(32, 16, BLOCK)
        whole_qkv = lax.all_gather(qkv_weight, AXES, axis=0, tiled=True)
        whole_out = lax.all_gather(out_weight, AXES, axis=0, tiled=True)
        whole_fc1 = lax.all_gather(fc1_weight, AXES, axis=0, tiled=True)
        whole_fc2 = lax.all_gather(fc2_weight, AXES, axis=0, tiled=True)
        gathered_a = eights(
            jnp.concatenate([full_pieces(whole_qkv.reshape(width, 3, 2, BLOCK), 3), lines], axis=1)
        )
        gathered_b1 = eights(full_pieces(whole_fc1.reshape(width, 2, 4, BLOCK), 4))
        split = whole_fc2.reshape(CHIPS, 2, 96, 2, BLOCK).transpose(1, 0, 3, 2, 4).reshape(32, 192, BLOCK)
        gathered_b2 = eights(
            jnp.concatenate([split, full_pieces(whole_out.reshape(width, 1, 2, BLOCK), 1)], axis=1)
        )

    if by_hand:
        gathered_a, on_b1, on_b2 = links.gather(*pieces)


    def call(kernel, operands, out_shape, out_specs, in_specs, flops, mib, vmem_mib, grid, scratch=(), name=None):
        return pl.pallas_call(
            kernel,
            grid=grid,
            out_shape=out_shape,
            in_specs=in_specs,
            out_specs=out_specs,
            scratch_shapes=list(scratch),
            compiler_params=pltpu.CompilerParams(vmem_limit_bytes=vmem_mib * MIB),
            cost_estimate=pl.CostEstimate(
                flops=int(flops), bytes_accessed=mib * MIB, transcendentals=0
            ),
            name=name,
        )(*operands)

    image_rows = lambda columns: pl.BlockSpec((padded, columns), lambda image: (image, 0))
    image_far = pl.BlockSpec((1, padded, padded), lambda image: (image, 0, 0))
    fixed = lambda *shape: pl.BlockSpec(shape, lambda step: (0,) * len(shape))
    step_rows = lambda columns: pl.BlockSpec((rows, columns), lambda step: (0, step))
    shares = lambda height, columns: struct((CHIPS, height, columns), BF)
    buffer, flag = pltpu.VMEM, pltpu.SemaphoreType.DMA
    low_rows, wide_rows = struct((rows, width), BF), struct((rows, width), F32)
    wide = 2 * BLOCK
    steps = hidden_width // wide
    third = 3 * BLOCK

    def join(value, *states):
        if not by_hand:
            return (value,) + states
        return lax.optimization_barrier((value,) + states)

    def reduce(stage, state):
        return links.reduce(stage, state) if by_hand else state

    vec, fcb, h1_turned, qkv = call(
        qkv_kernel,
        (place, *gathered_a, rows_in),
        (
            struct((2, 16, BLOCK), F32), struct((steps, 1, wide), F32), struct((width, rows), BF),
            struct((2, rows, third), BF),
        ),
        (
            fixed(2, 16, BLOCK), fixed(steps, 1, wide), fixed(width, rows),
            pl.BlockSpec((1, rows, third), lambda step: (step, 0, 0)),
        ),
        [smem] + [anywhere] * 4 + [fixed(rows, width)],
        2 * rows * width * 3 * width,
        14,
        30,
        grid=(2,),
        scratch=(
            buffer((2, width, third), BF), buffer((rows, width), BF), buffer((4, 16, BLOCK), F32),
            buffer((32, 16, BLOCK), BF), flag((3,)),
        ),
        name="qkv",
    )
    if by_hand:
        qkv, on_b1, on_b2 = lax.optimization_barrier((qkv, on_b1, on_b2))
        on_b1, on_b2 = links.gather_on(on_b1, on_b2)

    att = call(
        attention_kernel,
        (qkv, far),
        low_rows,
        image_rows(width),
        [pl.BlockSpec((2, padded, third), lambda image: (0, image, 0)), image_far],
        8 * rows * 256 * width,
        10,
        20,
        grid=(images,),
        name="attention",
    )
    if by_hand:
        att, on_b1, on_b2 = lax.optimization_barrier((att, on_b1, on_b2))
        gathered_b1, gathered_b2 = links.gather_end(on_b1, on_b2)

    step_shares = lambda height, columns: pl.BlockSpec((CHIPS, height, columns), lambda step: (0, 0, step))
    out, gresid, glow, keep_1, send_1, keep_2, send_2 = call(
        mlp_kernel,
        (place, counts, *gathered_b1, *gathered_b2, att, rows_in, gout, vec, fcb),
        (low_rows, wide_rows, low_rows) + (shares(24, hidden_width),) * 2 + (shares(128, wide),) * 2,
        (fixed(rows, width),) * 3 + (step_shares(24, wide),) * 2 + (anywhere,) * 2,
        [smem, smem] + [anywhere] * 8 + [fixed(rows, width)] * 3 + [
            fixed(2, 16, BLOCK), fixed(steps, 1, wide),
        ],
        12 * rows * width * hidden_width,
        32,
        60,
        grid=(steps,),
        scratch=(
            buffer((steps, width, wide), BF), buffer((hidden_width, width), BF), buffer((2, width, BLOCK), BF),
            buffer((rows, width), BF), buffer((width, rows), BF), buffer((rows, width), F32),
            buffer((rows, width), F32), buffer((rows, width), F32), buffer((width, wide), F32),
            buffer((width, wide), F32), buffer((2, CHIPS, 96, wide), BF), buffer((2, CHIPS, 32, wide), BF),
            buffer((steps, 8, wide), F32), buffer((rows, 128), F32), flag((steps,)), flag((steps,)), flag((3,)),
        ),
        name="mlp",
    )
    state_2, state_1 = reduce(0, (keep_2, send_2)), reduce(0, (keep_1, send_1))

    def attention_back(side, gradient):
        return call(
            lambda *refs: attention_back_kernel(side, *refs),
            (place, *gathered_b2, qkv, far_turned, gradient),
            struct((rows, third), BF),
            image_rows(third),
            [smem] + [anywhere] * 4 + [
                pl.BlockSpec((1, padded, third), lambda image: (side, image, 0)), image_far, image_rows(width),
            ],
            8 * rows * 256 * width,
            8,
            20,
            grid=(images,),
            scratch=(buffer((2, width, BLOCK), BF), flag),
            name="attention_back",
        )

    gqkv_0 = attention_back(0, glow)
    gqkv_0, state_1, state_2 = join(gqkv_0, state_1, state_2)
    state_2, state_1 = reduce(1, state_2), reduce(1, state_1)

    gh1, sums_0, keep_a, send_a = call(
        qkv_grad_kernel,
        (place, *gathered_a, h1_turned, gqkv_0),
        (wide_rows, struct((3, 8, BLOCK), F32)) + (shares(24, third),) * 2,
        (fixed(rows, width), fixed(3, 8, BLOCK)) + (step_shares(24, BLOCK),) * 2,
        [smem] + [anywhere] * 4 + [fixed(width, rows), step_rows(BLOCK)],
        6 * rows * width * width,
        10,
        24,
        grid=(3,),
        scratch=(buffer((width, BLOCK), F32), buffer((3, width, BLOCK), BF), flag((3,))),
        name="qkv_grad",
    )
    state_a = reduce(0, (keep_a, send_a))

    gqkv_1 = attention_back(1, join(glow, gh1)[0])
    gqkv_1, state_a, state_2 = join(gqkv_1, state_a, state_2)
    state_a, state_2 = reduce(1, state_a), reduce(2, state_2)

    ginput, keep_c, send_c = call(
        input_kernel,
        (place, *gathered_a, h1_turned, gqkv_1, sums_0, rows_in, vec, gresid, gh1),
        (low_rows,) + (shares(32, third),) * 2,
        (fixed(rows, width),) + (step_shares(32, BLOCK),) * 2,
        [smem] + [anywhere] * 4 + [
            fixed(width, rows), step_rows(BLOCK), fixed(3, 8, BLOCK), fixed(rows, width), fixed(2, 16, BLOCK),
            anywhere, anywhere,
        ],
        6 * rows * width * width,
        14,
        30,
        grid=(3,),
        scratch=(
            buffer((width, BLOCK), F32), buffer((3, width, BLOCK), BF), buffer((3, 8, BLOCK), F32),
            buffer((rows, width), F32), buffer((rows, width), F32), flag((3,)), flag((2,)),
        ),
        name="input_grad",
    )
    ginput, state_c, state_2, state_1, state_a = join(ginput, (keep_c, send_c), state_2, state_1, state_a)
    state_c, state_a, state_1 = reduce(0, state_c), reduce(2, state_a), reduce(2, state_1)

    def cut(value):
        return value.reshape(images, padded, width)[:, :length]

    if by_hand:
        state_c = reduce(1, state_c)
        state_2 = reduce(3, join(state_2, state_c[:2])[0])
        out, ginput = after(out, state_c[1]), after(ginput, state_c[1])
        state_1, state_a, state_c = join(state_1, state_a, state_c)
        state_c = reduce(2, state_c)
        state_1, state_a = reduce(3, state_1), reduce(3, state_a)
        state_c = reduce(3, join(state_c)[0])
        state_1, state_2, state_a, _ = join(state_1, state_2, state_a, state_c[3])
        mine_c = reduce(4, state_c)
        mine_1, mine_2, mine_a = reduce(4, state_1), reduce(4, state_2), reduce(4, state_a)
        device = place[49]

        def share(line, count):
            start = (device % (line.shape[0] // count)) * count
            return lax.dynamic_slice(line, (start,), (count,))

        heads = []
        for part in range(3):
            lanes = slice(BLOCK * part, BLOCK * (part + 1))
            heads += [mine_a[:, lanes], mine_c[:24, lanes]]
        small_c, small_2 = mine_c[24:, 2 * BLOCK :], mine_2[120:]
        return (
            cut(out),
            cut(ginput),
            share(small_c[0], 24),
            share(small_c[1], 24),
            jnp.concatenate(heads, axis=1),
            share(small_c[2], 48),
            mine_2[96:120],
            share(small_2[4], 24),
            share(small_2[0], 24),
            share(small_2[1], 24),
            mine_1,
            share(small_2[3], 96),
            mine_2[:96],
            share(small_2[2], 24),
        )

    both_a, both_c, both_1, both_2 = (
        jnp.stack(state, axis=1).astype(F32) for state in (state_a, state_c, state_1, state_2)
    )
    heads = jnp.stack(
        [both.reshape(CHIPS, 2, 24, 3, BLOCK) for both in (both_a, both_c[:, :, :24])], axis=4
    )

    def vector(lines, count):
        columns = lines.shape[-1]
        return lines.reshape(32 * count // columns, -1, columns)[:, 0].reshape(-1)

    small_c, small_2 = both_c[:, :, 24:, 2 * BLOCK :], both_2[:, :, 120:]
    totals = (
        vector(small_c[:, :, 0], 24),
        vector(small_c[:, :, 1], 24),
        heads.reshape(width, 3 * width),
        vector(small_c[:, :, 2], 48),
        both_2[:, :, 96:120].reshape(width, width),
        vector(small_2[:, :, 4], 24),
        vector(small_2[:, :, 0], 24),
        vector(small_2[:, :, 1], 24),
        both_1.reshape(width, hidden_width),
        vector(small_2[:, :, 3], 96),
        both_2[:, :, :96].reshape(hidden_width, width),
        vector(small_2[:, :, 2], 24),
    )
    return (cut(out), cut(ginput)) + tuple(
        lax.psum_scatter(total, AXES, scatter_dimension=0, tiled=True) for total in totals
    )


def solution(mesh):
    rows = P(AXES, None, None)
    table = P(AXES, None)
    line = P(AXES)
    in_specs = (
        rows, line, table, line, line, table, line, table, line, line, line, table, line, table, line, rows,
    )
    out_specs = (
        rows, rows, line, line, table, line, table, line, line, line, table, line, table, line,
    )
    mesh_shape = dict(mesh.shape)

    def body(*arrays):
        return shards(mesh_shape, *arrays)

    return jax.shard_map(body, mesh=mesh, in_specs=in_specs, out_specs=out_specs, check_vma=False)
```

time: 800 us -> 268 us (0.34)
  waiting for transfers between devices: 474 us -> 81.5 us
  matrix products: 114 us -> 0 us
  Pallas kernels: 0 us -> 92.4 us
  blocking collectives: 83.8 us -> 0 us
  local copies, waits for them, and re-layouts: 79.1 us -> 25.8 us
  starting transfers between devices: 0.74 us -> 50 us
  other arithmetic: 28 us -> 13.9 us
  between operations: 15.2 us -> 3.48 us
    reduce_scatter x4 -> x0, waiting for transfers between devices: 355 us -> none  [the longest x1 142 us: run_backward(): lax.psum_scatter(mlp_terms[4], ('dp', 'fsdp'), scatter_dimension=0, tiled...]
    all_gather x4 -> x0, waiting for transfers between devices: 116 us -> none  [the longest x1 61.9 us: shards(): lax.all_gather(fc1_weight, ('dp', 'fsdp'), axis=0, tiled=True)]
    dot_general x18 -> x0, matrix products: 114 us -> none  [the longest x1 23.8 us: run_forward(): jnp.dot(second_low, fc1_weight, preferred_element_type=jnp.float32)]
    pallas_call x0 -> x9, Pallas kernels: none -> 92.4 us  [the longest x7 88.7 us: call(): pl.pallas_call(kernel, grid=grid, out_shape=out_shape, in_specs=in_specs,...]
    unnamed x2 -> x0, blocking collectives: 83.8 us -> none
    ppermute x0 -> x46, waiting for transfers between devices: none -> 81.5 us  [move(): return lax.ppermute(value, AXES, pairs)]
    ppermute x0 -> x46, starting transfers between devices: none -> 50 us  [move(): return lax.ppermute(value, AXES, pairs)]
    convert_element_type x11 -> x0, local copies, waits for them, and re-layouts: 25.4 us -> none  [the longest x2 15.4 us: run_backward(): jnp.stack([queries_grad, keys_grad, values_grad], axis=2)]
  transfers between devices with their start and end apart: 8 -> 46, of which waited for: 7 -> 19; matrix products, arithmetic and copies ran while one was open for 25% -> 8% of each run, Pallas kernels for 0% -> 19%
where the time goes in v1:
time: 268 us; the launch traced here: 267 us
  Pallas kernels  92.4 us (34%)
  waiting for transfers between devices  81.5 us (30%)
  starting transfers between devices  50 us (19%)
  local copies, waits for them, and re-layouts  25.8 us (10%)
  other arithmetic  13.9 us (5%)
  between operations  3.48 us (1%)
    pallas_call x7, Pallas kernels, call(): pl.pallas_call(kernel, grid=grid, out_shape=out_shape, in_specs=in_specs,...  88.7 us
    ppermute x46, waiting for transfers between devices, move(): return lax.ppermute(value, AXES, pairs)  81.5 us
    ppermute x46, starting transfers between devices, move(): return lax.ppermute(value, AXES, pairs)  50 us
    unnamed x123, local copies, waits for them, and re-layouts  15.2 us
    add x8, other arithmetic, reduce(): wide = lambda *terms: sum((term.astype(F32) for term in terms))  6.76 us
  transfers between devices with their start and end apart: 46, of which 19 were waited for; matrix products, arithmetic and copies ran while one was open for 8% of the time, Pallas kernels for 19%

profile of v1, /device:TPU:0, one launch (start us, length us, event | category | flops | bytes accessed | tf_op | source)
XLA Modules:
  0.0 267.1 jit_solution(9546477833737288462)
XLA Ops:
  1.3 1.8 share.1
  3.6 1.2 collective-permute-done.got_ref
  5.5 1.9 pair.1
  7.4 2.9 %collective-permute-start.3 = (bf16[192,384]{1,0:T(8,128)(2,1)}, bf16[192,384]{1,0:T(8,128)(2,1)S(1)}, u32[]{:S(2)}, u32[]{:S(2)}) collective-permute-start(bf16[192,384]{1,0:T(8,128)(2,1)} %get-tuple-element.134), channel_id=1, source_target_pairs={{0,4},{1,3},{2,6},{3,1},{4,0},{5,7},{6,2},{7,5},{8,12},{9,11},{10,... | collective-permute-start | bytes 442376 | tf_op jit(solution)/shard_map/ppermute | solution.py:486
  10.2 1.6 collective-permute-start.1
  11.8 2.2 collective-permute-start.2
  14.0 4.4 %collective-permute-done.1 = bf16[160,384]{1,0:T(8,128)(2,1)S(1)} collective-permute-done((bf16[160,384]{1,0:T(8,128)(2,1)}, bf16[160,384]{1,0:T(8,128)(2,1)S(1)}, u32[]{:S(2)}, u32[]{:S(2)}) %collective-permute-start.1) | collective-permute-done | bytes 122912 | tf_op jit(solution)/shard_map/ppermute | solution.py:486
  18.4 1.1 collective-permute-done.2
  19.5 0.9 pad_maximum_fusion.3
  21.0 1.1 collective-permute-start.4
  22.1 0.9 constant_dynamic-update-slice_fusion.4
  23.1 5.5 %collective-permute-done.4 = bf16[160,384]{1,0:T(8,128)(2,1)S(1)} collective-permute-done((bf16[160,384]{1,0:T(8,128)(2,1)S(1)}, bf16[160,384]{1,0:T(8,128)(2,1)S(1)}, u32[]{:S(2)}, u32[]{:S(2)}) %collective-permute-start.4) | collective-permute-done | bytes 122912 | tf_op jit(solution)/shard_map/ppermute | solution.py:486
  28.5 1.0 pad_maximum_fusion.2
  30.8 3.3 %collective-permute-start.8 = (bf16[240,384]{1,0:T(8,128)(2,1)S(1)}, bf16[240,384]{1,0:T(8,128)(2,1)S(1)}, u32[]{:S(2)}, u32[]{:S(2)}) collective-permute-start(bf16[240,384]{1,0:T(8,128)(2,1)S(1)} %copy-done.46), channel_id=1, source_target_pairs={{0,24},{1,25},{2,26},{3,27},{4,28},{5,29},{6,30},{7,31},{8,0},{9,1... | collective-permute-start | bytes 552968 | tf_op jit(solution)/shard_map/ppermute | solution.py:486
  34.2 5.5 %collective-permute-done.7 = bf16[240,384]{1,0:T(8,128)(2,1)S(1)} collective-permute-done((bf16[240,384]{1,0:T(8,128)(2,1)S(1)}, bf16[240,384]{1,0:T(8,128)(2,1)S(1)}, u32[]{:S(2)}, u32[]{:S(2)}) %collective-permute-start.7) | collective-permute-done | bytes 184352 | tf_op jit(solution)/shard_map/ppermute | solution.py:486
  40.1 1.8 collective-permute-start.9
  42.0 2.9 %collective-permute-start.10 = (bf16[240,384]{1,0:T(8,128)(2,1)S(1)}, bf16[240,384]{1,0:T(8,128)(2,1)S(1)}, u32[]{:S(2)}, u32[]{:S(2)}) collective-permute-start(bf16[240,384]{1,0:T(8,128)(2,1)S(1)} %collective-permute-done.7), channel_id=1, source_target_pairs={{0,8},{1,9},{2,10},{3,11},{4,12},{5,13},{6,14},{7,15},{8,16},{9,17... | collective-permute-start | bytes 552968 | tf_op jit(solution)/shard_map/ppermute | solution.py:486
  44.9 13.9 %collective-permute-done.11 = bf16[4,192,384]{2,1,0:T(8,128)(2,1)S(1)} collective-permute-done((bf16[4,192,384]{2,1,0:T(8,128)(2,1)S(1)}, bf16[4,192,384]{2,1,0:T(8,128)(2,1)S(1)}, u32[]{:S(2)}, u32[]{:S(2)}) %collective-permute-start.11) | collective-permute-done | bytes 589856 | tf_op jit(solution)/shard_map/ppermute | solution.py:486
  58.9 2.0 collective-permute-done.10
  62.5 1.0 collective-permute-done.13.other1
  63.4 6.4 %qkv.1 = (f32[2,16,384]{2,1,0:T(8,128)S(1)}, f32[4,1,768]{2,1,0:T(1,128)S(1)}, bf16[768,640]{1,0:T(8,128)(2,1)S(1)}, bf16[2,640,1152]{2,1,0:T(8,128)(2,1)S(1)}) custom-call(s32[112]{0:T(128)S(1)} %copy-done.21, bf16[8,160,384]{2,1,0:T(8,128)(2,1)S(1)} %constant_dynamic-update-slice_fusion.own0, bf16[8,160,384]{2,1,0:T(8,128)(2,1)S(1)} %collective-permute-done.9.own1, ...), custom_call_target="tpu_custom_call" | custom-call | flops 2264924160 | bytes 14680064 | tf_op jit(solution)/shard_map/qkv/pallas_call | solution.py:687
  69.9 7.0 %collective-permute-done.14 = bf16[4,192,384]{2,1,0:T(8,128)(2,1)S(1)} collective-permute-done((bf16[4,192,384]{2,1,0:T(8,128)(2,1)S(1)}, bf16[4,192,384]{2,1,0:T(8,128)(2,1)S(1)}, u32[]{:S(2)}, u32[]{:S(2)}) %collective-permute-start.14) | collective-permute-done | bytes 589856 | tf_op jit(solution)/shard_map/ppermute | solution.py:486
  76.9 1.0 constant_dynamic-update-slice_fusion.8
  77.8 0.9 constant_dynamic-update-slice_fusion.7.b0.refs_1_
  78.8 1.5 collective-permute-start.18
  80.8 1.2 fusion
  82.0 6.3 %attention.1.att_ref = bf16[640,768]{1,0:T(8,128)(2,1)S(1)} custom-call(bf16[2,640,1152]{2,1,0:T(8,128)(2,1)S(1)} %get-tuple-element.149.qkv_ref.refs_5_, f32[4,160,160]{2,1,0:T(8,128)S(1)} %get-tuple-element.267.far_ref), custom_call_target="tpu_custom_call" | custom-call | flops 1006632960 | bytes 10485760 | tf_op jit(solution)/shard_map/attention/pallas_call | solution.py:687
  88.3 1.0 copy-done.9
  89.3 8.8 %collective-permute-done.16 = bf16[4,192,384]{2,1,0:T(8,128)(2,1)S(1)} collective-permute-done((bf16[4,192,384]{2,1,0:T(8,128)(2,1)S(1)}, bf16[4,192,384]{2,1,0:T(8,128)(2,1)S(1)}, u32[]{:S(2)}, u32[]{:S(2)}) %collective-permute-start.16) | collective-permute-done | bytes 589856 | tf_op jit(solution)/shard_map/ppermute | solution.py:486
  99.9 0.9 constant_dynamic-update-slice_fusion.9.a1
  101.0 1.9 pad_select_fusion
  102.9 1.1 copy.32
  104.0 2.0 collective-permute-done.19.a3
  106.0 38.0 %mlp.1 = (bf16[640,768]{1,0:T(8,128)(2,1)}, f32[640,768]{1,0:T(8,128)}, bf16[640,768]{1,0:T(8,128)(2,1)}, bf16[16,24,3072]{2,1,0:T(8,128)(2,1)}, bf16[16,24,3072...) custom-call(s32[112]{0:T(128)} %concatenate.23.place.refs_0_, s32[4]{0:T(128)} %counts.1, ...), custom_call_target="tpu_custom_call" | custom-call | flops 18119393280 | bytes 33554432 | tf_op jit(solution)/shard_map/mlp/pallas_call | solution.py:687
  144.6 1.1 copy-done
  145.6 1.2 copy-done.2
  146.9 8.9 %attention_back.2.gqkv_ref = bf16[640,1152]{1,0:T(8,128)(2,1)S(1)} custom-call(s32[112]{0:T(128)S(1)} %copy-done.22, bf16[8,240,384]{2,1,0:T(8,128)(2,1)} %constant_dynamic-update-slice_fusion.7.b0.refs_1_, bf16[8,240,384]{2,1,0:T(8,128)(2,1)} %collective-permute-done.18.b1.refs_2_, bf16[8,240,384]{2,1,0:T(8,128)(2,1)} %collective-permute-done.20.b2.refs_3_, ...), custom_call_target="tpu_custom_call" | custom-call | flops 1006632960 | bytes 8388608 | tf_op jit(solution)/shard_map/attention_back/pallas_call | solution.py:687
  156.2 1.5 collective-permute-start.25
  157.7 1.0 copy-done.11
  159.9 8.8 %qkv_grad.1 = (f32[640,768]{1,0:T(8,128)S(1)}, f32[3,8,384]{2,1,0:T(8,128)S(1)}, bf16[16,24,1152]{2,1,0:T(8,128)(2,1)S(1)}, bf16[16,24,1152]{2,1,0:T(8,128)(2,1)S(1)}) custom-call(s32[112]{0:T(128)S(1)} %copy-done.22, bf16[8,160,384]{2,1,0:T(8,128)(2,1)S(1)} %copy-done.8, bf16[8,160,384]{2,1,0:T(8,128)(2,1)S(1)} %copy-done.11, ...), custom_call_target="tpu_custom_call" | custom-call | flops 2264924160 | bytes 10485760 | tf_op jit(solution)/shard_map/qkv_grad/pallas_call | solution.py:687
  169.2 1.6 collective-permute-start.27
  170.8 8.4 %attention_back.3.gqkv_ref = bf16[640,1152]{1,0:T(8,128)(2,1)S(1)} custom-call(s32[112]{0:T(128)S(1)} %copy-done.22, bf16[8,240,384]{2,1,0:T(8,128)(2,1)} %constant_dynamic-update-slice_fusion.7.b0.refs_1_, bf16[8,240,384]{2,1,0:T(8,128)(2,1)} %collective-permute-done.18.b1.refs_2_, bf16[8,240,384]{2,1,0:T(8,128)(2,1)} %collective-permute-done.20.b2.refs_3_, ...), custom_call_target="tpu_custom_call" | custom-call | flops 1006632960 | bytes 8388608 | tf_op jit(solution)/shard_map/attention_back/pallas_call | solution.py:687
  180.2 1.1 collective-permute-start.28
  181.9 12.1 %input_grad.1 = (bf16[640,768]{1,0:T(8,128)(2,1)S(1)}, bf16[16,32,1152]{2,1,0:T(8,128)(2,1)S(1)}, bf16[16,32,1152]{2,1,0:T(8,128)(2,1)S(1)}) custom-call(s32[112]{0:T(128)S(1)} %copy-done.22, bf16[8,160,384]{2,1,0:T(8,128)(2,1)S(1)} %copy-done.8, bf16[8,160,384]{2,1,0:T(8,128)(2,1)S(1)} %copy-done.11, bf16[8,160,384]{2,1,0:T(8,128)(2,1)S(1)} %copy-done.13, ...), custom_call_target="tpu_custom_call" | custom-call | flops 2264924160 | bytes 14680064 | tf_op jit(solution)/shard_map/input_grad/pallas_call | solution.py:687
  194.0 2.6 collective-permute-done.27
  196.6 5.9 %collective-permute-done.28 = bf16[8,24,1152]{2,1,0:T(8,128)(2,1)S(1)} collective-permute-done((bf16[8,24,1152]{2,1,0:T(8,128)(2,1)S(1)}, bf16[8,24,1152]{2,1,0:T(8,128)(2,1)S(1)}, u32[]{:S(2)}, u32[]{:S(2)}) %collective-permute-start.28) | collective-permute-done | bytes 442400 | tf_op jit(solution)/shard_map/ppermute | solution.py:486
  202.8 0.9 collective-permute-start.30
  203.7 1.7 collective-permute-done.29
  205.6 1.5 collective-permute-start.32
  208.1 3.3 %collective-permute-start.41 = (bf16[128,768]{1,0:T(8,128)(2,1)S(1)}, bf16[128,768]{1,0:T(8,128)(2,1)S(1)}, u32[]{:S(2)}, u32[]{:S(2)}) collective-permute-start(bf16[128,768]{1,0:T(8,128)(2,1)S(1)} %get-tuple-element.247), channel_id=1, source_target_pairs={{0,16},{1,17},{2,18},{3,19},{4,20},{5,21},{6,22},{7,23},{8,24},{9,... | collective-permute-start | bytes 589832 | tf_op jit(solution)/shard_map/ppermute | solution.py:486
  211.4 10.0 %collective-permute-done.31 = bf16[4,24,1152]{2,1,0:T(8,128)(2,1)S(1)} collective-permute-done((bf16[4,24,1152]{2,1,0:T(8,128)(2,1)S(1)}, bf16[4,24,1152]{2,1,0:T(8,128)(2,1)S(1)}, u32[]{:S(2)}, u32[]{:S(2)}) %collective-permute-start.31) | collective-permute-done | bytes 221216 | tf_op jit(solution)/shard_map/ppermute | solution.py:486
  221.5 2.6 collective-permute-start.42
  224.2 1.5 collective-permute-start.33
  225.7 1.0 fusion.11
  227.3 3.3 %collective-permute-start.39 = (bf16[24,3072]{1,0:T(8,128)(2,1)}, bf16[24,3072]{1,0:T(8,128)(2,1)}, u32[]{:S(2)}, u32[]{:S(2)}) collective-permute-start(bf16[24,3072]{1,0:T(8,128)(2,1)} %get-tuple-element.249), channel_id=1, source_target_pairs={{0,24},{1,25},{2,26},{3,27},{4,28},{5,29},{6,30},{7,31},{8,0},{9,1... | collective-permute-start | bytes 442376 | tf_op jit(solution)/shard_map/ppermute | solution.py:486
  231.9 8.0 %collective-permute-done.43 = bf16[24,1152]{1,0:T(8,128)(2,1)S(1)} collective-permute-done((bf16[24,1152]{1,0:T(8,128)(2,1)S(1)}, bf16[24,1152]{1,0:T(8,128)(2,1)S(1)}, u32[]{:S(2)}, u32[]{:S(2)}) %collective-permute-start.43) | collective-permute-done | bytes 55328 | tf_op jit(solution)/shard_map/ppermute | solution.py:486
  239.9 4.4 %collective-permute-start.44 = (bf16[24,1152]{1,0:T(8,128)(2,1)}, bf16[24,1152]{1,0:T(8,128)(2,1)}, u32[]{:S(2)}, u32[]{:S(2)}) collective-permute-start(bf16[24,1152]{1,0:T(8,128)(2,1)} %get-tuple-element.256), channel_id=1, source_target_pairs={{0,16},{1,17},{2,18},{3,19},{4,20},{5,21},{6,22},{7,23},{8,24},{9,... | collective-permute-start | bytes 165896 | tf_op jit(solution)/shard_map/ppermute | solution.py:486
  248.1 2.9 %copy.35 = bf16[4,153,768]{2,0,1:T(4,128)(2,1)} copy(bf16[4,153,768]{2,1,0:T(8,128)(2,1)} %bitcast.89) | data formatting | bytes 1880064
  251.0 1.7 copy.36
  252.7 1.5 fusion.3
  255.7 1.1 collective-permute-start.36
  256.8 2.0 collective-permute-start.35
  258.8 1.0 fusion.15
  262.2 2.1 fusion.5
  (209 shorter events, 24.2 us)
Async XLA Ops:
  3.1 1.7 collective-permute-start
  7.4 22.9 %copy-start.46 = (bf16[240,384]{1,0:T(8,128)(2,1)S(1)}, bf16[240,384]{1,0:T(8,128)(2,1)}, u32[]{:S(2)}) copy-start(bf16[240,384]{1,0:T(8,128)(2,1)} %get-tuple-element.140) | copy-start | bytes 552964
  7.4 12.1 %collective-permute-start.3 = (bf16[192,384]{1,0:T(8,128)(2,1)}, bf16[192,384]{1,0:T(8,128)(2,1)S(1)}, u32[]{:S(2)}, u32[]{:S(2)}) collective-permute-start(bf16[192,384]{1,0:T(8,128)(2,1)} %get-tuple-element.134), channel_id=1, source_target_pairs={{0,4},{1,3},{2,6},{3,1},{4,0},{5,7},{6,2},{7,5},{8,12},{9,11},{10,... | collective-permute-start | bytes 442376 | tf_op jit(solution)/shard_map/ppermute | solution.py:486
  10.2 8.2 %collective-permute-start.1 = (bf16[160,384]{1,0:T(8,128)(2,1)}, bf16[160,384]{1,0:T(8,128)(2,1)S(1)}, u32[]{:S(2)}, u32[]{:S(2)}) collective-permute-start(bf16[160,384]{1,0:T(8,128)(2,1)} %get-tuple-element.133), channel_id=1, source_target_pairs={{0,8},{1,9},{2,10},{3,11},{4,12},{5,13},{6,14},{7,15},{8,16},{9,17... | collective-permute-start | bytes 368648 | tf_op jit(solution)/shard_map/ppermute | solution.py:486
  11.8 7.7 %collective-permute-start.2 = (bf16[160,384]{1,0:T(8,128)(2,1)}, bf16[160,384]{1,0:T(8,128)(2,1)S(1)}, u32[]{:S(2)}, u32[]{:S(2)}) collective-permute-start(bf16[160,384]{1,0:T(8,128)(2,1)} %get-tuple-element.133), channel_id=1, source_target_pairs={{0,24},{1,25},{2,26},{3,27},{4,28},{5,29},{6,30},{7,31},{8,0},{9,1... | collective-permute-start | bytes 368648 | tf_op jit(solution)/shard_map/ppermute | solution.py:486
  20.4 21.5 %copy-start.33 = (bf16[192,384]{1,0:T(8,128)(2,1)S(1)}, bf16[192,384]{1,0:T(8,128)(2,1)}, u32[]{:S(2)}) copy-start(bf16[192,384]{1,0:T(8,128)(2,1)} %get-tuple-element.134) | copy-start | bytes 442372
  20.4 8.1 %collective-permute-start.5 = (bf16[2,192,384]{2,1,0:T(8,128)(2,1)S(1)}, bf16[2,192,384]{2,1,0:T(8,128)(2,1)S(1)}, u32[]{:S(2)}, u32[]{:S(2)}) collective-permute-start(bf16[2,192,384]{2,1,0:T(8,128)(2,1)S(1)} %pad_maximum_fusion.3), channel_id=1, source_target_pairs={{0,2},{1,5},{2,0},{3,7},{4,6},{5,1},{6,4},{7,3},{8,10},{9,13},{10,... | collective-permute-start | bytes 884744 | tf_op jit(solution)/shard_map/ppermute | solution.py:486
  21.0 7.5 %collective-permute-start.4 = (bf16[160,384]{1,0:T(8,128)(2,1)S(1)}, bf16[160,384]{1,0:T(8,128)(2,1)S(1)}, u32[]{:S(2)}, u32[]{:S(2)}) collective-permute-start(bf16[160,384]{1,0:T(8,128)(2,1)S(1)} %collective-permute-done.1), channel_id=1, source_target_pairs={{0,8},{1,9},{2,10},{3,11},{4,12},{5,13},{6,14},{7,15},{8,16},{9,17... | collective-permute-start | bytes 368648 | tf_op jit(solution)/shard_map/ppermute | solution.py:486
  29.5 10.5 %collective-permute-start.6 = (bf16[4,160,384]{2,1,0:T(8,128)(2,1)S(1)}, bf16[4,160,384]{2,1,0:T(8,128)(2,1)S(1)}, u32[]{:S(2)}, u32[]{:S(2)}) collective-permute-start(bf16[4,160,384]{2,1,0:T(8,128)(2,1)S(1)} %pad_maximum_fusion.2), channel_id=1, source_target_pairs={{0,4},{1,3},{2,6},{3,1},{4,0},{5,7},{6,2},{7,5},{8,12},{9,11},{10,... | collective-permute-start | bytes 1474568 | tf_op jit(solution)/shard_map/ppermute | solution.py:486
  30.3 9.4 %collective-permute-start.7 = (bf16[240,384]{1,0:T(8,128)(2,1)S(1)}, bf16[240,384]{1,0:T(8,128)(2,1)S(1)}, u32[]{:S(2)}, u32[]{:S(2)}) collective-permute-start(bf16[240,384]{1,0:T(8,128)(2,1)S(1)} %copy-done.46), channel_id=1, source_target_pairs={{0,8},{1,9},{2,10},{3,11},{4,12},{5,13},{6,14},{7,15},{8,16},{9,17... | collective-permute-start | bytes 552968 | tf_op jit(solution)/shard_map/ppermute | solution.py:486
  30.8 9.2 %collective-permute-start.8 = (bf16[240,384]{1,0:T(8,128)(2,1)S(1)}, bf16[240,384]{1,0:T(8,128)(2,1)S(1)}, u32[]{:S(2)}, u32[]{:S(2)}) collective-permute-start(bf16[240,384]{1,0:T(8,128)(2,1)S(1)} %copy-done.46), channel_id=1, source_target_pairs={{0,24},{1,25},{2,26},{3,27},{4,28},{5,29},{6,30},{7,31},{8,0},{9,1... | collective-permute-start | bytes 552968 | tf_op jit(solution)/shard_map/ppermute | solution.py:486
  40.1 23.3 %copy-start.7 = (bf16[8,160,384]{2,1,0:T(8,128)(2,1)}, bf16[8,160,384]{2,1,0:T(8,128)(2,1)S(1)}, u32[]{:S(2)}) copy-start(bf16[8,160,384]{2,1,0:T(8,128)(2,1)S(1)} %constant_dynamic-update-slice_fusion.own0) | copy-start | bytes 2949124
  40.1 22.2 %copy-start.30 = (bf16[4,153,768]{2,0,1:T(4,128)(2,1)S(1)}, bf16[4,153,768]{2,0,1:T(4,128)(2,1)}, u32[]{:S(2)}) copy-start(bf16[4,153,768]{2,0,1:T(4,128)(2,1)} %param.16) | copy-start | bytes 2820100
  40.1 20.8 %collective-permute-start.9 = (bf16[8,160,384]{2,1,0:T(8,128)(2,1)S(1)}, bf16[8,160,384]{2,1,0:T(8,128)(2,1)S(1)}, u32[]{:S(2)}, u32[]{:S(2)}) collective-permute-start(bf16[8,160,384]{2,1,0:T(8,128)(2,1)S(1)} %constant_dynamic-update-slice_fusion.own0), channel_id=1, source_target_pairs={{0,2},{1,5},{2,0},{3,7},{4,6},{5,1},{6,4},{7,3},{8,10},{9,13},{10,... | collective-permute-start | bytes 2949128 | tf_op jit(solution)/shard_map/ppermute | solution.py:486
  42.0 16.9 %collective-permute-start.11 = (bf16[4,192,384]{2,1,0:T(8,128)(2,1)S(1)}, bf16[4,192,384]{2,1,0:T(8,128)(2,1)S(1)}, u32[]{:S(2)}, u32[]{:S(2)}) collective-permute-start(bf16[4,192,384]{2,1,0:T(8,128)(2,1)S(1)} %pad_maximum_fusion.1), channel_id=1, source_target_pairs={{0,8},{1,9},{2,10},{3,11},{4,12},{5,13},{6,14},{7,15},{8,16},{9,17... | collective-permute-start | bytes 1769480 | tf_op jit(solution)/shard_map/ppermute | solution.py:486
  42.0 18.8 %collective-permute-start.10 = (bf16[240,384]{1,0:T(8,128)(2,1)S(1)}, bf16[240,384]{1,0:T(8,128)(2,1)S(1)}, u32[]{:S(2)}, u32[]{:S(2)}) collective-permute-start(bf16[240,384]{1,0:T(8,128)(2,1)S(1)} %collective-permute-done.7), channel_id=1, source_target_pairs={{0,8},{1,9},{2,10},{3,11},{4,12},{5,13},{6,14},{7,15},{8,16},{9,17... | collective-permute-start | bytes 552968 | tf_op jit(solution)/shard_map/ppermute | solution.py:486
  44.9 17.5 %collective-permute-start.12 = (bf16[8,160,384]{2,1,0:T(8,128)(2,1)S(1)}, bf16[8,160,384]{2,1,0:T(8,128)(2,1)S(1)}, u32[]{:S(2)}, u32[]{:S(2)}) collective-permute-start(bf16[8,160,384]{2,1,0:T(8,128)(2,1)S(1)} %constant_dynamic-update-slice_fusion.own0), channel_id=1, source_target_pairs={{0,1},{1,0},{2,3},{3,2},{4,5},{5,4},{6,7},{7,6},{8,9},{9,8},{10,11... | collective-permute-start | bytes 2949128 | tf_op jit(solution)/shard_map/ppermute | solution.py:486
  60.8 2.6 collective-permute-start.13
  61.0 15.9 %collective-permute-start.15 = (bf16[4,240,384]{2,1,0:T(8,128)(2,1)S(1)}, bf16[4,240,384]{2,1,0:T(8,128)(2,1)S(1)}, u32[]{:S(2)}, u32[]{:S(2)}) collective-permute-start(bf16[4,240,384]{2,1,0:T(8,128)(2,1)S(1)} %pad_maximum_fusion), channel_id=1, source_target_pairs={{0,4},{1,3},{2,6},{3,1},{4,0},{5,7},{6,2},{7,5},{8,12},{9,11},{10,... | collective-permute-start | bytes 2211848 | tf_op jit(solution)/shard_map/ppermute | solution.py:486
  61.4 15.5 %collective-permute-start.14 = (bf16[4,192,384]{2,1,0:T(8,128)(2,1)S(1)}, bf16[4,192,384]{2,1,0:T(8,128)(2,1)S(1)}, u32[]{:S(2)}, u32[]{:S(2)}) collective-permute-start(bf16[4,192,384]{2,1,0:T(8,128)(2,1)S(1)} %pad_maximum_fusion.1), channel_id=1, source_target_pairs={{0,24},{1,25},{2,26},{3,27},{4,28},{5,29},{6,30},{7,31},{8,0},{9,1... | collective-permute-start | bytes 1769480 | tf_op jit(solution)/shard_map/ppermute | solution.py:486
  78.8 19.7 %collective-permute-start.18 = (bf16[8,240,384]{2,1,0:T(8,128)(2,1)}, bf16[8,240,384]{2,1,0:T(8,128)(2,1)}, u32[]{:S(2)}, u32[]{:S(2)}) collective-permute-start(bf16[8,240,384]{2,1,0:T(8,128)(2,1)} %constant_dynamic-update-slice_fusion.7.b0.refs_1_), channel_id=1, source_target_pairs={{0,2},{1,5},{2,0},{3,7},{4,6},{5,1},{6,4},{7,3},{8,10},{9,13},{10,... | collective-permute-start | bytes 4423688 | tf_op jit(solution)/shard_map/ppermute | solution.py:486
  80.5 17.6 %collective-permute-start.17 = (bf16[8,192,384]{2,1,0:T(8,128)(2,1)S(1)}, bf16[8,192,384]{2,1,0:T(8,128)(2,1)S(1)}, u32[]{:S(2)}, u32[]{:S(2)}) collective-permute-start(bf16[8,192,384]{2,1,0:T(8,128)(2,1)S(1)} %constant_dynamic-update-slice_fusion.5.a0), channel_id=1, source_target_pairs={{0,1},{1,0},{2,3},{3,2},{4,5},{5,4},{6,7},{7,6},{8,9},{9,8},{10,11... | collective-permute-start | bytes 3538952 | tf_op jit(solution)/shard_map/ppermute | solution.py:486
  80.6 17.5 %collective-permute-start.16 = (bf16[4,192,384]{2,1,0:T(8,128)(2,1)S(1)}, bf16[4,192,384]{2,1,0:T(8,128)(2,1)S(1)}, u32[]{:S(2)}, u32[]{:S(2)}) collective-permute-start(bf16[4,192,384]{2,1,0:T(8,128)(2,1)S(1)} %collective-permute-done.11), channel_id=1, source_target_pairs={{0,8},{1,9},{2,10},{3,11},{4,12},{5,13},{6,14},{7,15},{8,16},{9,17... | collective-permute-start | bytes 1769480 | tf_op jit(solution)/shard_map/ppermute | solution.py:486
  98.5 7.4 %collective-permute-start.20 = (bf16[8,240,384]{2,1,0:T(8,128)(2,1)}, bf16[8,240,384]{2,1,0:T(8,128)(2,1)}, u32[]{:S(2)}, u32[]{:S(2)}) collective-permute-start(bf16[8,240,384]{2,1,0:T(8,128)(2,1)} %constant_dynamic-update-slice_fusion.7.b0.refs_1_), channel_id=1, source_target_pairs={{0,1},{1,0},{2,3},{3,2},{4,5},{5,4},{6,7},{7,6},{8,9},{9,8},{10,11... | collective-permute-start | bytes 4423688 | tf_op jit(solution)/shard_map/ppermute | solution.py:486
  98.5 7.4 %collective-permute-start.21 = (bf16[8,240,384]{2,1,0:T(8,128)(2,1)}, bf16[8,240,384]{2,1,0:T(8,128)(2,1)}, u32[]{:S(2)}, u32[]{:S(2)}) collective-permute-start(bf16[8,240,384]{2,1,0:T(8,128)(2,1)} %collective-permute-done.18.b1.refs_2_), channel_id=1, source_target_pairs={{0,1},{1,0},{2,3},{3,2},{4,5},{5,4},{6,7},{7,6},{8,9},{9,8},{10,11... | collective-permute-start | bytes 4423688 | tf_op jit(solution)/shard_map/ppermute | solution.py:486
  100.8 5.1 %collective-permute-start.19 = (bf16[8,192,384]{2,1,0:T(8,128)(2,1)}, bf16[8,192,384]{2,1,0:T(8,128)(2,1)}, u32[]{:S(2)}, u32[]{:S(2)}) collective-permute-start(bf16[8,192,384]{2,1,0:T(8,128)(2,1)} %constant_dynamic-update-slice_fusion.9.a1), channel_id=1, source_target_pairs={{0,1},{1,0},{2,3},{3,2},{4,5},{5,4},{6,7},{7,6},{8,9},{9,8},{10,11... | collective-permute-start | bytes 3538952 | tf_op jit(solution)/shard_map/ppermute | solution.py:486
  106.0 38.6 %copy-start.22 = (s32[112]{0:T(128)S(1)}, s32[112]{0:T(128)}, u32[]{:S(2)}) copy-start(s32[112]{0:T(128)} %concatenate.23.place.refs_0_) | copy-start | bytes 1348
  144.0 11.8 %collective-permute-start.23 = (bf16[16,128,768]{2,1,0:T(8,128)(2,1)}, bf16[16,128,768]{2,1,0:T(8,128)(2,1)S(1)}, u32[]{:S(2)}, u32[]{:S(2)}) collective-permute-start(bf16[16,128,768]{2,1,0:T(8,128)(2,1)} %get-tuple-element.170), channel_id=1, source_target_pairs={{0,1},{1,0},{2,3},{3,2},{4,5},{5,4},{6,7},{7,6},{8,9},{9,8},{10,11... | collective-permute-start | bytes 9437192 | tf_op jit(solution)/shard_map/ppermute | solution.py:486
  144.2 11.6 %collective-permute-start.22 = (bf16[16,24,3072]{2,1,0:T(8,128)(2,1)}, bf16[16,24,3072]{2,1,0:T(8,128)(2,1)S(1)}, u32[]{:S(2)}, u32[]{:S(2)}) collective-permute-start(bf16[16,24,3072]{2,1,0:T(8,128)(2,1)} %get-tuple-element.168), channel_id=1, source_target_pairs={{0,1},{1,0},{2,3},{3,2},{4,5},{5,4},{6,7},{7,6},{8,9},{9,8},{10,11... | collective-permute-start | bytes 7077896 | tf_op jit(solution)/shard_map/ppermute | solution.py:486
  146.8 8.9 %copy-start.24 = (bf16[16,128,768]{2,1,0:T(8,128)(2,1)S(1)}, bf16[16,128,768]{2,1,0:T(8,128)(2,1)}, u32[]{:S(2)}) copy-start(bf16[16,128,768]{2,1,0:T(8,128)(2,1)} %get-tuple-element.232) | copy-start | bytes 9437188
  146.8 10.9 %copy-start.17 = (bf16[768,640]{1,0:T(8,128)(2,1)S(1)}, bf16[768,640]{1,0:T(8,128)(2,1)}, u32[]{:S(2)}) copy-start(bf16[768,640]{1,0:T(8,128)(2,1)} %copy-done.16) | copy-start | bytes 2949124
  155.8 70.0 %copy-start.27 = (bf16[16,24,3072]{2,1,0:T(8,128)(2,1)}, bf16[16,24,3072]{2,1,0:T(8,128)(2,1)S(1)}, u32[]{:S(2)}) copy-start(bf16[16,24,3072]{2,1,0:T(8,128)(2,1)S(1)} %collective-permute-done.22) | copy-start | bytes 7077892
  155.8 52.0 %copy-start.25 = (bf16[16,128,768]{2,1,0:T(8,128)(2,1)}, bf16[16,128,768]{2,1,0:T(8,128)(2,1)S(1)}, u32[]{:S(2)}) copy-start(bf16[16,128,768]{2,1,0:T(8,128)(2,1)S(1)} %collective-permute-done.23) | copy-start | bytes 9437188
  156.2 23.0 %collective-permute-start.25 = (bf16[8,128,768]{2,1,0:T(8,128)(2,1)S(1)}, bf16[8,128,768]{2,1,0:T(8,128)(2,1)S(1)}, u32[]{:S(2)}, u32[]{:S(2)}) collective-permute-start(bf16[8,128,768]{2,1,0:T(8,128)(2,1)S(1)} %add_convert_fusion), channel_id=1, source_target_pairs={{0,2},{1,5},{2,0},{3,7},{4,6},{5,1},{6,4},{7,3},{8,10},{9,13},{10,... | collective-permute-start | bytes 4718600 | tf_op jit(solution)/shard_map/ppermute | solution.py:486
  159.8 9.0 %copy-start.26 = (bf16[16,24,3072]{2,1,0:T(8,128)(2,1)S(1)}, bf16[16,24,3072]{2,1,0:T(8,128)(2,1)}, u32[]{:S(2)}) copy-start(bf16[16,24,3072]{2,1,0:T(8,128)(2,1)} %get-tuple-element.239) | copy-start | bytes 7077892
  168.6 62.0 %copy-start.18 = (bf16[16,24,1152]{2,1,0:T(8,128)(2,1)}, bf16[16,24,1152]{2,1,0:T(8,128)(2,1)S(1)}, u32[]{:S(2)}) copy-start(bf16[16,24,1152]{2,1,0:T(8,128)(2,1)S(1)} %get-tuple-element.225) | copy-start | bytes 2654212
  168.6 10.5 %collective-permute-start.24 = (bf16[16,24,1152]{2,1,0:T(8,128)(2,1)S(1)}, bf16[16,24,1152]{2,1,0:T(8,128)(2,1)S(1)}, u32[]{:S(2)}, u32[]{:S(2)}) collective-permute-start(bf16[16,24,1152]{2,1,0:T(8,128)(2,1)S(1)} %get-tuple-element.175), channel_id=1, source_target_pairs={{0,1},{1,0},{2,3},{3,2},{4,5},{5,4},{6,7},{7,6},{8,9},{9,8},{10,11... | collective-permute-start | bytes 2654216 | tf_op jit(solution)/shard_map/ppermute | solution.py:486
  169.2 27.4 %collective-permute-start.27 = (bf16[8,24,3072]{2,1,0:T(8,128)(2,1)S(1)}, bf16[8,24,3072]{2,1,0:T(8,128)(2,1)S(1)}, u32[]{:S(2)}, u32[]{:S(2)}) collective-permute-start(bf16[8,24,3072]{2,1,0:T(8,128)(2,1)S(1)} %add_convert_fusion.1), channel_id=1, source_target_pairs={{0,2},{1,5},{2,0},{3,7},{4,6},{5,1},{6,4},{7,3},{8,10},{9,13},{10,... | collective-permute-start | bytes 3538952 | tf_op jit(solution)/shard_map/ppermute | solution.py:486
  179.2 51.4 %copy-start.31 = (bf16[16,24,1152]{2,1,0:T(8,128)(2,1)}, bf16[16,24,1152]{2,1,0:T(8,128)(2,1)S(1)}, u32[]{:S(2)}) copy-start(bf16[16,24,1152]{2,1,0:T(8,128)(2,1)S(1)} %collective-permute-done.24) | copy-start | bytes 2654212
  179.2 28.6 %copy-start.28 = (bf16[8,128,768]{2,1,0:T(8,128)(2,1)}, bf16[8,128,768]{2,1,0:T(8,128)(2,1)S(1)}, u32[]{:S(2)}) copy-start(bf16[8,128,768]{2,1,0:T(8,128)(2,1)S(1)} %collective-permute-done.25) | copy-start | bytes 4718596
  179.5 23.0 %collective-permute-start.26 = (bf16[4,128,768]{2,1,0:T(8,128)(2,1)S(1)}, bf16[4,128,768]{2,1,0:T(8,128)(2,1)S(1)}, u32[]{:S(2)}, u32[]{:S(2)}) collective-permute-start(bf16[4,128,768]{2,1,0:T(8,128)(2,1)S(1)} %add_convert_fusion.2), channel_id=1, source_target_pairs={{0,4},{1,3},{2,6},{3,1},{4,0},{5,7},{6,2},{7,5},{8,12},{9,11},{10,... | collective-permute-start | bytes 2359304 | tf_op jit(solution)/shard_map/ppermute | solution.py:486
  180.2 22.3 %collective-permute-start.28 = (bf16[8,24,1152]{2,1,0:T(8,128)(2,1)S(1)}, bf16[8,24,1152]{2,1,0:T(8,128)(2,1)S(1)}, u32[]{:S(2)}, u32[]{:S(2)}) collective-permute-start(bf16[8,24,1152]{2,1,0:T(8,128)(2,1)S(1)} %add_convert_fusion.5), channel_id=1, source_target_pairs={{0,2},{1,5},{2,0},{3,7},{4,6},{5,1},{6,4},{7,3},{8,10},{9,13},{10,... | collective-permute-start | bytes 1327112 | tf_op jit(solution)/shard_map/ppermute | solution.py:486
  196.6 29.1 %copy-start.29 = (bf16[8,24,3072]{2,1,0:T(8,128)(2,1)}, bf16[8,24,3072]{2,1,0:T(8,128)(2,1)S(1)}, u32[]{:S(2)}) copy-start(bf16[8,24,3072]{2,1,0:T(8,128)(2,1)S(1)} %collective-permute-done.27) | copy-start | bytes 3538948
  202.5 28.1 %copy-start.37 = (bf16[8,24,1152]{2,1,0:T(8,128)(2,1)}, bf16[8,24,1152]{2,1,0:T(8,128)(2,1)S(1)}, u32[]{:S(2)}) copy-start(bf16[8,24,1152]{2,1,0:T(8,128)(2,1)S(1)} %collective-permute-done.28) | copy-start | bytes 1327108
  202.5 2.9 %collective-permute-start.29 = (bf16[16,32,1152]{2,1,0:T(8,128)(2,1)S(1)}, bf16[16,32,1152]{2,1,0:T(8,128)(2,1)S(1)}, u32[]{:S(2)}, u32[]{:S(2)}) collective-permute-start(bf16[16,32,1152]{2,1,0:T(8,128)(2,1)S(1)} %get-tuple-element.191), channel_id=1, source_target_pairs={{0,1},{1,0},{2,3},{3,2},{4,5},{5,4},{6,7},{7,6},{8,9},{9,8},{10,11... | collective-permute-start | bytes 3538952 | tf_op jit(solution)/shard_map/ppermute | solution.py:486
  202.8 21.3 %collective-permute-start.30 = (bf16[4,24,3072]{2,1,0:T(8,128)(2,1)S(1)}, bf16[4,24,3072]{2,1,0:T(8,128)(2,1)S(1)}, u32[]{:S(2)}, u32[]{:S(2)}) collective-permute-start(bf16[4,24,3072]{2,1,0:T(8,128)(2,1)S(1)} %add_convert_fusion.4), channel_id=1, source_target_pairs={{0,4},{1,3},{2,6},{3,1},{4,0},{5,7},{6,2},{7,5},{8,12},{9,11},{10,... | collective-permute-start | bytes 1769480 | tf_op jit(solution)/shard_map/ppermute | solution.py:486
  205.6 18.5 %collective-permute-start.32 = (bf16[8,32,1152]{2,1,0:T(8,128)(2,1)S(1)}, bf16[8,32,1152]{2,1,0:T(8,128)(2,1)S(1)}, u32[]{:S(2)}, u32[]{:S(2)}) collective-permute-start(bf16[8,32,1152]{2,1,0:T(8,128)(2,1)S(1)} %add_convert_fusion.3), channel_id=1, source_target_pairs={{0,2},{1,5},{2,0},{3,7},{4,6},{5,1},{6,4},{7,3},{8,10},{9,13},{10,... | collective-permute-start | bytes 1769480 | tf_op jit(solution)/shard_map/ppermute | solution.py:486
  207.2 14.3 %collective-permute-start.31 = (bf16[4,24,1152]{2,1,0:T(8,128)(2,1)S(1)}, bf16[4,24,1152]{2,1,0:T(8,128)(2,1)S(1)}, u32[]{:S(2)}, u32[]{:S(2)}) collective-permute-start(bf16[4,24,1152]{2,1,0:T(8,128)(2,1)S(1)} %add_convert_fusion.7), channel_id=1, source_target_pairs={{0,4},{1,3},{2,6},{3,1},{4,0},{5,7},{6,2},{7,5},{8,12},{9,11},{10,... | collective-permute-start | bytes 663560 | tf_op jit(solution)/shard_map/ppermute | solution.py:486
  208.1 18.6 %collective-permute-start.40 = (bf16[128,768]{1,0:T(8,128)(2,1)S(1)}, bf16[128,768]{1,0:T(8,128)(2,1)S(1)}, u32[]{:S(2)}, u32[]{:S(2)}) collective-permute-start(bf16[128,768]{1,0:T(8,128)(2,1)S(1)} %get-tuple-element.248), channel_id=1, source_target_pairs={{0,8},{1,9},{2,10},{3,11},{4,12},{5,13},{6,14},{7,15},{8,16},{9,17... | collective-permute-start | bytes 589832 | tf_op jit(solution)/shard_map/ppermute | solution.py:486
  208.1 19.2 %collective-permute-start.41 = (bf16[128,768]{1,0:T(8,128)(2,1)S(1)}, bf16[128,768]{1,0:T(8,128)(2,1)S(1)}, u32[]{:S(2)}, u32[]{:S(2)}) collective-permute-start(bf16[128,768]{1,0:T(8,128)(2,1)S(1)} %get-tuple-element.247), channel_id=1, source_target_pairs={{0,16},{1,17},{2,18},{3,19},{4,20},{5,21},{6,22},{7,23},{8,24},{9,... | collective-permute-start | bytes 589832 | tf_op jit(solution)/shard_map/ppermute | solution.py:486
  221.5 9.2 %copy-start.41 = (bf16[4,24,1152]{2,1,0:T(8,128)(2,1)}, bf16[4,24,1152]{2,1,0:T(8,128)(2,1)S(1)}, u32[]{:S(2)}) copy-start(bf16[4,24,1152]{2,1,0:T(8,128)(2,1)S(1)} %collective-permute-done.31) | copy-start | bytes 663556
  221.5 9.9 %collective-permute-start.42 = (bf16[128,768]{1,0:T(8,128)(2,1)S(1)}, bf16[128,768]{1,0:T(8,128)(2,1)S(1)}, u32[]{:S(2)}, u32[]{:S(2)}) collective-permute-start(bf16[128,768]{1,0:T(8,128)(2,1)S(1)} %get-tuple-element.246), channel_id=1, source_target_pairs={{0,24},{1,25},{2,26},{3,27},{4,28},{5,29},{6,30},{7,31},{8,0},{9,1... | collective-permute-start | bytes 589832 | tf_op jit(solution)/shard_map/ppermute | solution.py:486
  224.2 20.1 %collective-permute-start.33 = (bf16[4,32,1152]{2,1,0:T(8,128)(2,1)S(1)}, bf16[4,32,1152]{2,1,0:T(8,128)(2,1)S(1)}, u32[]{:S(2)}, u32[]{:S(2)}) collective-permute-start(bf16[4,32,1152]{2,1,0:T(8,128)(2,1)S(1)} %add_convert_fusion.6), channel_id=1, source_target_pairs={{0,4},{1,3},{2,6},{3,1},{4,0},{5,7},{6,2},{7,5},{8,12},{9,11},{10,... | collective-permute-start | bytes 884744 | tf_op jit(solution)/shard_map/ppermute | solution.py:486
  226.7 26.0 %collective-permute-start.37 = (bf16[24,3072]{1,0:T(8,128)(2,1)}, bf16[24,3072]{1,0:T(8,128)(2,1)}, u32[]{:S(2)}, u32[]{:S(2)}) collective-permute-start(bf16[24,3072]{1,0:T(8,128)(2,1)} %get-tuple-element.251), channel_id=1, source_target_pairs={{0,8},{1,9},{2,10},{3,11},{4,12},{5,13},{6,14},{7,15},{8,16},{9,17... | collective-permute-start | bytes 442376 | tf_op jit(solution)/shard_map/ppermute | solution.py:486
  226.7 26.0 %collective-permute-start.38 = (bf16[24,3072]{1,0:T(8,128)(2,1)}, bf16[24,3072]{1,0:T(8,128)(2,1)}, u32[]{:S(2)}, u32[]{:S(2)}) collective-permute-start(bf16[24,3072]{1,0:T(8,128)(2,1)} %get-tuple-element.250), channel_id=1, source_target_pairs={{0,16},{1,17},{2,18},{3,19},{4,20},{5,21},{6,22},{7,23},{8,24},{9,... | collective-permute-start | bytes 442376 | tf_op jit(solution)/shard_map/ppermute | solution.py:486
  227.3 17.7 %copy-start.42 = (bf16[128,768]{1,0:T(8,128)(2,1)}, bf16[128,768]{1,0:T(8,128)(2,1)S(1)}, u32[]{:S(2)}) copy-start(bf16[128,768]{1,0:T(8,128)(2,1)S(1)} %collective-permute-done.41) | copy-start | bytes 589828
  227.3 25.4 %collective-permute-start.39 = (bf16[24,3072]{1,0:T(8,128)(2,1)}, bf16[24,3072]{1,0:T(8,128)(2,1)}, u32[]{:S(2)}, u32[]{:S(2)}) collective-permute-start(bf16[24,3072]{1,0:T(8,128)(2,1)} %get-tuple-element.249), channel_id=1, source_target_pairs={{0,24},{1,25},{2,26},{3,27},{4,28},{5,29},{6,30},{7,31},{8,0},{9,1... | collective-permute-start | bytes 442376 | tf_op jit(solution)/shard_map/ppermute | solution.py:486
  231.3 14.1 %copy-start.44 = (bf16[128,768]{1,0:T(8,128)(2,1)}, bf16[128,768]{1,0:T(8,128)(2,1)S(1)}, u32[]{:S(2)}) copy-start(bf16[128,768]{1,0:T(8,128)(2,1)S(1)} %collective-permute-done.42) | copy-start | bytes 589828
  231.3 8.6 %collective-permute-start.43 = (bf16[24,1152]{1,0:T(8,128)(2,1)S(1)}, bf16[24,1152]{1,0:T(8,128)(2,1)S(1)}, u32[]{:S(2)}, u32[]{:S(2)}) collective-permute-start(bf16[24,1152]{1,0:T(8,128)(2,1)S(1)} %get-tuple-element.257), channel_id=1, source_target_pairs={{0,8},{1,9},{2,10},{3,11},{4,12},{5,13},{6,14},{7,15},{8,16},{9,17... | collective-permute-start | bytes 165896 | tf_op jit(solution)/shard_map/ppermute | solution.py:486
  239.9 12.7 %collective-permute-start.44 = (bf16[24,1152]{1,0:T(8,128)(2,1)}, bf16[24,1152]{1,0:T(8,128)(2,1)}, u32[]{:S(2)}, u32[]{:S(2)}) collective-permute-start(bf16[24,1152]{1,0:T(8,128)(2,1)} %get-tuple-element.256), channel_id=1, source_target_pairs={{0,16},{1,17},{2,18},{3,19},{4,20},{5,21},{6,22},{7,23},{8,24},{9,... | collective-permute-start | bytes 165896 | tf_op jit(solution)/shard_map/ppermute | solution.py:486
  245.0 7.6 %collective-permute-start.45 = (bf16[24,1152]{1,0:T(8,128)(2,1)}, bf16[24,1152]{1,0:T(8,128)(2,1)}, u32[]{:S(2)}, u32[]{:S(2)}) collective-permute-start(bf16[24,1152]{1,0:T(8,128)(2,1)} %get-tuple-element.255), channel_id=1, source_target_pairs={{0,24},{1,25},{2,26},{3,27},{4,28},{5,29},{6,30},{7,31},{8,0},{9,1... | collective-permute-start | bytes 165896 | tf_op jit(solution)/shard_map/ppermute | solution.py:486
  255.7 9.2 %collective-permute-start.36 = (bf16[32,1152]{1,0:T(8,128)(2,1)S(1)}, bf16[32,1152]{1,0:T(8,128)(2,1)S(1)}, u32[]{:S(2)}, u32[]{:S(2)}) collective-permute-start(bf16[32,1152]{1,0:T(8,128)(2,1)S(1)} %get-tuple-element.253), channel_id=1, source_target_pairs={{0,24},{1,25},{2,26},{3,27},{4,28},{5,29},{6,30},{7,31},{8,0},{9,1... | collective-permute-start | bytes 221192 | tf_op jit(solution)/shard_map/ppermute | solution.py:486
  256.8 8.3 %collective-permute-start.35 = (bf16[32,1152]{1,0:T(8,128)(2,1)S(1)}, bf16[32,1152]{1,0:T(8,128)(2,1)S(1)}, u32[]{:S(2)}, u32[]{:S(2)}) collective-permute-start(bf16[32,1152]{1,0:T(8,128)(2,1)S(1)} %get-tuple-element.254), channel_id=1, source_target_pairs={{0,16},{1,17},{2,18},{3,19},{4,20},{5,21},{6,22},{7,23},{8,24},{9,... | collective-permute-start | bytes 221192 | tf_op jit(solution)/shard_map/ppermute | solution.py:486
  258.8 6.3 %collective-permute-start.34 = (bf16[32,1152]{1,0:T(8,128)(2,1)S(1)}, bf16[32,1152]{1,0:T(8,128)(2,1)S(1)}, u32[]{:S(2)}, u32[]{:S(2)}) collective-permute-start(bf16[32,1152]{1,0:T(8,128)(2,1)S(1)} %get-tuple-element.252), channel_id=1, source_target_pairs={{0,8},{1,9},{2,10},{3,11},{4,12},{5,13},{6,14},{7,15},{8,16},{9,17... | collective-permute-start | bytes 221192 | tf_op jit(solution)/shard_map/ppermute | solution.py:486
  (36 other events, 134.7 us)

commit v2 on v1

--- a/solution.py
+++ b/solution.py
@@ -15,6 +15,7 @@
 FAR = 1e30
 CHIPS = 16
 BLOCK = 384
+SMALL, LARGE = (32, 96), (112, 128)
 MIB = 1024 * 1024
 
 BF = jnp.bfloat16
@@ -146,7 +147,7 @@
 
 def qkv_kernel(
     place, own0, own1, other0, other1, rows_ref,
-    vec_ref, fcb_ref, h1_turned, qkv_ref,
+    vec_ref, fcb_ref, h1_turned, qkv_ref, wq_out,
     wq, h1, qvb, small, sems,
 ):
     sources = (own0, own1, other0, other1)
@@ -175,10 +176,13 @@
         h1_turned[...] = low.T
 
     wait_all(wq.at[side], sems.at[side])
+    keeping = pltpu.make_async_copy(wq.at[side], wq_out.at[side], sems.at[3])
+    keeping.start()
     bias = jnp.concatenate(
         [qvb[side, 6:7, :], jnp.zeros((1, BLOCK), F32), qvb[2 + side, 6:7, :]], axis=1
     )
     qkv_ref[0] = (dot(h1[...], wq[side]) + bias).astype(BF)
+    keeping.wait()
 
 
 def two_heads(pair_rows, low_half):
@@ -210,11 +214,11 @@
         ).astype(BF)
 
 
-def give_rows(place, total, keep_ref, send_ref, extra=None):
+def give_rows(place, tables, total, keep_ref, send_ref, extra=None):
     for chip in range(CHIPS):
         below = None if extra is None else extra(chip)
         for which, target in enumerate((keep_ref, send_ref)):
-            slot = place[32 + 64 * which + chip]
+            slot = place[tables[which] + chip]
             owner = place[48] if which == 0 else 1 - place[48]
             share = total[pl.ds(pl.multiple_of(48 * chip + 24 * owner, 8), 24), :]
             if below is not None:
@@ -234,7 +238,7 @@
 
 def mlp_kernel(
     place, counts, a0, a1, a2, a3, b0, b1, b2, b3, att_ref, rows_ref, gout_ref, vec_ref, fcb_ref,
-    out_ref, gresid_ref, glow_ref, keep1_ref, send1_ref, keep2, send2,
+    out_ref, gresid_ref, glow_ref, keep1_ref, send1_ref, keep2, send2, wo_out,
     w1, w2, wo, h2, h2_turned, normed, total, gh2, product1, product2, stage, stage_end, fcg, scales,
     sems1, sems2, sems,
 ):
@@ -267,6 +271,7 @@
         each_piece(place, 64, (a0, a1, a2, a3), work1)
         each_piece(place, 0, (b0, b1, b2, b3), work2)
         wait_all(wo, sems.at[2])
+        pltpu.make_async_copy(wo, wo_out, sems.at[2]).start()
         bias = row_of(vec_ref, 2)
         for part in range(2):
             lanes = slice(BLOCK * part, BLOCK * (part + 1))
@@ -292,14 +297,14 @@
     branch = dot(activated, w2[rows_of, :])
     gradient = dot(ghidden, w1[block], 1, 1)
     fcg[block] = stack_rows([None, None, None, sum_rows(ghidden)])
-    give_rows(place, product1, keep1_ref, send1_ref)
+    give_rows(place, LARGE, product1, keep1_ref, send1_ref)
     for pair in range(4):
         for which, target in enumerate((keep2, send2)):
             chip = 4 * block + pair
             owner = place[48] if which == 0 else 1 - place[48]
             start = pl.multiple_of(192 * pair + 96 * owner, 8)
             stage[which, chip] = product2[pl.ds(start, 96), :].astype(BF)
-            slot = place[32 + 64 * which + chip]
+            slot = place[LARGE[which] + chip]
             pltpu.make_async_copy(stage.at[which, chip], target.at[slot, pl.ds(0, 96)], sems.at[which]).start()
 
     @pl.when(block < pl.num_programs(0) - 1)
@@ -335,22 +340,17 @@
                 owner = place[48] if which == 0 else 1 - place[48]
                 share = product1[pl.ds(pl.multiple_of(48 * chip + 24 * owner, 8), 24), :]
                 stage_end[which, chip] = jnp.concatenate([share, below], axis=0).astype(BF)
-                slot = place[32 + 64 * which + chip]
+                slot = place[LARGE[which] + chip]
                 pltpu.make_async_copy(
                     stage_end.at[which, chip], target.at[slot, pl.ds(96, 32)], sems.at[which]
                 ).start()
+        wait_all(wo, sems.at[2])
         wait_all(keep2, sems.at[0])
         wait_all(send2, sems.at[1])
 
 
-def attention_back_kernel(
-    side, place, own0, own1, other0, other1, qkv_ref, far_ref, glow_ref, gqkv_ref, wo, sem
-):
-    @pl.when(pl.program_id(0) == 0)
-    def _():
-        bring_out_weight(place, (own0, own1, other0, other1), wo, sem)
-        wait_all(wo, sem)
-
+def attention_back_kernel(side, wo, qkv_ref, far_ref, glow_ref, *refs):
+    gqkv_ref = refs[-1]
     low = glow_ref[...]
     mine = slice(BLOCK * side, BLOCK * (side + 1))
     gatt = (
@@ -387,47 +387,35 @@
             ).astype(BF)
 
 
-def qkv_grad_step(side, place, sources, h1_turned, gqkv_ref, product, wq, sems):
+def qkv_grad_kernel(
+    place, h1_turned, gqkv_ref, wq_ref, gh1_ref, sums_ref, keep_ref, send_ref, product
+):
     part = pl.program_id(0)
-
-    @pl.when(part == 0)
-    def _():
-        bring_qkv_weight(place, sources, side, wq, None, sems)
-
     product[...] = dot(h1_turned[...], gqkv_ref[...])
-    wait_all(wq.at[part], sems.at[part])
-    return part, dot(gqkv_ref[...], wq[part], 1, 1)
-
-
-def qkv_grad_kernel(
-    place, own0, own1, other0, other1, h1_turned, gqkv_ref, gh1_ref, sums_ref, keep_ref, send_ref, product, wq, sems
-):
-    part, gradient = qkv_grad_step(
-        0, place, (own0, own1, other0, other1), h1_turned, gqkv_ref, product, wq, sems
-    )
+    gradient = dot(gqkv_ref[...], wq_ref[0], 1, 1)
     gh1_ref[...] = jnp.where(part == 0, gradient, gh1_ref[...] + gradient)
     sums_ref[part] = stack_rows([None, None, sum_rows(gqkv_ref[...])])
-    give_rows(place, product, keep_ref, send_ref)
+    give_rows(place, SMALL, product, keep_ref, send_ref)
 
 
 def input_kernel(
-    place, own0, own1, other0, other1, h1_turned, gqkv_ref, before_ref, rows_ref, vec_ref, gresid, gh1,
+    place, h1_turned, gqkv_ref, wq_ref, before_ref, rows_ref, vec_ref, gresid, gh1,
     ginput_ref, keep_ref, send_ref,
-    product, wq, sums, gresid_here, total, sems, sems_in,
+    product, sums, gresid_here, total, sems_in,
 ):
+    part = pl.program_id(0)
     loads = [
         pltpu.make_async_copy(gh1, total, sems_in.at[0]),
         pltpu.make_async_copy(gresid, gresid_here, sems_in.at[1]),
     ]
 
-    @pl.when(pl.program_id(0) == 0)
+    @pl.when(part == 0)
     def _():
         for load in loads:
             load.start()
 
-    part, gradient = qkv_grad_step(
-        1, place, (own0, own1, other0, other1), h1_turned, gqkv_ref, product, wq, sems
-    )
+    product[...] = dot(h1_turned[...], gqkv_ref[...])
+    gradient = dot(gqkv_ref[...], wq_ref[0], 1, 1)
 
     @pl.when(part == 0)
     def _():
@@ -438,7 +426,7 @@
 
     @pl.when(part < 2)
     def _():
-        give_rows(place, product, keep_ref, send_ref, lambda chip: jnp.zeros((8, BLOCK), F32))
+        give_rows(place, SMALL, product, keep_ref, send_ref, lambda chip: jnp.zeros((8, BLOCK), F32))
 
     @pl.when(part == 2)
     def _():
@@ -455,7 +443,41 @@
             biases = (before_ref[0], sums[0], before_ref[2], sums[2])[chip // 4]
             return stack_rows([gain[:, lanes], shift[:, lanes]]) + biases
 
-        give_rows(place, product, keep_ref, send_ref, below)
+        give_rows(place, SMALL, product, keep_ref, send_ref, below)
+
+
+def add_up(parts):
+    return sum(part.astype(F32) for part in parts)
+
+
+def give_vector(target, line, device):
+    count, columns = target.shape[0], line.shape[1]
+    start = lax.rem(device, columns // count) * count
+    moved = pltpu.roll(line, lax.rem(columns - start, columns), 1)
+    target[...] = moved[:, :count].reshape(count)
+
+
+def last_second_kernel(place, *refs):
+    sources, (fc2_out, out_out, gain, shift, fc2_bias, out_bias, fc1_bias) = refs[:6], refs[6:]
+    total = add_up([source[0] for source in sources])
+    fc2_out[...] = total[:96]
+    out_out[...] = total[96:120]
+    device = place[49]
+    for line, target in enumerate((gain, shift, fc2_bias, fc1_bias, out_bias)):
+        give_vector(target, total[120 + line : 121 + line], device)
+
+
+def last_heads_kernel(place, *refs):
+    sources, (grad_out, gain, shift, bias) = refs[:12], refs[12:]
+    total_a = add_up([source[0] for source in sources[:6]])
+    total_c = add_up([source[0] for source in sources[6:]])
+    for part in range(3):
+        lanes = slice(BLOCK * part, BLOCK * (part + 1))
+        grad_out[:, 2 * BLOCK * part : 2 * BLOCK * part + BLOCK] = total_a[:, lanes]
+        grad_out[:, 2 * BLOCK * part + BLOCK : 2 * BLOCK * (part + 1)] = total_c[:24, lanes]
+    device = place[49]
+    for line, target in enumerate((gain, shift, bias)):
+        give_vector(target, total_c[24 + line : 25 + line, 2 * BLOCK :], device)
 
 
 def after(value, *others):
@@ -481,6 +503,8 @@
         self.first = table(lambda z, x, y, c: (z, x, 1 - y, c) if c else (z, 1 - x, y, c))
         self.second = table(lambda z, x, y, c: (z, 1 - x, y, c) if c else (z, x, 1 - y, c))
         self.cores = table(lambda z, x, y, c: (z, x, y, 1 - c))
+        self.near = table(lambda z, x, y, c: (z ^ 1, x, y, c))
+        self.far = table(lambda z, x, y, c: (z ^ 2, x, y, c))
 
     def move(self, value, pairs):
         return lax.ppermute(value, AXES, pairs)
@@ -501,15 +525,25 @@
         x_first = chip(whose, index % 2, (index // 2) % 2, (index // 4) % 4)
         chips = jnp.arange(16, dtype=jnp.int32)
         turn_x, turn_y = ((chips // 2) % 2) ^ x, (chips % 2) ^ y
-        step = (chips // 4 - z) % self.depth
-        slots0 = turn_y * 8 + turn_x * 4 + step
-        slots1 = turn_x * 8 + turn_y * 4 + step
-        own_slots = jnp.where(core == 0, slots0, slots1)
-        other_slots = jnp.where(core == 0, slots1, slots0)
+        far_z = (chips // 4) ^ z
+        near, wide_step = far_z % 2, far_z // 2
+
+        def slots(order):
+            turns = {"x": turn_x, "y": turn_y, "near": near, "far": wide_step}
+            return sum(turns[name] * weight for name, weight in zip(order, (8, 4, 2, 1)))
+
         rest = jnp.where(jnp.arange(16) == 1, dp * 4 + fsdp, core).astype(jnp.int32)
-        return jnp.concatenate([z_first, own_slots, rest, x_first, other_slots]).astype(jnp.int32)
-
-    def gather(self, piece_a, piece_b1, piece_b2):
+        tables = []
+        for orders in (
+            (("y", "x", "near", "far"), ("x", "y", "near", "far")),
+            (("y", "near", "x", "far"), ("x", "near", "y", "far")),
+        ):
+            both = [slots(order) for order in orders]
+            tables += [jnp.where(core == 0, both[0], both[1]), jnp.where(core == 0, both[1], both[0])]
+        parts = [z_first, tables[0], rest, x_first] + tables[1:]
+        return jnp.concatenate(parts).astype(jnp.int32)
+
+    def gather(self, piece_a, piece_b1, piece_b2, early):
         hold = lax.optimization_barrier
         up = lambda value, step: self.move(value, self.ups[step])
         a_one, a_three, b1_two = hold((up(piece_a, 1), up(piece_a, 3), self.move(piece_b1, self.first)))
@@ -518,12 +552,14 @@
         a_four = jnp.stack([piece_a, a_one, a_two, a_three])
         b1_four = jnp.concatenate([b1_two, b1_four])
         piece_b2 = after(piece_b2, a_two)
-        a_rest, b2_one, b2_three = hold((self.move(a_four, self.first), up(piece_b2, 1), up(piece_b2, 3)))
+        a_rest, b2_one, b2_three, early = hold(
+            (self.move(a_four, self.first), up(piece_b2, 1), up(piece_b2, 3), early)
+        )
         a_eight = jnp.concatenate([a_four, a_rest])
         a_other, b2_two, b1_one = hold((self.move(a_eight, self.second), up(b2_one, 1), up(b1_four, 1)))
         b2_four = jnp.stack([piece_b2, b2_one, b2_two, b2_three])
         a = self.finish(a_eight, a_other)
-        return a, (b1_four, b1_one, up(b1_four, 3)), (b2_four, self.move(b2_four, self.first))
+        return a, (b1_four, b1_one, up(b1_four, 3)), (b2_four, self.move(b2_four, self.first)), early
 
     def gather_on(self, b1, b2):
         b1_four, b1_one, b1_three = b1
@@ -541,28 +577,9 @@
     def finish(self, eight, rest):
         return (eight, rest, self.move(eight, self.cores), self.move(rest, self.cores))
 
-    def reduce(self, stage, state):
-        keep = state[0]
-        wide = lambda *terms: sum(term.astype(F32) for term in terms)
-        if stage == 0:
-            return keep, self.move(state[1], self.cores)
-        got = state[1]
-        if stage == 1:
-            return keep, got, self.move(wide(keep[8:], got[8:]).astype(BF), self.second)
-        got1 = state[2]
-        if stage == 2:
-            part = wide(keep[4:8], got[4:8], got1[4:]).astype(BF)
-            return keep, got, got1, self.move(part, self.first)
-        got2 = state[3]
-        if stage == 3:
-            parts = [
-                wide(keep[step], got[step], got1[step], got2[step]).astype(BF) for step in (1, 2, 3)
-            ]
-            return state + tuple(
-                self.move(part, self.ups[step]) for part, step in zip(parts, (1, 2, 3))
-            )
-        return wide(keep[0], got[0], got1[0], got2[0], *state[4:])
-
+    def fold(self, state):
+        left = 32 >> (len(state) - 1)
+        return add_up([part[left // 2 : left] for part in state]).astype(BF)
 
 def full_pieces(full, blocks):
     split = full.reshape((CHIPS, 48) + full.shape[1:])
@@ -652,8 +669,7 @@
                 jnp.arange(32, dtype=jnp.int32) % 16,
                 jnp.arange(16, dtype=jnp.int32),
                 jnp.zeros((16,), jnp.int32),
-                jnp.arange(32, dtype=jnp.int32) % 16,
-                jnp.arange(16, dtype=jnp.int32),
+                jnp.arange(80, dtype=jnp.int32) % 16,
             ]
         )
         whole = [lax.all_gather(part, AXES, axis=0, tiled=True) for part in small_parts]
@@ -670,6 +686,7 @@
         whole_out = lax.all_gather(out_weight, AXES, axis=0, tiled=True)
         whole_fc1 = lax.all_gather(fc1_weight, AXES, axis=0, tiled=True)
         whole_fc2 = lax.all_gather(fc2_weight, AXES, axis=0, tiled=True)
+        split = whole_fc2.reshape(CHIPS, 2, 96, 2, BLOCK).transpose(1, 0, 3, 2, 4).reshape(32, 192, BLOCK)
         gathered_a = eights(
             jnp.concatenate([full_pieces(whole_qkv.reshape(width, 3, 2, BLOCK), 3), lines], axis=1)
         )
@@ -680,7 +697,8 @@
         )
 
     if by_hand:
-        gathered_a, on_b1, on_b2 = links.gather(*pieces)
+        gathered_a, on_b1, on_b2, early = links.gather(*pieces, (rows_in, gout, far, far_turned))
+        rows_in, gout, far, far_turned = early
 
 
     def call(kernel, operands, out_shape, out_specs, in_specs, flops, mib, vmem_mib, grid, scratch=(), name=None):
@@ -709,24 +727,19 @@
     steps = hidden_width // wide
     third = 3 * BLOCK
 
-    def join(value, *states):
-        if not by_hand:
-            return (value,) + states
-        return lax.optimization_barrier((value,) + states)
-
-    def reduce(stage, state):
-        return links.reduce(stage, state) if by_hand else state
-
-    vec, fcb, h1_turned, qkv = call(
+    def join(value, *others):
+        return after(value, *others) if by_hand else value
+
+    vec, fcb, h1_turned, qkv, wq = call(
         qkv_kernel,
         (place, *gathered_a, rows_in),
         (
             struct((2, 16, BLOCK), F32), struct((steps, 1, wide), F32), struct((width, rows), BF),
-            struct((2, rows, third), BF),
+            struct((2, rows, third), BF), struct((2, width, third), BF),
         ),
         (
             fixed(2, 16, BLOCK), fixed(steps, 1, wide), fixed(width, rows),
-            pl.BlockSpec((1, rows, third), lambda step: (step, 0, 0)),
+            pl.BlockSpec((1, rows, third), lambda step: (step, 0, 0)), anywhere,
         ),
         [smem] + [anywhere] * 4 + [fixed(rows, width)],
         2 * rows * width * 3 * width,
@@ -735,7 +748,7 @@
         grid=(2,),
         scratch=(
             buffer((2, width, third), BF), buffer((rows, width), BF), buffer((4, 16, BLOCK), F32),
-            buffer((32, 16, BLOCK), BF), flag((3,)),
+            buffer((32, 16, BLOCK), BF), flag((4,)),
         ),
         name="qkv",
     )
@@ -760,11 +773,14 @@
         gathered_b1, gathered_b2 = links.gather_end(on_b1, on_b2)
 
     step_shares = lambda height, columns: pl.BlockSpec((CHIPS, height, columns), lambda step: (0, 0, step))
-    out, gresid, glow, keep_1, send_1, keep_2, send_2 = call(
+    out, gresid, glow, keep_1, send_1, keep_2, send_2, wo = call(
         mlp_kernel,
         (place, counts, *gathered_b1, *gathered_b2, att, rows_in, gout, vec, fcb),
-        (low_rows, wide_rows, low_rows) + (shares(24, hidden_width),) * 2 + (shares(128, wide),) * 2,
-        (fixed(rows, width),) * 3 + (step_shares(24, wide),) * 2 + (anywhere,) * 2,
+        (low_rows, wide_rows, low_rows)
+        + (shares(24, hidden_width),) * 2
+        + (shares(128, wide),) * 2
+        + (struct((2, width, BLOCK), BF),),
+        (fixed(rows, width),) * 3 + (step_shares(24, wide),) * 2 + (anywhere,) * 3,
         [smem, smem] + [anywhere] * 8 + [fixed(rows, width)] * 3 + [
             fixed(2, 16, BLOCK), fixed(steps, 1, wide),
         ],
@@ -781,55 +797,74 @@
         ),
         name="mlp",
     )
-    state_2, state_1 = reduce(0, (keep_2, send_2)), reduce(0, (keep_1, send_1))
-
-    def attention_back(side, gradient):
-        return call(
+    if by_hand:
+        state_2 = keep_2, links.move(send_2, links.cores)
+        state_1 = keep_1, links.move(after(send_1, keep_2), links.cores)
+
+    def attention_back(side, gradient, first, count, vmem_mib, before=()):
+        some_rows = lambda columns: pl.BlockSpec((padded, columns), lambda image: (first + image, 0))
+        return pl.pallas_call(
             lambda *refs: attention_back_kernel(side, *refs),
-            (place, *gathered_b2, qkv, far_turned, gradient),
-            struct((rows, third), BF),
-            image_rows(third),
-            [smem] + [anywhere] * 4 + [
-                pl.BlockSpec((1, padded, third), lambda image: (side, image, 0)), image_far, image_rows(width),
-            ],
-            8 * rows * 256 * width,
-            8,
-            20,
-            grid=(images,),
-            scratch=(buffer((2, width, BLOCK), BF), flag),
+            grid=(count,),
+            out_shape=struct((rows, third), BF),
+            in_specs=[
+                fixed(2, width, BLOCK),
+                pl.BlockSpec((1, padded, third), lambda image: (side, first + image, 0)),
+                pl.BlockSpec((1, padded, padded), lambda image: (first + image, 0, 0)),
+                some_rows(width),
+            ]
+            + [anywhere] * len(before),
+            out_specs=some_rows(third),
+            input_output_aliases={4: 0} if before else {},
+            compiler_params=pltpu.CompilerParams(vmem_limit_bytes=vmem_mib * MIB),
+            cost_estimate=pl.CostEstimate(flops=1, bytes_accessed=1, transcendentals=0),
             name="attention_back",
-        )
-
-    gqkv_0 = attention_back(0, glow)
-    gqkv_0, state_1, state_2 = join(gqkv_0, state_1, state_2)
-    state_2, state_1 = reduce(1, state_2), reduce(1, state_1)
-
+        )(wo, qkv, far_turned, gradient, *before)
+
+    gqkv_0 = attention_back(0, glow, 0, images // 2, 60)
+    part_2 = glow
+    if by_hand:
+        state_2, gqkv_0 = lax.optimization_barrier((state_2, gqkv_0))
+        part_2 = links.fold(state_2)
+        state_2 += (links.move(part_2, links.second),)
+    gqkv_0 = attention_back(0, join(glow, part_2), images // 2, images - images // 2, 60, (gqkv_0,))
+    if by_hand:
+        state_1, gqkv_0 = lax.optimization_barrier((state_1, gqkv_0))
+        state_1 += (links.move(links.fold(state_1), links.second),)
+
+    step_weight = lambda side: pl.BlockSpec((1, width, BLOCK), lambda step: (side, 0, step))
     gh1, sums_0, keep_a, send_a = call(
         qkv_grad_kernel,
-        (place, *gathered_a, h1_turned, gqkv_0),
+        (place, h1_turned, gqkv_0, wq),
         (wide_rows, struct((3, 8, BLOCK), F32)) + (shares(24, third),) * 2,
         (fixed(rows, width), fixed(3, 8, BLOCK)) + (step_shares(24, BLOCK),) * 2,
-        [smem] + [anywhere] * 4 + [fixed(width, rows), step_rows(BLOCK)],
+        [smem, fixed(width, rows), step_rows(BLOCK), step_weight(0)],
         6 * rows * width * width,
         10,
         24,
         grid=(3,),
-        scratch=(buffer((width, BLOCK), F32), buffer((3, width, BLOCK), BF), flag((3,))),
+        scratch=(buffer((width, BLOCK), F32),),
         name="qkv_grad",
     )
-    state_a = reduce(0, (keep_a, send_a))
-
-    gqkv_1 = attention_back(1, join(glow, gh1)[0])
-    gqkv_1, state_a, state_2 = join(gqkv_1, state_a, state_2)
-    state_a, state_2 = reduce(1, state_a), reduce(2, state_2)
+    part_2 = gh1
+    if by_hand:
+        state_a = keep_a, links.move(send_a, links.cores)
+        state_2, gh1 = lax.optimization_barrier((state_2, gh1))
+        part_2 = links.fold(state_2)
+        state_2 += (links.move(part_2, links.near),)
+
+    gqkv_1 = attention_back(1, join(glow, gh1, part_2), 0, images, 20)
+    if by_hand:
+        state_a, gqkv_1 = lax.optimization_barrier((state_a, gqkv_1))
+        state_a += (links.move(links.fold(state_a), links.second),)
 
     ginput, keep_c, send_c = call(
         input_kernel,
-        (place, *gathered_a, h1_turned, gqkv_1, sums_0, rows_in, vec, gresid, gh1),
+        (place, h1_turned, gqkv_1, wq, sums_0, rows_in, vec, gresid, gh1),
         (low_rows,) + (shares(32, third),) * 2,
         (fixed(rows, width),) + (step_shares(32, BLOCK),) * 2,
-        [smem] + [anywhere] * 4 + [
-            fixed(width, rows), step_rows(BLOCK), fixed(3, 8, BLOCK), fixed(rows, width), fixed(2, 16, BLOCK),
+        [
+            smem, fixed(width, rows), step_rows(BLOCK), step_weight(1), fixed(3, 8, BLOCK), fixed(rows, width), fixed(2, 16, BLOCK),
             anywhere, anywhere,
         ],
         6 * rows * width * width,
@@ -837,58 +872,74 @@
         30,
         grid=(3,),
         scratch=(
-            buffer((width, BLOCK), F32), buffer((3, width, BLOCK), BF), buffer((3, 8, BLOCK), F32),
-            buffer((rows, width), F32), buffer((rows, width), F32), flag((3,)), flag((2,)),
+            buffer((width, BLOCK), F32), buffer((3, 8, BLOCK), F32), buffer((rows, width), F32),
+            buffer((rows, width), F32), flag((2,)),
         ),
         name="input_grad",
     )
-    ginput, state_c, state_2, state_1, state_a = join(ginput, (keep_c, send_c), state_2, state_1, state_a)
-    state_c, state_a, state_1 = reduce(0, state_c), reduce(2, state_a), reduce(2, state_1)
-
     def cut(value):
         return value.reshape(images, padded, width)[:, :length]
 
     if by_hand:
-        state_c = reduce(1, state_c)
-        state_2 = reduce(3, join(state_2, state_c[:2])[0])
-        out, ginput = after(out, state_c[1]), after(ginput, state_c[1])
-        state_1, state_a, state_c = join(state_1, state_a, state_c)
-        state_c = reduce(2, state_c)
-        state_1, state_a = reduce(3, state_1), reduce(3, state_a)
-        state_c = reduce(3, join(state_c)[0])
-        state_1, state_2, state_a, _ = join(state_1, state_2, state_a, state_c[3])
-        mine_c = reduce(4, state_c)
-        mine_1, mine_2, mine_a = reduce(4, state_1), reduce(4, state_2), reduce(4, state_a)
-        device = place[49]
-
-        def share(line, count):
-            start = (device % (line.shape[0] // count)) * count
-            return lax.dynamic_slice(line, (start,), (count,))
-
-        heads = []
-        for part in range(3):
-            lanes = slice(BLOCK * part, BLOCK * (part + 1))
-            heads += [mine_a[:, lanes], mine_c[:24, lanes]]
-        small_c, small_2 = mine_c[24:, 2 * BLOCK :], mine_2[120:]
+        fold, move = links.fold, links.move
+
+        def last_sum(kernel, state, heights, counts_out):
+            first = lambda part: pl.BlockSpec((1,) + part.shape[1:], lambda step: (0, 0, 0))
+            columns = 3 * width if kernel is last_heads_kernel else width
+            return pl.pallas_call(
+                kernel,
+                grid=(1,),
+                out_shape=tuple(struct((height, columns), F32) for height in heights)
+                + tuple(struct((count,), F32) for count in counts_out),
+                in_specs=[smem] + [first(part) for part in state],
+                out_specs=tuple(fixed(height, columns) for height in heights)
+                + tuple(pl.BlockSpec((count,), lambda step: (0,)) for count in counts_out),
+                compiler_params=pltpu.CompilerParams(vmem_limit_bytes=30 * MIB),
+                name="last_sum",
+            )(place, *state)
+
+        state_c = keep_c, move(send_c, links.cores)
+        state_1 = after(state_1, keep_c)
+        part = fold(state_1)
+        state_1 += (move(part, links.near),)
+        part = fold(after(state_c, part))
+        state_c += (move(part, links.second),)
+        state_2, state_a = after((state_2, state_a), part)
+        parts = fold(state_2), fold(state_a)
+        state_2 += (move(parts[0], links.first),)
+        state_a += (move(parts[1], links.first),)
+        out, ginput = after((out, ginput), parts)
+        out, ginput = cut(out), cut(ginput)
+        part = fold(after(state_c, parts))
+        state_c += (move(part, links.first),)
+        state_1, state_2, state_a, out, ginput = after((state_1, state_2, state_a, out, ginput), part)
+        parts = fold(state_2), fold(state_1), fold(state_a)
+        state_2 += (move(parts[0], links.far),)
+        state_1 += (move(parts[1], links.first),)
+        state_a += (move(parts[2], links.near),)
+        part = fold(after(state_c, parts))
+        state_c += (move(part, links.near),)
+        state_1, state_a = after((state_1, state_a), part)
+        parts = fold(state_1), fold(state_a)
+        state_1 += (move(parts[0], links.far),)
+        state_a += (move(parts[1], links.far),)
+        part = fold(after(state_c, parts))
+        state_c += (move(part, links.far),)
+        state_2 = after(state_2, part)
+        mine_2 = last_sum(last_second_kernel, state_2, (96, 24), (24, 24, 24, 24, 96))
+        state_1 = after(state_1, mine_2)
+        mine_1 = add_up([part[0] for part in state_1])
+        mine_c = last_sum(last_heads_kernel, state_a + state_c, (24,), (24, 24, 48))
+        fc2_grad, out_grad, ln2_gain_grad, ln2_bias_grad, fc2_bias_grad, out_bias_grad, fc1_bias_grad = mine_2
+        qkv_grad, ln1_gain_grad, ln1_bias_grad, qv_bias_grad = mine_c
         return (
-            cut(out),
-            cut(ginput),
-            share(small_c[0], 24),
-            share(small_c[1], 24),
-            jnp.concatenate(heads, axis=1),
-            share(small_c[2], 48),
-            mine_2[96:120],
-            share(small_2[4], 24),
-            share(small_2[0], 24),
-            share(small_2[1], 24),
-            mine_1,
-            share(small_2[3], 96),
-            mine_2[:96],
-            share(small_2[2], 24),
+            out, ginput, ln1_gain_grad, ln1_bias_grad, qkv_grad, qv_bias_grad, out_grad, out_bias_grad,
+            ln2_gain_grad, ln2_bias_grad, mine_1, fc1_bias_grad, fc2_grad, fc2_bias_grad,
         )
 
     both_a, both_c, both_1, both_2 = (
-        jnp.stack(state, axis=1).astype(F32) for state in (state_a, state_c, state_1, state_2)
+        jnp.stack(pair, axis=1).astype(F32)
+        for pair in ((keep_a, send_a), (keep_c, send_c), (keep_1, send_1), (keep_2, send_2))
     )
     heads = jnp.stack(
         [both.reshape(CHIPS, 2, 24, 3, BLOCK) for both in (both_a, both_c[:, :, :24])], axis=4

time: 268 us -> 241 us (0.90)
  local copies, waits for them, and re-layouts: 25.8 us -> 16 us
  waiting for transfers between devices: 81.5 us -> 72 us
  starting transfers between devices: 50 us -> 41.2 us
  other arithmetic: 13.9 us -> 20.1 us
  Pallas kernels: 92.4 us -> 89.7 us
    pallas_call x7 -> x5, Pallas kernels: 88.7 us -> 64.8 us  [call(): pl.pallas_call(kernel, grid=grid, out_shape=out_shape, in_specs=in_specs,...]
    pallas_call x0 -> x5, Pallas kernels: none -> 21.2 us  [the longest x3 17.8 us: attention_back(): pl.pallas_call(lambda *refs: attention_back_kernel(side, *refs), grid=(co...]
    convert_element_type x8 -> x16, other arithmetic: 1.73 us -> 13.5 us  [fold(): return add_up([part[left // 2:left] for part in state]).astype(BF)]
    ppermute x46 -> x42, waiting for transfers between devices: 81.5 us -> 72 us  [move(): return lax.ppermute(value, AXES, pairs)]
    ppermute x46 -> x42, starting transfers between devices: 50 us -> 41.2 us  [move(): return lax.ppermute(value, AXES, pairs)]
    add x8 -> x1, other arithmetic: 6.76 us -> 1.74 us  [add_up(): return sum((part.astype(F32) for part in parts))]
    unnamed x123 -> x84, local copies, waits for them, and re-layouts: 15.2 us -> 10.4 us
    dynamic_slice x8 -> x0, local copies, waits for them, and re-layouts: 4.67 us -> none  [share(): return lax.dynamic_slice(line, (start,), (count,))]
  transfers between devices with their start and end apart: 46 -> 42, of which waited for: 19 -> 17; matrix products, arithmetic and copies ran while one was open for 8% -> 10% of each run, Pallas kernels for 19% -> 19%
where the time goes in v2:
time: 241 us; the launch traced here: 240 us
  Pallas kernels  89.7 us (37%)
  waiting for transfers between devices  72 us (30%)
  starting transfers between devices  41.2 us (17%)
  other arithmetic  20.1 us (8%)
  local copies, waits for them, and re-layouts  16 us (7%)
    ppermute x42, waiting for transfers between devices, move(): return lax.ppermute(value, AXES, pairs)  72 us
    pallas_call x5, Pallas kernels, call(): pl.pallas_call(kernel, grid=grid, out_shape=out_shape, in_specs=in_specs,...  64.8 us
    ppermute x42, starting transfers between devices, move(): return lax.ppermute(value, AXES, pairs)  41.2 us
    pallas_call x3, Pallas kernels, attention_back(): pl.pallas_call(lambda *refs: attention_back_kernel(side, *refs), grid=(co...  17.8 us
    convert_element_type x16, other arithmetic, fold(): return add_up([part[left // 2:left] for part in state]).astype(BF)  13.5 us
    unnamed x84, local copies, waits for them, and re-layouts  10.4 us
  transfers between devices with their start and end apart: 42, of which 17 were waited for; matrix products, arithmetic and copies ran while one was open for 10% of the time, Pallas kernels for 19%

profile of v2, /device:TPU:0, one launch (start us, length us, event | category | flops | bytes accessed | tf_op | source)
XLA Modules:
  0.0 240.4 jit_solution(1401131460587465049)
XLA Ops:
  1.4 1.8 share.1
  5.8 1.9 pair.1
  7.7 4.8 %collective-permute-start.2 = (bf16[160,384]{1,0:T(8,128)(2,1)}, bf16[160,384]{1,0:T(8,128)(2,1)S(1)}, u32[]{:S(2)}, u32[]{:S(2)}) collective-permute-start(bf16[160,384]{1,0:T(8,128)(2,1)} %get-tuple-element.162), channel_id=1, source_target_pairs={{0,24},{1,25},{2,26},{3,27},{4,28},{5,29},{6,30},{7,31},{8,0},{9,1... | collective-permute-start | bytes 368648 | tf_op jit(solution)/shard_map/ppermute | solution.py:510
  12.4 1.5 collective-permute-start.3
  13.9 1.5 fusion
  16.5 3.3 %collective-permute-done.1 = bf16[160,384]{1,0:T(8,128)(2,1)S(1)} collective-permute-done((bf16[160,384]{1,0:T(8,128)(2,1)}, bf16[160,384]{1,0:T(8,128)(2,1)S(1)}, u32[]{:S(2)}, u32[]{:S(2)}) %collective-permute-start.1) | collective-permute-done | bytes 122912 | tf_op jit(solution)/shard_map/ppermute | solution.py:510
  19.8 0.9 pad_maximum_fusion.3
  20.7 1.6 collective-permute-start.5
  23.0 1.0 copy.33
  24.3 1.2 collective-permute-start.4
  25.5 5.5 %collective-permute-done.4 = bf16[160,384]{1,0:T(8,128)(2,1)S(1)} collective-permute-done((bf16[160,384]{1,0:T(8,128)(2,1)S(1)}, bf16[160,384]{1,0:T(8,128)(2,1)S(1)}, u32[]{:S(2)}, u32[]{:S(2)}) %collective-permute-start.4) | collective-permute-done | bytes 122912 | tf_op jit(solution)/shard_map/ppermute | solution.py:510
  31.1 1.6 collective-permute-start.6
  32.8 2.0 collective-permute-start.7
  34.8 6.9 %collective-permute-done.8 = bf16[240,384]{1,0:T(8,128)(2,1)S(1)} collective-permute-done((bf16[240,384]{1,0:T(8,128)(2,1)S(1)}, bf16[240,384]{1,0:T(8,128)(2,1)S(1)}, u32[]{:S(2)}, u32[]{:S(2)}) %collective-permute-start.8) | collective-permute-done | bytes 184352 | tf_op jit(solution)/shard_map/ppermute | solution.py:510
  42.4 1.3 collective-permute-start.10
  43.7 15.0 %collective-permute-done.11 = bf16[4,192,384]{2,1,0:T(8,128)(2,1)S(1)} collective-permute-done((bf16[4,192,384]{2,1,0:T(8,128)(2,1)S(1)}, bf16[4,192,384]{2,1,0:T(8,128)(2,1)S(1)}, u32[]{:S(2)}, u32[]{:S(2)}) %collective-permute-start.11) | collective-permute-done | bytes 589856 | tf_op jit(solution)/shard_map/ppermute | solution.py:510
  58.7 2.0 collective-permute-done.10
  60.8 1.8 collective-permute-start.15
  63.2 7.1 %qkv.1 = (f32[2,16,384]{2,1,0:T(8,128)S(1)}, f32[4,1,768]{2,1,0:T(1,128)S(1)}, bf16[768,640]{1,0:T(8,128)(2,1)S(1)}, bf16[2,640,1152]{2,1,0:T(8,128)(2,1)S(1)}, bf16[2,768,1152]{2,1,0:T(8,128)(2,1)S(1)}) custom-call(s32[144]{0:T(256)S(1)} %copy-done.19, bf16[8,160,384]{2,1,0:T(8,128)(2,1)S(1)} %constant_dynamic-update-slice_fusion.own0, ...), custom_call_target="tpu_custom_call" | custom-call | flops 2264924160 | bytes 14680064 | tf_op jit(solution)/shard_map/qkv/pallas_call | solution.py:705
  70.3 1.8 copy-done.9
  72.2 1.0 copy-done.15
  74.4 2.3 collective-permute-done.14
  76.9 1.7 collective-permute-start.18
  79.2 6.3 %attention.1.att_ref = bf16[640,768]{1,0:T(8,128)(2,1)S(1)} custom-call(bf16[2,640,1152]{2,1,0:T(8,128)(2,1)S(1)} %get-tuple-element.179.qkv_ref.refs_1_, f32[4,160,160]{2,1,0:T(8,128)S(1)} %copy-done.12), custom_call_target="tpu_custom_call" | custom-call | flops 1006632960 | bytes 10485760 | tf_op jit(solution)/shard_map/attention/pallas_call | solution.py:705
  86.4 10.0 %collective-permute-done.16 = bf16[4,192,384]{2,1,0:T(8,128)(2,1)S(1)} collective-permute-done((bf16[4,192,384]{2,1,0:T(8,128)(2,1)S(1)}, bf16[4,192,384]{2,1,0:T(8,128)(2,1)S(1)}, u32[]{:S(2)}, u32[]{:S(2)}) %collective-permute-start.16) | collective-permute-done | bytes 589856 | tf_op jit(solution)/shard_map/ppermute | solution.py:510
  97.4 6.2 %collective-permute-done.19.a3 = bf16[8,192,384]{2,1,0:T(8,128)(2,1)S(1)} collective-permute-done((bf16[8,192,384]{2,1,0:T(8,128)(2,1)S(1)}, bf16[8,192,384]{2,1,0:T(8,128)(2,1)S(1)}, u32[]{:S(2)}, u32[]{:S(2)}) %collective-permute-start.19) | collective-permute-done | bytes 1179680 | tf_op jit(solution)/shard_map/ppermute | solution.py:510
  103.6 1.1 copy-done.35
  105.6 38.0 %mlp.1 = (bf16[640,768]{1,0:T(8,128)(2,1)}, f32[640,768]{1,0:T(8,128)}, bf16[640,768]{1,0:T(8,128)(2,1)}, bf16[16,24,3072]{2,1,0:T(8,128)(2,1)}, bf16[16,24,3072...) custom-call(s32[144]{0:T(256)} %concatenate.20.place, ...), custom_call_target="tpu_custom_call" | custom-call | flops 18119393280 | bytes 33554432 | tf_op jit(solution)/shard_map/mlp/pallas_call | solution.py:705
  144.1 5.7 %attention_back.3.refs_4_ = bf16[640,1152]{1,0:T(8,128)(2,1)} custom-call(bf16[2,768,384]{2,1,0:T(8,128)(2,1)} %get-tuple-element.200.refs_0_, bf16[2,640,1152]{2,1,0:T(8,128)(2,1)} %copy-done, f32[4,160,160]{2,1,0:T(8,128)} %get-tuple-element.201.refs_2_, bf16[640,768]{1,0:T(8,128)(2,1)} %get-tuple-element.220.refs_3_), custom_call_target="tpu_custom_call" | custom-call | flops 1 | bytes 1 | tf_op jit(solution)/shard_map/attention_back/pallas_call | solution.py:806
  149.8 2.9 %add_convert_fusion = bf16[8,128,768]{2,1,0:T(8,128)(2,1)} fusion(bf16[16,128,768]{2,1,0:T(8,128)(2,1)} %collective-permute-done.23.refs_1_, bf16[16,128,768]{2,1,0:T(8,128)(2,1)S(1)} %copy-done.2), kind=kLoop, calls=%fused_computation | loop fusion | flops 3145728 | bytes 4718592 | tf_op jit(solution)/shard_map/convert_element_type | solution.py:582
  152.8 1.5 collective-permute-start.26
  154.2 5.6 %attention_back.4.gqkv_ref = bf16[640,1152]{1,0:T(8,128)(2,1)} custom-call(bf16[2,768,384]{2,1,0:T(8,128)(2,1)} %get-tuple-element.200.refs_0_, bf16[2,640,1152]{2,1,0:T(8,128)(2,1)} %copy-done, f32[4,160,160]{2,1,0:T(8,128)} %get-tuple-element.201.refs_2_, bf16[640,768]{1,0:T(8,128)(2,1)} %get-tuple-element.220.refs_3_, ...), custom_call_target="tpu_custom_call", output_to_operand_aliasing={{}: (4, {})} | custom-call | flops 1 | bytes 1 | tf_op jit(solution)/shard_map/attention_back/pallas_call | solution.py:806
  159.9 2.2 add_convert_fusion.1
  162.7 2.0 copy-done.10
  164.7 5.0 %qkv_grad.1 = (f32[640,768]{1,0:T(8,128)S(1)}, f32[3,8,384]{2,1,0:T(8,128)S(1)}, bf16[16,24,1152]{2,1,0:T(8,128)(2,1)S(1)}, bf16[16,24,1152]{2,1,0:T(8,128)(2,1)S(1)}) custom-call(s32[144]{0:T(256)S(1)} %copy-done.20, bf16[768,640]{1,0:T(8,128)(2,1)S(1)} %copy-done.16, bf16[640,1152]{1,0:T(8,128)(2,1)S(1)} %copy-done.6, bf16[2,768,1152]{2,1,0:T(8,128)(2,1)S(1)} %copy-done.10), custom_call_target="tpu_custom_call" | custom-call | flops 2264924160 | bytes 10485760 | tf_op jit(solution)/shard_map/qkv_grad/pallas_call | solution.py:705
  169.8 3.7 %collective-permute-done.26.refs_2_ = bf16[8,128,768]{2,1,0:T(8,128)(2,1)} collective-permute-done((bf16[8,128,768]{2,1,0:T(8,128)(2,1)}, bf16[8,128,768]{2,1,0:T(8,128)(2,1)}, u32[]{:S(2)}, u32[]{:S(2)}) %collective-permute-start.26) | collective-permute-done | bytes 1572896 | tf_op jit(solution)/shard_map/ppermute | solution.py:510
  173.5 1.8 add_convert_fusion.2
  175.8 6.5 %attention_back.5.gqkv_ref = bf16[640,1152]{1,0:T(8,128)(2,1)S(1)} custom-call(bf16[2,768,384]{2,1,0:T(8,128)(2,1)S(1)} %copy-done.3, bf16[2,640,1152]{2,1,0:T(8,128)(2,1)S(1)} %copy-done.1, f32[4,160,160]{2,1,0:T(8,128)S(1)} %copy-done.4, bf16[640,768]{1,0:T(8,128)(2,1)S(1)} %copy-done.5), custom_call_target="tpu_custom_call" | custom-call | flops 1 | bytes 1 | tf_op jit(solution)/shard_map/attention_back/pallas_call | solution.py:806
  182.4 8.4 %input_grad.1 = (bf16[640,768]{1,0:T(8,128)(2,1)S(1)}, bf16[16,32,1152]{2,1,0:T(8,128)(2,1)S(1)}, bf16[16,32,1152]{2,1,0:T(8,128)(2,1)S(1)}) custom-call(s32[144]{0:T(256)S(1)} %copy-done.20, bf16[768,640]{1,0:T(8,128)(2,1)S(1)} %copy-done.16, bf16[640,1152]{1,0:T(8,128)(2,1)S(1)} %attention_back.5.gqkv_ref, bf16[2,768,1152]{2,1,0:T(8,128)(2,1)S(1)} %copy-done.11, ...), custom_call_target="tpu_custom_call" | custom-call | flops 2264924160 | bytes 14680064 | tf_op jit(solution)/shard_map/input_grad/pallas_call | solution.py:705
  191.0 1.5 collective-permute-start.29
  192.6 1.3 add_convert_fusion.4
  193.9 1.7 collective-permute-start.27
  196.4 3.0 %collective-permute-done.29.refs_2_ = bf16[8,24,1152]{2,1,0:T(8,128)(2,1)S(1)} collective-permute-done((bf16[8,24,1152]{2,1,0:T(8,128)(2,1)S(1)}, bf16[8,24,1152]{2,1,0:T(8,128)(2,1)S(1)}, u32[]{:S(2)}, u32[]{:S(2)}) %collective-permute-start.29) | collective-permute-done | bytes 442400 | tf_op jit(solution)/shard_map/ppermute | solution.py:510
  199.5 1.6 collective-permute-start.32
  201.1 1.3 add_convert_fusion.6
  203.0 1.7 copy.36
  204.6 1.7 copy.37
  206.3 3.3 %collective-permute-done.33.refs_8_ = bf16[8,32,1152]{2,1,0:T(8,128)(2,1)S(1)} collective-permute-done((bf16[8,32,1152]{2,1,0:T(8,128)(2,1)S(1)}, bf16[8,32,1152]{2,1,0:T(8,128)(2,1)S(1)}, u32[]{:S(2)}, u32[]{:S(2)}) %collective-permute-start.33) | collective-permute-done | bytes 589856 | tf_op jit(solution)/shard_map/ppermute | solution.py:510
  209.7 1.6 collective-permute-start.36
  211.9 1.7 collective-permute-start.35
  213.6 1.2 add_convert_fusion.10
  214.8 1.0 collective-permute-start.40
  215.8 1.1 add_convert_fusion.7
  216.9 1.8 collective-permute-start.34
  218.7 1.7 collective-permute-start.38
  220.5 3.2 %collective-permute-done.34 = bf16[2,24,3072]{2,1,0:T(8,128)(2,1)S(1)} collective-permute-done((bf16[2,24,3072]{2,1,0:T(8,128)(2,1)S(1)}, bf16[2,24,3072]{2,1,0:T(8,128)(2,1)S(1)}, u32[]{:S(2)}, u32[]{:S(2)}) %collective-permute-start.34) | collective-permute-done | bytes 294944 | tf_op jit(solution)/shard_map/ppermute | solution.py:510
  223.7 2.1 collective-permute-start.37
  225.8 1.0 add_convert_fusion.11
  226.8 1.0 collective-permute-start.41
  228.2 1.7 collective-permute-start.39
  229.9 2.0 last_sum.3
  231.9 5.4 %collective-permute-done.41 = bf16[1,24,3072]{2,1,0:T(8,128)(2,1)S(1)} collective-permute-done((bf16[1,24,3072]{2,1,0:T(8,128)(2,1)S(1)}, bf16[1,24,3072]{2,1,0:T(8,128)(2,1)S(1)}, u32[]{:S(2)}, u32[]{:S(2)}) %collective-permute-start.41) | collective-permute-done | bytes 147488 | tf_op jit(solution)/shard_map/ppermute | solution.py:510
  237.3 1.7 add_bitcast_fusion
  239.1 1.4 last_sum.2
  (155 shorter events, 16.1 us)
Async XLA Ops:
  0.6 21.7 %copy-start.24 = (bf16[4,153,768]{2,0,1:T(4,128)(2,1)S(1)}, bf16[4,153,768]{2,0,1:T(4,128)(2,1)}, u32[]{:S(2)}) copy-start(bf16[4,153,768]{2,0,1:T(4,128)(2,1)} %param.31) | copy-start | bytes 2820100
  3.3 1.9 collective-permute-start
  7.7 8.8 %collective-permute-start.2 = (bf16[160,384]{1,0:T(8,128)(2,1)}, bf16[160,384]{1,0:T(8,128)(2,1)S(1)}, u32[]{:S(2)}, u32[]{:S(2)}) collective-permute-start(bf16[160,384]{1,0:T(8,128)(2,1)} %get-tuple-element.162), channel_id=1, source_target_pairs={{0,24},{1,25},{2,26},{3,27},{4,28},{5,29},{6,30},{7,31},{8,0},{9,1... | collective-permute-start | bytes 368648 | tf_op jit(solution)/shard_map/ppermute | solution.py:510
  12.4 7.3 %collective-permute-start.1 = (bf16[160,384]{1,0:T(8,128)(2,1)}, bf16[160,384]{1,0:T(8,128)(2,1)S(1)}, u32[]{:S(2)}, u32[]{:S(2)}) collective-permute-start(bf16[160,384]{1,0:T(8,128)(2,1)} %get-tuple-element.162), channel_id=1, source_target_pairs={{0,8},{1,9},{2,10},{3,11},{4,12},{5,13},{6,14},{7,15},{8,16},{9,17... | collective-permute-start | bytes 368648 | tf_op jit(solution)/shard_map/ppermute | solution.py:510
  12.4 7.3 %collective-permute-start.3 = (bf16[192,384]{1,0:T(8,128)(2,1)}, bf16[192,384]{1,0:T(8,128)(2,1)S(1)}, u32[]{:S(2)}, u32[]{:S(2)}) collective-permute-start(bf16[192,384]{1,0:T(8,128)(2,1)} %get-tuple-element.163), channel_id=1, source_target_pairs={{0,4},{1,3},{2,6},{3,1},{4,0},{5,7},{6,2},{7,5},{8,12},{9,11},{10,... | collective-permute-start | bytes 442376 | tf_op jit(solution)/shard_map/ppermute | solution.py:510
  20.7 3.4 %copy-start.25 = (bf16[4,153,768]{2,0,1:T(4,128)(2,1)S(1)}, bf16[4,153,768]{2,0,1:T(4,128)(2,1)}, u32[]{:S(2)}) copy-start(bf16[4,153,768]{2,0,1:T(4,128)(2,1)} %param.16) | copy-start | bytes 2820100
  20.7 10.3 %collective-permute-start.5 = (bf16[2,192,384]{2,1,0:T(8,128)(2,1)S(1)}, bf16[2,192,384]{2,1,0:T(8,128)(2,1)S(1)}, u32[]{:S(2)}, u32[]{:S(2)}) collective-permute-start(bf16[2,192,384]{2,1,0:T(8,128)(2,1)S(1)} %pad_maximum_fusion.3), channel_id=1, source_target_pairs={{0,2},{1,5},{2,0},{3,7},{4,6},{5,1},{6,4},{7,3},{8,10},{9,13},{10,... | collective-permute-start | bytes 884744 | tf_op jit(solution)/shard_map/ppermute | solution.py:510
  24.2 8.5 %copy-start.31 = (bf16[240,384]{1,0:T(8,128)(2,1)S(1)}, bf16[240,384]{1,0:T(8,128)(2,1)}, u32[]{:S(2)}) copy-start(bf16[240,384]{1,0:T(8,128)(2,1)} %get-tuple-element.169) | copy-start | bytes 552964
  24.3 38.9 %copy-start.7 = (bf16[4,160,768]{2,1,0:T(8,128)(2,1)}, bf16[4,160,768]{2,1,0:T(8,128)(2,1)S(1)}, u32[]{:S(2)}) copy-start(bf16[4,160,768]{2,1,0:T(8,128)(2,1)S(1)} %pad.11.clone) | copy-start | bytes 2949124
  24.3 18.0 %copy-start.26 = (bf16[192,384]{1,0:T(8,128)(2,1)S(1)}, bf16[192,384]{1,0:T(8,128)(2,1)}, u32[]{:S(2)}) copy-start(bf16[192,384]{1,0:T(8,128)(2,1)} %get-tuple-element.163) | copy-start | bytes 442372
  24.3 6.7 %collective-permute-start.4 = (bf16[160,384]{1,0:T(8,128)(2,1)S(1)}, bf16[160,384]{1,0:T(8,128)(2,1)S(1)}, u32[]{:S(2)}, u32[]{:S(2)}) collective-permute-start(bf16[160,384]{1,0:T(8,128)(2,1)S(1)} %collective-permute-done.1), channel_id=1, source_target_pairs={{0,8},{1,9},{2,10},{3,11},{4,12},{5,13},{6,14},{7,15},{8,16},{9,17... | collective-permute-start | bytes 368648 | tf_op jit(solution)/shard_map/ppermute | solution.py:510
  31.1 10.6 %collective-permute-start.6 = (bf16[4,160,384]{2,1,0:T(8,128)(2,1)S(1)}, bf16[4,160,384]{2,1,0:T(8,128)(2,1)S(1)}, u32[]{:S(2)}, u32[]{:S(2)}) collective-permute-start(bf16[4,160,384]{2,1,0:T(8,128)(2,1)S(1)} %pad_maximum_fusion.2), channel_id=1, source_target_pairs={{0,4},{1,3},{2,6},{3,1},{4,0},{5,7},{6,2},{7,5},{8,12},{9,11},{10,... | collective-permute-start | bytes 1474568 | tf_op jit(solution)/shard_map/ppermute | solution.py:510
  32.7 9.0 %collective-permute-start.8 = (bf16[240,384]{1,0:T(8,128)(2,1)S(1)}, bf16[240,384]{1,0:T(8,128)(2,1)S(1)}, u32[]{:S(2)}, u32[]{:S(2)}) collective-permute-start(bf16[240,384]{1,0:T(8,128)(2,1)S(1)} %copy-done.31), channel_id=1, source_target_pairs={{0,24},{1,25},{2,26},{3,27},{4,28},{5,29},{6,30},{7,31},{8,0},{9,1... | collective-permute-start | bytes 552968 | tf_op jit(solution)/shard_map/ppermute | solution.py:510
  32.8 8.9 %collective-permute-start.7 = (bf16[240,384]{1,0:T(8,128)(2,1)S(1)}, bf16[240,384]{1,0:T(8,128)(2,1)S(1)}, u32[]{:S(2)}, u32[]{:S(2)}) collective-permute-start(bf16[240,384]{1,0:T(8,128)(2,1)S(1)} %copy-done.31), channel_id=1, source_target_pairs={{0,8},{1,9},{2,10},{3,11},{4,12},{5,13},{6,14},{7,15},{8,16},{9,17... | collective-permute-start | bytes 552968 | tf_op jit(solution)/shard_map/ppermute | solution.py:510
  41.8 21.4 %copy-start.19 = (s32[144]{0:T(256)S(1)}, s32[144]{0:T(256)}, u32[]{:S(2)}) copy-start(s32[144]{0:T(256)} %concatenate.20.place) | copy-start | bytes 1732
  41.8 18.8 %collective-permute-start.9 = (bf16[8,160,384]{2,1,0:T(8,128)(2,1)S(1)}, bf16[8,160,384]{2,1,0:T(8,128)(2,1)S(1)}, u32[]{:S(2)}, u32[]{:S(2)}) collective-permute-start(bf16[8,160,384]{2,1,0:T(8,128)(2,1)S(1)} %constant_dynamic-update-slice_fusion.own0), channel_id=1, source_target_pairs={{0,2},{1,5},{2,0},{3,7},{4,6},{5,1},{6,4},{7,3},{8,10},{9,13},{10,... | collective-permute-start | bytes 2949128 | tf_op jit(solution)/shard_map/ppermute | solution.py:510
  42.4 16.3 %collective-permute-start.11 = (bf16[4,192,384]{2,1,0:T(8,128)(2,1)S(1)}, bf16[4,192,384]{2,1,0:T(8,128)(2,1)S(1)}, u32[]{:S(2)}, u32[]{:S(2)}) collective-permute-start(bf16[4,192,384]{2,1,0:T(8,128)(2,1)S(1)} %pad_maximum_fusion.1), channel_id=1, source_target_pairs={{0,8},{1,9},{2,10},{3,11},{4,12},{5,13},{6,14},{7,15},{8,16},{9,17... | collective-permute-start | bytes 1769480 | tf_op jit(solution)/shard_map/ppermute | solution.py:510
  42.4 18.2 %collective-permute-start.10 = (bf16[240,384]{1,0:T(8,128)(2,1)S(1)}, bf16[240,384]{1,0:T(8,128)(2,1)S(1)}, u32[]{:S(2)}, u32[]{:S(2)}) collective-permute-start(bf16[240,384]{1,0:T(8,128)(2,1)S(1)} %collective-permute-done.7), channel_id=1, source_target_pairs={{0,8},{1,9},{2,10},{3,11},{4,12},{5,13},{6,14},{7,15},{8,16},{9,17... | collective-permute-start | bytes 552968 | tf_op jit(solution)/shard_map/ppermute | solution.py:510
  43.7 19.1 %collective-permute-start.12 = (bf16[8,160,384]{2,1,0:T(8,128)(2,1)S(1)}, bf16[8,160,384]{2,1,0:T(8,128)(2,1)S(1)}, u32[]{:S(2)}, u32[]{:S(2)}) collective-permute-start(bf16[8,160,384]{2,1,0:T(8,128)(2,1)S(1)} %constant_dynamic-update-slice_fusion.own0), channel_id=1, source_target_pairs={{0,1},{1,0},{2,3},{3,2},{4,5},{5,4},{6,7},{7,6},{8,9},{9,8},{10,11... | collective-permute-start | bytes 2949128 | tf_op jit(solution)/shard_map/ppermute | solution.py:510
  60.6 2.6 %collective-permute-start.13 = (bf16[8,160,384]{2,1,0:T(8,128)(2,1)S(1)}, bf16[8,160,384]{2,1,0:T(8,128)(2,1)S(1)}, u32[]{:S(2)}, u32[]{:S(2)}) collective-permute-start(bf16[8,160,384]{2,1,0:T(8,128)(2,1)S(1)} %collective-permute-done.9.own1), channel_id=1, source_target_pairs={{0,1},{1,0},{2,3},{3,2},{4,5},{5,4},{6,7},{7,6},{8,9},{9,8},{10,11... | collective-permute-start | bytes 2949128 | tf_op jit(solution)/shard_map/ppermute | solution.py:510
  60.8 15.9 %collective-permute-start.15 = (bf16[4,240,384]{2,1,0:T(8,128)(2,1)S(1)}, bf16[4,240,384]{2,1,0:T(8,128)(2,1)S(1)}, u32[]{:S(2)}, u32[]{:S(2)}) collective-permute-start(bf16[4,240,384]{2,1,0:T(8,128)(2,1)S(1)} %pad_maximum_fusion), channel_id=1, source_target_pairs={{0,4},{1,3},{2,6},{3,1},{4,0},{5,7},{6,2},{7,5},{8,12},{9,11},{10,... | collective-permute-start | bytes 2211848 | tf_op jit(solution)/shard_map/ppermute | solution.py:510
  62.6 14.1 %collective-permute-start.14 = (bf16[4,192,384]{2,1,0:T(8,128)(2,1)S(1)}, bf16[4,192,384]{2,1,0:T(8,128)(2,1)S(1)}, u32[]{:S(2)}, u32[]{:S(2)}) collective-permute-start(bf16[4,192,384]{2,1,0:T(8,128)(2,1)S(1)} %pad_maximum_fusion.1), channel_id=1, source_target_pairs={{0,24},{1,25},{2,26},{3,27},{4,28},{5,29},{6,30},{7,31},{8,0},{9,1... | collective-permute-start | bytes 1769480 | tf_op jit(solution)/shard_map/ppermute | solution.py:510
  74.4 4.8 %copy-start = (bf16[2,640,1152]{2,1,0:T(8,128)(2,1)}, bf16[2,640,1152]{2,1,0:T(8,128)(2,1)S(1)}, u32[]{:S(2)}) copy-start(bf16[2,640,1152]{2,1,0:T(8,128)(2,1)S(1)} %get-tuple-element.179.qkv_ref.refs_1_) | copy-start | bytes 8847364
  76.9 19.6 %copy-start.28 = (bf16[8,240,384]{2,1,0:T(8,128)(2,1)}, bf16[8,240,384]{2,1,0:T(8,128)(2,1)S(1)}, u32[]{:S(2)}) copy-start(bf16[8,240,384]{2,1,0:T(8,128)(2,1)S(1)} %constant_dynamic-update-slice_fusion.7.b0) | copy-start | bytes 4423684
  76.9 19.5 %collective-permute-start.18 = (bf16[8,240,384]{2,1,0:T(8,128)(2,1)S(1)}, bf16[8,240,384]{2,1,0:T(8,128)(2,1)S(1)}, u32[]{:S(2)}, u32[]{:S(2)}) collective-permute-start(bf16[8,240,384]{2,1,0:T(8,128)(2,1)S(1)} %constant_dynamic-update-slice_fusion.7.b0), channel_id=1, source_target_pairs={{0,2},{1,5},{2,0},{3,7},{4,6},{5,1},{6,4},{7,3},{8,10},{9,13},{10,... | collective-permute-start | bytes 4423688 | tf_op jit(solution)/shard_map/ppermute | solution.py:510
  78.8 6.6 %copy-start.30 = (bf16[8,192,384]{2,1,0:T(8,128)(2,1)}, bf16[8,192,384]{2,1,0:T(8,128)(2,1)S(1)}, u32[]{:S(2)}) copy-start(bf16[8,192,384]{2,1,0:T(8,128)(2,1)S(1)} %constant_dynamic-update-slice_fusion.5.a0) | copy-start | bytes 3538948
  78.8 17.6 %collective-permute-start.17 = (bf16[8,192,384]{2,1,0:T(8,128)(2,1)S(1)}, bf16[8,192,384]{2,1,0:T(8,128)(2,1)S(1)}, u32[]{:S(2)}, u32[]{:S(2)}) collective-permute-start(bf16[8,192,384]{2,1,0:T(8,128)(2,1)S(1)} %constant_dynamic-update-slice_fusion.5.a0), channel_id=1, source_target_pairs={{0,1},{1,0},{2,3},{3,2},{4,5},{5,4},{6,7},{7,6},{8,9},{9,8},{10,11... | collective-permute-start | bytes 3538952 | tf_op jit(solution)/shard_map/ppermute | solution.py:510
  78.9 17.5 %collective-permute-start.16 = (bf16[4,192,384]{2,1,0:T(8,128)(2,1)S(1)}, bf16[4,192,384]{2,1,0:T(8,128)(2,1)S(1)}, u32[]{:S(2)}, u32[]{:S(2)}) collective-permute-start(bf16[4,192,384]{2,1,0:T(8,128)(2,1)S(1)} %collective-permute-done.11), channel_id=1, source_target_pairs={{0,8},{1,9},{2,10},{3,11},{4,12},{5,13},{6,14},{7,15},{8,16},{9,17... | collective-permute-start | bytes 1769480 | tf_op jit(solution)/shard_map/ppermute | solution.py:510
  96.4 8.3 %copy-start.36 = (bf16[8,192,384]{2,1,0:T(8,128)(2,1)}, bf16[8,192,384]{2,1,0:T(8,128)(2,1)S(1)}, u32[]{:S(2)}) copy-start(bf16[8,192,384]{2,1,0:T(8,128)(2,1)S(1)} %collective-permute-done.17.a2) | copy-start | bytes 3538948
  96.4 8.7 %copy-start.33 = (bf16[8,240,384]{2,1,0:T(8,128)(2,1)}, bf16[8,240,384]{2,1,0:T(8,128)(2,1)S(1)}, u32[]{:S(2)}) copy-start(bf16[8,240,384]{2,1,0:T(8,128)(2,1)S(1)} %collective-permute-done.18.b1) | copy-start | bytes 4423684
  96.5 7.1 %collective-permute-start.20 = (bf16[8,240,384]{2,1,0:T(8,128)(2,1)S(1)}, bf16[8,240,384]{2,1,0:T(8,128)(2,1)S(1)}, u32[]{:S(2)}, u32[]{:S(2)}) collective-permute-start(bf16[8,240,384]{2,1,0:T(8,128)(2,1)S(1)} %constant_dynamic-update-slice_fusion.7.b0), channel_id=1, source_target_pairs={{0,1},{1,0},{2,3},{3,2},{4,5},{5,4},{6,7},{7,6},{8,9},{9,8},{10,11... | collective-permute-start | bytes 4423688 | tf_op jit(solution)/shard_map/ppermute | solution.py:510
  96.5 7.1 %collective-permute-start.21 = (bf16[8,240,384]{2,1,0:T(8,128)(2,1)S(1)}, bf16[8,240,384]{2,1,0:T(8,128)(2,1)S(1)}, u32[]{:S(2)}, u32[]{:S(2)}) collective-permute-start(bf16[8,240,384]{2,1,0:T(8,128)(2,1)S(1)} %collective-permute-done.18.b1), channel_id=1, source_target_pairs={{0,1},{1,0},{2,3},{3,2},{4,5},{5,4},{6,7},{7,6},{8,9},{9,8},{10,11... | collective-permute-start | bytes 4423688 | tf_op jit(solution)/shard_map/ppermute | solution.py:510
  97.2 7.9 %copy-start.29 = (bf16[8,192,384]{2,1,0:T(8,128)(2,1)}, bf16[8,192,384]{2,1,0:T(8,128)(2,1)S(1)}, u32[]{:S(2)}) copy-start(bf16[8,192,384]{2,1,0:T(8,128)(2,1)S(1)} %constant_dynamic-update-slice_fusion.9.a1) | copy-start | bytes 3538948
  97.2 6.4 %collective-permute-start.19 = (bf16[8,192,384]{2,1,0:T(8,128)(2,1)S(1)}, bf16[8,192,384]{2,1,0:T(8,128)(2,1)S(1)}, u32[]{:S(2)}, u32[]{:S(2)}) collective-permute-start(bf16[8,192,384]{2,1,0:T(8,128)(2,1)S(1)} %constant_dynamic-update-slice_fusion.9.a1), channel_id=1, source_target_pairs={{0,1},{1,0},{2,3},{3,2},{4,5},{5,4},{6,7},{7,6},{8,9},{9,8},{10,11... | collective-permute-start | bytes 3538952 | tf_op jit(solution)/shard_map/ppermute | solution.py:510
  143.5 6.3 %collective-permute-start.23 = (bf16[16,128,768]{2,1,0:T(8,128)(2,1)}, bf16[16,128,768]{2,1,0:T(8,128)(2,1)}, u32[]{:S(2)}, u32[]{:S(2)}) collective-permute-start(bf16[16,128,768]{2,1,0:T(8,128)(2,1)} %get-tuple-element.203), channel_id=1, source_target_pairs={{0,1},{1,0},{2,3},{3,2},{4,5},{5,4},{6,7},{7,6},{8,9},{9,8},{10,11... | collective-permute-start | bytes 9437192 | tf_op jit(solution)/shard_map/ppermute | solution.py:510
  143.7 16.2 %collective-permute-start.22 = (bf16[16,24,3072]{2,1,0:T(8,128)(2,1)}, bf16[16,24,3072]{2,1,0:T(8,128)(2,1)}, u32[]{:S(2)}, u32[]{:S(2)}) collective-permute-start(bf16[16,24,3072]{2,1,0:T(8,128)(2,1)} %get-tuple-element.199), channel_id=1, source_target_pairs={{0,1},{1,0},{2,3},{3,2},{4,5},{5,4},{6,7},{7,6},{8,9},{9,8},{10,11... | collective-permute-start | bytes 7077896 | tf_op jit(solution)/shard_map/ppermute | solution.py:510
  144.1 5.8 %copy-start.2 = (bf16[16,128,768]{2,1,0:T(8,128)(2,1)S(1)}, bf16[16,128,768]{2,1,0:T(8,128)(2,1)}, u32[]{:S(2)}) copy-start(bf16[16,128,768]{2,1,0:T(8,128)(2,1)} %get-tuple-element.285.refs_0_) | copy-start | bytes 9437188
  152.8 20.7 %collective-permute-start.26 = (bf16[8,128,768]{2,1,0:T(8,128)(2,1)}, bf16[8,128,768]{2,1,0:T(8,128)(2,1)}, u32[]{:S(2)}, u32[]{:S(2)}) collective-permute-start(bf16[8,128,768]{2,1,0:T(8,128)(2,1)} %add_convert_fusion), channel_id=1, source_target_pairs={{0,2},{1,5},{2,0},{3,7},{4,6},{5,1},{6,4},{7,3},{8,10},{9,13},{10,... | collective-permute-start | bytes 4718600 | tf_op jit(solution)/shard_map/ppermute | solution.py:510
  162.1 28.7 %collective-permute-start.24 = (bf16[8,24,3072]{2,1,0:T(8,128)(2,1)S(1)}, bf16[8,24,3072]{2,1,0:T(8,128)(2,1)S(1)}, u32[]{:S(2)}, u32[]{:S(2)}) collective-permute-start(bf16[8,24,3072]{2,1,0:T(8,128)(2,1)S(1)} %add_convert_fusion.1), channel_id=1, source_target_pairs={{0,2},{1,5},{2,0},{3,7},{4,6},{5,1},{6,4},{7,3},{8,10},{9,13},{10,... | collective-permute-start | bytes 3538952 | tf_op jit(solution)/shard_map/ppermute | solution.py:510
  164.7 10.7 %copy-start.3 = (bf16[2,768,384]{2,1,0:T(8,128)(2,1)S(1)}, bf16[2,768,384]{2,1,0:T(8,128)(2,1)}, u32[]{:S(2)}) copy-start(bf16[2,768,384]{2,1,0:T(8,128)(2,1)} %get-tuple-element.200.refs_0_) | copy-start | bytes 3538948
  164.7 10.7 %copy-start.4 = (f32[4,160,160]{2,1,0:T(8,128)S(1)}, f32[4,160,160]{2,1,0:T(8,128)}, u32[]{:S(2)}) copy-start(f32[4,160,160]{2,1,0:T(8,128)} %get-tuple-element.201.refs_2_) | copy-start | bytes 1228804
  164.7 10.7 %copy-start.5 = (bf16[640,768]{1,0:T(8,128)(2,1)S(1)}, bf16[640,768]{1,0:T(8,128)(2,1)}, u32[]{:S(2)}) copy-start(bf16[640,768]{1,0:T(8,128)(2,1)} %get-tuple-element.220.refs_3_) | copy-start | bytes 2949124
  169.8 12.5 %collective-permute-start.25 = (bf16[16,24,1152]{2,1,0:T(8,128)(2,1)S(1)}, bf16[16,24,1152]{2,1,0:T(8,128)(2,1)S(1)}, u32[]{:S(2)}, u32[]{:S(2)}) collective-permute-start(bf16[16,24,1152]{2,1,0:T(8,128)(2,1)S(1)} %get-tuple-element.214), channel_id=1, source_target_pairs={{0,1},{1,0},{2,3},{3,2},{4,5},{5,4},{6,7},{7,6},{8,9},{9,8},{10,11... | collective-permute-start | bytes 2654216 | tf_op jit(solution)/shard_map/ppermute | solution.py:510
  175.3 7.0 %copy-start.8 = (bf16[4,160,768]{2,1,0:T(8,128)(2,1)S(1)}, bf16[4,160,768]{2,1,0:T(8,128)(2,1)}, u32[]{:S(2)}) copy-start(bf16[4,160,768]{2,1,0:T(8,128)(2,1)} %copy-done.7) | copy-start | bytes 2949124
  175.3 7.0 %copy-start.13 = (f32[640,768]{1,0:T(8,128)S(1)}, f32[640,768]{1,0:T(8,128)}, u32[]{:S(2)}) copy-start(f32[640,768]{1,0:T(8,128)} %get-tuple-element.223.gresid) | copy-start | bytes 5898244
  175.3 7.0 %copy-start.18 = (f32[2,16,384]{2,1,0:T(8,128)S(1)}, f32[2,16,384]{2,1,0:T(8,128)}, u32[]{:S(2)}) copy-start(f32[2,16,384]{2,1,0:T(8,128)} %copy-done.17) | copy-start | bytes 147460
  175.3 24.1 %collective-permute-start.28 = (bf16[4,128,768]{2,1,0:T(8,128)(2,1)S(1)}, bf16[4,128,768]{2,1,0:T(8,128)(2,1)S(1)}, u32[]{:S(2)}, u32[]{:S(2)}) collective-permute-start(bf16[4,128,768]{2,1,0:T(8,128)(2,1)S(1)} %add_convert_fusion.2), channel_id=1, source_target_pairs={{0,8},{1,9},{2,10},{3,11},{4,12},{5,13},{6,14},{7,15},{8,0},{9,1},... | collective-permute-start | bytes 2359304 | tf_op jit(solution)/shard_map/ppermute | solution.py:510
  175.8 6.5 %copy-start.11 = (bf16[2,768,1152]{2,1,0:T(8,128)(2,1)S(1)}, bf16[2,768,1152]{2,1,0:T(8,128)(2,1)}, u32[]{:S(2)}) copy-start(bf16[2,768,1152]{2,1,0:T(8,128)(2,1)} %copy-done.9) | copy-start | bytes 10616836
  182.3 10.2 %copy-start.22 = (bf16[16,24,3072]{2,1,0:T(8,128)(2,1)S(1)}, bf16[16,24,3072]{2,1,0:T(8,128)(2,1)}, u32[]{:S(2)}) copy-start(bf16[16,24,3072]{2,1,0:T(8,128)(2,1)} %get-tuple-element.298) | copy-start | bytes 7077892
  190.8 4.8 %collective-permute-start.30 = (bf16[16,32,1152]{2,1,0:T(8,128)(2,1)S(1)}, bf16[16,32,1152]{2,1,0:T(8,128)(2,1)S(1)}, u32[]{:S(2)}, u32[]{:S(2)}) collective-permute-start(bf16[16,32,1152]{2,1,0:T(8,128)(2,1)S(1)} %get-tuple-element.230), channel_id=1, source_target_pairs={{0,1},{1,0},{2,3},{3,2},{4,5},{5,4},{6,7},{7,6},{8,9},{9,8},{10,11... | collective-permute-start | bytes 3538952 | tf_op jit(solution)/shard_map/ppermute | solution.py:510
  191.0 8.4 %collective-permute-start.29 = (bf16[8,24,1152]{2,1,0:T(8,128)(2,1)S(1)}, bf16[8,24,1152]{2,1,0:T(8,128)(2,1)S(1)}, u32[]{:S(2)}, u32[]{:S(2)}) collective-permute-start(bf16[8,24,1152]{2,1,0:T(8,128)(2,1)S(1)} %add_convert_fusion.5), channel_id=1, source_target_pairs={{0,2},{1,5},{2,0},{3,7},{4,6},{5,1},{6,4},{7,3},{8,10},{9,13},{10,... | collective-permute-start | bytes 1327112 | tf_op jit(solution)/shard_map/ppermute | solution.py:510
  193.9 17.4 %collective-permute-start.27 = (bf16[4,24,3072]{2,1,0:T(8,128)(2,1)S(1)}, bf16[4,24,3072]{2,1,0:T(8,128)(2,1)S(1)}, u32[]{:S(2)}, u32[]{:S(2)}) collective-permute-start(bf16[4,24,3072]{2,1,0:T(8,128)(2,1)S(1)} %add_convert_fusion.4), channel_id=1, source_target_pairs={{0,8},{1,9},{2,10},{3,11},{4,12},{5,13},{6,14},{7,15},{8,0},{9,1},... | collective-permute-start | bytes 1769480 | tf_op jit(solution)/shard_map/ppermute | solution.py:510
  195.7 7.2 %copy-start.23 = (bf16[640,768]{1,0:T(8,128)(2,1)S(1)}, bf16[640,768]{1,0:T(8,128)(2,1)}, u32[]{:S(2)}) copy-start(bf16[640,768]{1,0:T(8,128)(2,1)} %get-tuple-element.242) | copy-start | bytes 2949124
  195.8 13.8 %collective-permute-start.33 = (bf16[8,32,1152]{2,1,0:T(8,128)(2,1)S(1)}, bf16[8,32,1152]{2,1,0:T(8,128)(2,1)S(1)}, u32[]{:S(2)}, u32[]{:S(2)}) collective-permute-start(bf16[8,32,1152]{2,1,0:T(8,128)(2,1)S(1)} %add_convert_fusion.3), channel_id=1, source_target_pairs={{0,2},{1,5},{2,0},{3,7},{4,6},{5,1},{6,4},{7,3},{8,10},{9,13},{10,... | collective-permute-start | bytes 1769480 | tf_op jit(solution)/shard_map/ppermute | solution.py:510
  199.5 11.8 %collective-permute-start.32 = (bf16[4,24,1152]{2,1,0:T(8,128)(2,1)S(1)}, bf16[4,24,1152]{2,1,0:T(8,128)(2,1)S(1)}, u32[]{:S(2)}, u32[]{:S(2)}) collective-permute-start(bf16[4,24,1152]{2,1,0:T(8,128)(2,1)S(1)} %add_convert_fusion.9), channel_id=1, source_target_pairs={{0,4},{1,3},{2,6},{3,1},{4,0},{5,7},{6,2},{7,5},{8,12},{9,11},{10,... | collective-permute-start | bytes 663560 | tf_op jit(solution)/shard_map/ppermute | solution.py:510
  202.4 9.4 %collective-permute-start.31 = (bf16[2,128,768]{2,1,0:T(8,128)(2,1)S(1)}, bf16[2,128,768]{2,1,0:T(8,128)(2,1)S(1)}, u32[]{:S(2)}, u32[]{:S(2)}) collective-permute-start(bf16[2,128,768]{2,1,0:T(8,128)(2,1)S(1)} %add_convert_fusion.6), channel_id=1, source_target_pairs={{0,4},{1,3},{2,6},{3,1},{4,0},{5,7},{6,2},{7,5},{8,12},{9,11},{10,... | collective-permute-start | bytes 1179656 | tf_op jit(solution)/shard_map/ppermute | solution.py:510
  209.7 9.0 %collective-permute-start.36 = (bf16[4,32,1152]{2,1,0:T(8,128)(2,1)S(1)}, bf16[4,32,1152]{2,1,0:T(8,128)(2,1)S(1)}, u32[]{:S(2)}, u32[]{:S(2)}) collective-permute-start(bf16[4,32,1152]{2,1,0:T(8,128)(2,1)S(1)} %add_convert_fusion.8), channel_id=1, source_target_pairs={{0,4},{1,3},{2,6},{3,1},{4,0},{5,7},{6,2},{7,5},{8,12},{9,11},{10,... | collective-permute-start | bytes 884744 | tf_op jit(solution)/shard_map/ppermute | solution.py:510
  211.9 8.6 %collective-permute-start.35 = (bf16[2,24,1152]{2,1,0:T(8,128)(2,1)S(1)}, bf16[2,24,1152]{2,1,0:T(8,128)(2,1)S(1)}, u32[]{:S(2)}, u32[]{:S(2)}) collective-permute-start(bf16[2,24,1152]{2,1,0:T(8,128)(2,1)S(1)} %add_convert_fusion.13), channel_id=1, source_target_pairs={{0,8},{1,9},{2,10},{3,11},{4,12},{5,13},{6,14},{7,15},{8,0},{9,1},... | collective-permute-start | bytes 331784 | tf_op jit(solution)/shard_map/ppermute | solution.py:510
  214.8 15.1 %collective-permute-start.40 = (bf16[1,128,768]{2,1,0:T(8,128)(2,1)S(1)}, bf16[1,128,768]{2,1,0:T(8,128)(2,1)S(1)}, u32[]{:S(2)}, u32[]{:S(2)}) collective-permute-start(bf16[1,128,768]{2,1,0:T(8,128)(2,1)S(1)} %add_convert_fusion.10), channel_id=1, source_target_pairs={{0,16},{1,17},{2,18},{3,19},{4,20},{5,21},{6,22},{7,23},{8,24},{9,... | collective-permute-start | bytes 589832 | tf_op jit(solution)/shard_map/ppermute | solution.py:510
  216.9 6.8 %collective-permute-start.34 = (bf16[2,24,3072]{2,1,0:T(8,128)(2,1)S(1)}, bf16[2,24,3072]{2,1,0:T(8,128)(2,1)S(1)}, u32[]{:S(2)}, u32[]{:S(2)}) collective-permute-start(bf16[2,24,3072]{2,1,0:T(8,128)(2,1)S(1)} %add_convert_fusion.7), channel_id=1, source_target_pairs={{0,4},{1,3},{2,6},{3,1},{4,0},{5,7},{6,2},{7,5},{8,12},{9,11},{10,... | collective-permute-start | bytes 884744 | tf_op jit(solution)/shard_map/ppermute | solution.py:510
  218.7 9.4 %collective-permute-start.38 = (bf16[2,32,1152]{2,1,0:T(8,128)(2,1)S(1)}, bf16[2,32,1152]{2,1,0:T(8,128)(2,1)S(1)}, u32[]{:S(2)}, u32[]{:S(2)}) collective-permute-start(bf16[2,32,1152]{2,1,0:T(8,128)(2,1)S(1)} %add_convert_fusion.12), channel_id=1, source_target_pairs={{0,8},{1,9},{2,10},{3,11},{4,12},{5,13},{6,14},{7,15},{8,0},{9,1},... | collective-permute-start | bytes 442376 | tf_op jit(solution)/shard_map/ppermute | solution.py:510
  223.7 15.4 %collective-permute-start.37 = (bf16[1,24,1152]{2,1,0:T(8,128)(2,1)S(1)}, bf16[1,24,1152]{2,1,0:T(8,128)(2,1)S(1)}, u32[]{:S(2)}, u32[]{:S(2)}) collective-permute-start(bf16[1,24,1152]{2,1,0:T(8,128)(2,1)S(1)} %add_convert_fusion.15), channel_id=1, source_target_pairs={{0,16},{1,17},{2,18},{3,19},{4,20},{5,21},{6,22},{7,23},{8,24},{9,... | collective-permute-start | bytes 165896 | tf_op jit(solution)/shard_map/ppermute | solution.py:510
  226.8 10.5 %collective-permute-start.41 = (bf16[1,24,3072]{2,1,0:T(8,128)(2,1)S(1)}, bf16[1,24,3072]{2,1,0:T(8,128)(2,1)S(1)}, u32[]{:S(2)}, u32[]{:S(2)}) collective-permute-start(bf16[1,24,3072]{2,1,0:T(8,128)(2,1)S(1)} %add_convert_fusion.11), channel_id=1, source_target_pairs={{0,16},{1,17},{2,18},{3,19},{4,20},{5,21},{6,22},{7,23},{8,24},{9,... | collective-permute-start | bytes 442376 | tf_op jit(solution)/shard_map/ppermute | solution.py:510
  228.2 10.9 %collective-permute-start.39 = (bf16[1,32,1152]{2,1,0:T(8,128)(2,1)S(1)}, bf16[1,32,1152]{2,1,0:T(8,128)(2,1)S(1)}, u32[]{:S(2)}, u32[]{:S(2)}) collective-permute-start(bf16[1,32,1152]{2,1,0:T(8,128)(2,1)S(1)} %add_convert_fusion.14), channel_id=1, source_target_pairs={{0,16},{1,17},{2,18},{3,19},{4,20},{5,21},{6,22},{7,23},{8,24},{9,... | collective-permute-start | bytes 221192 | tf_op jit(solution)/shard_map/ppermute | solution.py:510
  (16 other events, 26.8 us)

commit v3 on v2

--- a/solution.py
+++ b/solution.py
@@ -214,16 +214,33 @@
         ).astype(BF)
 
 
+def at_slot(target, slot, work):
+    if not isinstance(target, tuple):
+        work(target, slot)
+        return
+
+    @pl.when(slot >= 8)
+    def _():
+        work(target[0], slot - 8)
+
+    @pl.when(slot < 8)
+    def _():
+        work(target[1], slot)
+
+
 def give_rows(place, tables, total, keep_ref, send_ref, extra=None):
     for chip in range(CHIPS):
         below = None if extra is None else extra(chip)
         for which, target in enumerate((keep_ref, send_ref)):
-            slot = place[tables[which] + chip]
             owner = place[48] if which == 0 else 1 - place[48]
             share = total[pl.ds(pl.multiple_of(48 * chip + 24 * owner, 8), 24), :]
             if below is not None:
                 share = jnp.concatenate([share, below], axis=0)
-            target[slot] = share.astype(BF)
+
+            def put(ref, slot, share=share):
+                ref[slot] = share.astype(BF)
+
+            at_slot(target, place[tables[which] + chip], put)
 
 
 def stack_rows(rows):
@@ -237,42 +254,69 @@
 
 
 def mlp_kernel(
-    place, counts, a0, a1, a2, a3, b0, b1, b2, b3, att_ref, rows_ref, gout_ref, vec_ref, fcb_ref,
-    out_ref, gresid_ref, glow_ref, keep1_ref, send1_ref, keep2, send2, wo_out,
-    w1, w2, wo, h2, h2_turned, normed, total, gh2, product1, product2, stage, stage_end, fcg, scales,
-    sems1, sems2, sems,
+    place, counts, a0, a1, a2, a3, b0, b1, b2, b3, att_far, rows_far, gout_far, vec_ref, fcb_ref,
+    out_ref, glow_ref, keep1_ref, send1_ref, sums_ref, fcg, keep2, upper2, lower2, wo_out,
+    w1, w2, wo, att_ref, rows_ref, gout_ref, h2, h2_turned, normed, total, gh2, product1, product2,
+    stage, scales, sems1, sems2, sems,
 ):
-    block = pl.program_id(0)
+    step = pl.program_id(0)
     wide = 2 * BLOCK
+    core, z = place[48], place[50]
+    block_of = lambda step: lax.rem(z + 4 - step, 4)
+    block = block_of(step)
     gain = row_of(vec_ref, 3)
-
-    @pl.when(block == 0)
+    loads = [
+        pltpu.make_async_copy(source, target, sems.at[3 + index])
+        for index, (source, target) in enumerate(
+            ((att_far, att_ref), (rows_far, rows_ref), (gout_far, gout_ref))
+        )
+    ]
+
+    @pl.when(step == 0)
     def _():
-        def work1(source, index, chip, half):
-            spot = pl.ds(pl.multiple_of(chip * 48, 16), 48)
-            for part in range(4):
-                column = 2 * half + part // 2
-                pltpu.make_async_copy(
-                    source.at[index, pl.ds(48 * part, 48)],
-                    w1.at[column, spot, pl.ds(BLOCK * (part % 2), BLOCK)],
-                    sems1.at[column],
-                ).start()
-
-        def work2(source, index, chip, half):
-            spot = pl.ds(pl.multiple_of(chip * 192 + half * 96, 16), 96)
-            for part in range(2):
-                pltpu.make_async_copy(
-                    source.at[index, pl.ds(96 * part, 96)],
-                    w2.at[spot, pl.ds(BLOCK * part, BLOCK)],
-                    sems2.at[chip // 4],
-                ).start()
-
         bring_out_weight(place, (b0, b1, b2, b3), wo, sems.at[2])
-        each_piece(place, 64, (a0, a1, a2, a3), work1)
-        each_piece(place, 0, (b0, b1, b2, b3), work2)
+        loads[0].start()
+        loads[1].start()
+        for later in range(4):
+            column = block_of(later)
+            for first, here in ((0, column // 2 == core), (2, column // 2 != core)):
+
+                @pl.when(here)
+                def _(first=first, column=column):
+                    for number in (first, first + 1):
+
+                        def bring(index, _, source=(a0, a1, a2, a3)[number], number=number, column=column):
+                            spot = pl.ds(pl.multiple_of(place[64 + number * 8 + index] * 48, 16), 48)
+                            for part in range(2):
+                                start = pl.multiple_of(lax.rem(column, 2) * 96 + 48 * part, 16)
+                                pltpu.make_async_copy(
+                                    source.at[index, pl.ds(start, 48)],
+                                    w1.at[column, spot, pl.ds(BLOCK * part, BLOCK)],
+                                    sems1.at[column],
+                                ).start()
+                            return 0
+
+                        lax.fori_loop(0, 8, bring, 0)
+
+            if later == 0:
+                loads[2].start()
+            for number, source in enumerate((b0, b1, b2, b3)):
+                half = core if number < 2 else 1 - core
+                for index in (later, 4 + later):
+                    chip = place[number * 8 + index]
+                    spot = pl.ds(pl.multiple_of(chip * 192 + half * 96, 16), 96)
+                    for part in range(2):
+                        pltpu.make_async_copy(
+                            source.at[index, pl.ds(96 * part, 96)],
+                            w2.at[spot, pl.ds(BLOCK * part, BLOCK)],
+                            sems2.at[column],
+                        ).start()
+
         wait_all(wo, sems.at[2])
         pltpu.make_async_copy(wo, wo_out, sems.at[2]).start()
         bias = row_of(vec_ref, 2)
+        loads[0].wait()
+        loads[1].wait()
         for part in range(2):
             lanes = slice(BLOCK * part, BLOCK * (part + 1))
             total[:, lanes] = rows_ref[:, lanes].astype(F32) + dot(att_ref[...], wo[part]) + bias[:, lanes]
@@ -282,7 +326,9 @@
         low = (normal * gain + row_of(vec_ref, 4)).astype(BF)
         h2[...] = low
         h2_turned[...] = low.T
+        total[...] += row_of(vec_ref, 5)
         gh2[...] = jnp.zeros_like(gh2)
+        loads[2].wait()
 
     wait_all(w1.at[block], sems1.at[block])
     hidden = dot(h2[...], w1[block]) + fcb_ref[block]
@@ -294,63 +340,46 @@
     ghidden = (gactivated * slope).astype(BF)
     product1[...] = dot(h2_turned[...], ghidden)
     product2[...] = dot(activated, gout_ref[...], 0, 0)
-    branch = dot(activated, w2[rows_of, :])
-    gradient = dot(ghidden, w1[block], 1, 1)
+    total[...] += dot(activated, w2[rows_of, :])
+    gh2[...] += dot(ghidden, w1[block], 1, 1)
     fcg[block] = stack_rows([None, None, None, sum_rows(ghidden)])
     give_rows(place, LARGE, product1, keep1_ref, send1_ref)
     for pair in range(4):
-        for which, target in enumerate((keep2, send2)):
-            chip = 4 * block + pair
+        chip = 4 * block + pair
+        for which, target in enumerate((keep2, (upper2, lower2))):
             owner = place[48] if which == 0 else 1 - place[48]
             start = pl.multiple_of(192 * pair + 96 * owner, 8)
             stage[which, chip] = product2[pl.ds(start, 96), :].astype(BF)
-            slot = place[LARGE[which] + chip]
-            pltpu.make_async_copy(stage.at[which, chip], target.at[slot, pl.ds(0, 96)], sems.at[which]).start()
-
-    @pl.when(block < pl.num_programs(0) - 1)
-    def _():
-        @pl.when(block == 0)
-        def _():
-            total[...] = total[...] + row_of(vec_ref, 5)
-
-        total[...] += branch
-        gh2[...] += gradient
-
-    @pl.when(block == pl.num_programs(0) - 1)
+
+            def send(ref, slot, which=which, chip=chip):
+                sem = sems.at[1 if ref is upper2 else 6 if ref is lower2 else 0]
+                pltpu.make_async_copy(stage.at[which, chip], ref.at[slot], sem).start()
+
+            at_slot(target, place[LARGE[which] + chip], send)
+
+    @pl.when(step == pl.num_programs(0) - 1)
     def _():
         length = out_ref.shape[0] // 4
         row_index = lax.broadcasted_iota(jnp.int32, (length, 1), 0)
         for image in range(4):
             rows = slice(length * image, length * (image + 1))
-            value = total[rows, :] + branch[rows]
+            value = total[rows, :]
             out_ref[rows, :] = jnp.where(row_index < counts[image], value, 0.0).astype(BF)
-        whole = gh2[...] + gradient
+        whole = gh2[...]
         gout = gout_ref[...].astype(F32)
         gresid = gout + norm_back(whole * gain, normed[...], scales[:, 0:1])
-        gresid_ref[...] = gresid
         low = gresid.astype(BF)
         glow_ref[...] = low
-        sums = stack_rows(
+        sums_ref[...] = stack_rows(
             [sum_rows(whole * normed[...]), sum_rows(whole), sum_rows(gout), None, sum_rows(low)]
         )
-        product1[...] = dot(att_ref[...], low, 0, 0)
-        for chip in range(CHIPS):
-            below = sums + fcg[chip // 4]
-            for which, target in enumerate((keep2, send2)):
-                owner = place[48] if which == 0 else 1 - place[48]
-                share = product1[pl.ds(pl.multiple_of(48 * chip + 24 * owner, 8), 24), :]
-                stage_end[which, chip] = jnp.concatenate([share, below], axis=0).astype(BF)
-                slot = place[LARGE[which] + chip]
-                pltpu.make_async_copy(
-                    stage_end.at[which, chip], target.at[slot, pl.ds(96, 32)], sems.at[which]
-                ).start()
         wait_all(wo, sems.at[2])
         wait_all(keep2, sems.at[0])
-        wait_all(send2, sems.at[1])
-
-
-def attention_back_kernel(side, wo, qkv_ref, far_ref, glow_ref, *refs):
-    gqkv_ref = refs[-1]
+        wait_all(upper2, sems.at[1])
+        wait_all(lower2, sems.at[6])
+
+
+def attention_back_kernel(side, wo, qkv_ref, far_ref, glow_ref, gqkv_ref):
     low = glow_ref[...]
     mine = slice(BLOCK * side, BLOCK * (side + 1))
     gatt = (
@@ -388,53 +417,58 @@
 
 
 def qkv_grad_kernel(
-    place, h1_turned, gqkv_ref, wq_ref, gh1_ref, sums_ref, keep_ref, send_ref, product
+    place, h1_turned, gqkv_ref, wq_ref, att_ref, glow_ref, gh1_ref, sums_ref, keep_ref, send_ref, product
 ):
     part = pl.program_id(0)
+
+    @pl.when(part < 3)
+    def _():
+        product[...] = dot(h1_turned[...], gqkv_ref[...])
+        gradient = dot(gqkv_ref[...], wq_ref[0], 1, 1)
+        gh1_ref[...] = jnp.where(part == 0, gradient, gh1_ref[...] + gradient)
+        sums_ref[jnp.minimum(part, 2)] = stack_rows([None, None, sum_rows(gqkv_ref[...])])
+
+    @pl.when(part >= 3)
+    def _():
+        product[...] = dot(att_ref[...], glow_ref[...], 0, 0)
+
+    give_rows(place, SMALL, product, keep_ref, send_ref)
+
+
+def input_kernel(
+    place, h1_turned, gqkv_ref, wq_ref, before_ref, mlp_ref, fcg_ref, rows_ref, vec_ref, glow_ref, gh1,
+    ginput_ref, keep_ref, upper_ref, lower_ref,
+    product, sums, total, sems_in,
+):
+    part = pl.program_id(0)
+    load = pltpu.make_async_copy(gh1, total, sems_in)
+
+    @pl.when(part == 0)
+    def _():
+        load.start()
+
     product[...] = dot(h1_turned[...], gqkv_ref[...])
     gradient = dot(gqkv_ref[...], wq_ref[0], 1, 1)
-    gh1_ref[...] = jnp.where(part == 0, gradient, gh1_ref[...] + gradient)
-    sums_ref[part] = stack_rows([None, None, sum_rows(gqkv_ref[...])])
-    give_rows(place, SMALL, product, keep_ref, send_ref)
-
-
-def input_kernel(
-    place, h1_turned, gqkv_ref, wq_ref, before_ref, rows_ref, vec_ref, gresid, gh1,
-    ginput_ref, keep_ref, send_ref,
-    product, sums, gresid_here, total, sems_in,
-):
-    part = pl.program_id(0)
-    loads = [
-        pltpu.make_async_copy(gh1, total, sems_in.at[0]),
-        pltpu.make_async_copy(gresid, gresid_here, sems_in.at[1]),
-    ]
 
     @pl.when(part == 0)
     def _():
-        for load in loads:
-            load.start()
-
-    product[...] = dot(h1_turned[...], gqkv_ref[...])
-    gradient = dot(gqkv_ref[...], wq_ref[0], 1, 1)
-
-    @pl.when(part == 0)
-    def _():
-        loads[0].wait()
+        load.wait()
 
     total[...] += gradient
     sums[part] = stack_rows([None, None, sum_rows(gqkv_ref[...])])
 
+    send_ref = upper_ref, lower_ref
+
     @pl.when(part < 2)
     def _():
-        give_rows(place, SMALL, product, keep_ref, send_ref, lambda chip: jnp.zeros((8, BLOCK), F32))
+        give_rows(place, SMALL, product, keep_ref, send_ref, lambda chip: mlp_ref[...] + fcg_ref[chip // 4])
 
     @pl.when(part == 2)
     def _():
-        loads[1].wait()
         gradient = total[...]
         normed, scale = normed_rows(rows_ref[...].astype(F32))
         ginput_ref[...] = (
-            gresid_here[...] + norm_back(gradient * row_of(vec_ref, 0), normed, scale)
+            glow_ref[...].astype(F32) + norm_back(gradient * row_of(vec_ref, 0), normed, scale)
         ).astype(BF)
         gain, shift = sum_rows(gradient * normed), sum_rows(gradient)
 
@@ -457,27 +491,20 @@
     target[...] = moved[:, :count].reshape(count)
 
 
-def last_second_kernel(place, *refs):
-    sources, (fc2_out, out_out, gain, shift, fc2_bias, out_bias, fc1_bias) = refs[:6], refs[6:]
-    total = add_up([source[0] for source in sources])
-    fc2_out[...] = total[:96]
-    out_out[...] = total[96:120]
-    device = place[49]
-    for line, target in enumerate((gain, shift, fc2_bias, fc1_bias, out_bias)):
-        give_vector(target, total[120 + line : 121 + line], device)
-
-
-def last_heads_kernel(place, *refs):
-    sources, (grad_out, gain, shift, bias) = refs[:12], refs[12:]
+def last_kernel(place, *refs):
+    sources, (qkv_out, out_out), smalls = refs[:12], refs[12:14], refs[14:]
     total_a = add_up([source[0] for source in sources[:6]])
     total_c = add_up([source[0] for source in sources[6:]])
     for part in range(3):
         lanes = slice(BLOCK * part, BLOCK * (part + 1))
-        grad_out[:, 2 * BLOCK * part : 2 * BLOCK * part + BLOCK] = total_a[:, lanes]
-        grad_out[:, 2 * BLOCK * part + BLOCK : 2 * BLOCK * (part + 1)] = total_c[:24, lanes]
+        qkv_out[:, 2 * BLOCK * part : 2 * BLOCK * part + BLOCK] = total_a[:, lanes]
+        qkv_out[:, 2 * BLOCK * part + BLOCK : 2 * BLOCK * (part + 1)] = total_c[:24, lanes]
+    out_out[...] = total_a[:, 3 * BLOCK :]
     device = place[49]
-    for line, target in enumerate((gain, shift, bias)):
+    for line, target in enumerate(smalls[:3]):
         give_vector(target, total_c[24 + line : 25 + line, 2 * BLOCK :], device)
+    for line, target in enumerate(smalls[3:]):
+        give_vector(target, total_c[24 + line : 25 + line, : 2 * BLOCK], device)
 
 
 def after(value, *others):
@@ -532,7 +559,8 @@
             turns = {"x": turn_x, "y": turn_y, "near": near, "far": wide_step}
             return sum(turns[name] * weight for name, weight in zip(order, (8, 4, 2, 1)))
 
-        rest = jnp.where(jnp.arange(16) == 1, dp * 4 + fsdp, core).astype(jnp.int32)
+        others = jnp.stack([core, dp * 4 + fsdp, z]).astype(jnp.int32)
+        rest = jnp.concatenate([others, jnp.zeros((13,), jnp.int32)])
         tables = []
         for orders in (
             (("y", "x", "near", "far"), ("x", "y", "near", "far")),
@@ -587,7 +615,18 @@
     return split.reshape(2 * CHIPS, blocks * 48, BLOCK)
 
 
-def eights(pieces):
+STILL = [
+    16 * core + ((-step % 4) * 2 + (flip2 if core else flip1)) * 2 + (flip1 if core else flip2)
+    for core in range(2)
+    for flip2 in range(2)
+    for flip1 in range(2)
+    for step in range(4)
+]
+
+
+def eights(pieces, order=None):
+    if order is not None:
+        pieces = jnp.stack([pieces[index] for index in order])
     return tuple(pieces[8 * index : 8 * (index + 1)] for index in range(4))
 
 
@@ -666,7 +705,7 @@
         links = None
         place = jnp.concatenate(
             [
-                jnp.arange(32, dtype=jnp.int32) % 16,
+                jnp.array([chip % CHIPS for chip in STILL], jnp.int32),
                 jnp.arange(16, dtype=jnp.int32),
                 jnp.zeros((16,), jnp.int32),
                 jnp.arange(80, dtype=jnp.int32) % 16,
@@ -688,12 +727,12 @@
         whole_fc2 = lax.all_gather(fc2_weight, AXES, axis=0, tiled=True)
         split = whole_fc2.reshape(CHIPS, 2, 96, 2, BLOCK).transpose(1, 0, 3, 2, 4).reshape(32, 192, BLOCK)
         gathered_a = eights(
-            jnp.concatenate([full_pieces(whole_qkv.reshape(width, 3, 2, BLOCK), 3), lines], axis=1)
+            jnp.concatenate([full_pieces(whole_qkv.reshape(width, 3, 2, BLOCK), 3), lines], axis=1), STILL
         )
         gathered_b1 = eights(full_pieces(whole_fc1.reshape(width, 2, 4, BLOCK), 4))
         split = whole_fc2.reshape(CHIPS, 2, 96, 2, BLOCK).transpose(1, 0, 3, 2, 4).reshape(32, 192, BLOCK)
         gathered_b2 = eights(
-            jnp.concatenate([split, full_pieces(whole_out.reshape(width, 1, 2, BLOCK), 1)], axis=1)
+            jnp.concatenate([split, full_pieces(whole_out.reshape(width, 1, 2, BLOCK), 1)], axis=1), STILL
         )
 
     if by_hand:
@@ -711,7 +750,7 @@
             scratch_shapes=list(scratch),
             compiler_params=pltpu.CompilerParams(vmem_limit_bytes=vmem_mib * MIB),
             cost_estimate=pl.CostEstimate(
-                flops=int(flops), bytes_accessed=mib * MIB, transcendentals=0
+                flops=1, bytes_accessed=1, transcendentals=0
             ),
             name=name,
         )(*operands)
@@ -773,76 +812,83 @@
         gathered_b1, gathered_b2 = links.gather_end(on_b1, on_b2)
 
     step_shares = lambda height, columns: pl.BlockSpec((CHIPS, height, columns), lambda step: (0, 0, step))
-    out, gresid, glow, keep_1, send_1, keep_2, send_2, wo = call(
+    still = lambda *shape: pl.BlockSpec(shape, lambda step, place: (0,) * len(shape))
+    turned_shares = pl.BlockSpec(
+        (CHIPS, 24, wide), lambda step, place: (0, 0, lax.rem(place[50] + 4 - step, 4))
+    )
+    low_buffer, wide_buffer = buffer((rows, width), BF), buffer((rows, width), F32)
+    out, glow, keep_1, send_1, sums, fcg, keep_2, upper_2, lower_2, wo = pl.pallas_call(
         mlp_kernel,
-        (place, counts, *gathered_b1, *gathered_b2, att, rows_in, gout, vec, fcb),
-        (low_rows, wide_rows, low_rows)
+        grid_spec=pltpu.PrefetchScalarGridSpec(
+            num_scalar_prefetch=1,
+            grid=(steps,),
+            in_specs=[smem] + [anywhere] * 11 + [still(2, 16, BLOCK), still(steps, 1, wide)],
+            out_specs=(still(rows, width),) * 2
+            + (turned_shares,) * 2
+            + (still(8, wide), still(steps, 8, wide))
+            + (anywhere,) * 4,
+            scratch_shapes=[
+                buffer((steps, width, wide), BF), buffer((hidden_width, width), BF), buffer((2, width, BLOCK), BF),
+                low_buffer, low_buffer, low_buffer, low_buffer, buffer((width, rows), BF),
+                wide_buffer, wide_buffer, wide_buffer, buffer((width, wide), F32), buffer((width, wide), F32),
+                buffer((2, CHIPS, 96, wide), BF), buffer((rows, 128), F32), flag((steps,)), flag((steps,)), flag((7,)),
+            ],
+        ),
+        out_shape=(low_rows, low_rows)
         + (shares(24, hidden_width),) * 2
-        + (shares(128, wide),) * 2
+        + (struct((8, wide), F32), struct((steps, 8, wide), F32))
+        + (shares(96, wide),)
+        + (struct((8, 96, wide), BF),) * 2
         + (struct((2, width, BLOCK), BF),),
-        (fixed(rows, width),) * 3 + (step_shares(24, wide),) * 2 + (anywhere,) * 3,
-        [smem, smem] + [anywhere] * 8 + [fixed(rows, width)] * 3 + [
-            fixed(2, 16, BLOCK), fixed(steps, 1, wide),
-        ],
-        12 * rows * width * hidden_width,
-        32,
-        60,
-        grid=(steps,),
-        scratch=(
-            buffer((steps, width, wide), BF), buffer((hidden_width, width), BF), buffer((2, width, BLOCK), BF),
-            buffer((rows, width), BF), buffer((width, rows), BF), buffer((rows, width), F32),
-            buffer((rows, width), F32), buffer((rows, width), F32), buffer((width, wide), F32),
-            buffer((width, wide), F32), buffer((2, CHIPS, 96, wide), BF), buffer((2, CHIPS, 32, wide), BF),
-            buffer((steps, 8, wide), F32), buffer((rows, 128), F32), flag((steps,)), flag((steps,)), flag((3,)),
-        ),
+        compiler_params=pltpu.CompilerParams(vmem_limit_bytes=60 * MIB),
+        cost_estimate=pl.CostEstimate(flops=1, bytes_accessed=1, transcendentals=0),
         name="mlp",
-    )
+    )(place, counts, *gathered_b1, *gathered_b2, att, rows_in, gout, vec, fcb)
+
     if by_hand:
-        state_2 = keep_2, links.move(send_2, links.cores)
-        state_1 = keep_1, links.move(after(send_1, keep_2), links.cores)
-
-    def attention_back(side, gradient, first, count, vmem_mib, before=()):
-        some_rows = lambda columns: pl.BlockSpec((padded, columns), lambda image: (first + image, 0))
-        return pl.pallas_call(
+        state_2 = keep_2, links.move(upper_2, links.cores)
+
+    def attention_back(side, gradient):
+        return call(
             lambda *refs: attention_back_kernel(side, *refs),
-            grid=(count,),
-            out_shape=struct((rows, third), BF),
-            in_specs=[
-                fixed(2, width, BLOCK),
-                pl.BlockSpec((1, padded, third), lambda image: (side, first + image, 0)),
-                pl.BlockSpec((1, padded, padded), lambda image: (first + image, 0, 0)),
-                some_rows(width),
-            ]
-            + [anywhere] * len(before),
-            out_specs=some_rows(third),
-            input_output_aliases={4: 0} if before else {},
-            compiler_params=pltpu.CompilerParams(vmem_limit_bytes=vmem_mib * MIB),
-            cost_estimate=pl.CostEstimate(flops=1, bytes_accessed=1, transcendentals=0),
+            (wo, qkv, far_turned, gradient),
+            struct((rows, third), BF),
+            image_rows(third),
+            [
+                fixed(2, width, BLOCK), pl.BlockSpec((1, padded, third), lambda image: (side, image, 0)),
+                image_far, image_rows(width),
+            ],
+            8 * rows * 256 * width,
+            8,
+            20,
+            grid=(images,),
             name="attention_back",
-        )(wo, qkv, far_turned, gradient, *before)
-
-    gqkv_0 = attention_back(0, glow, 0, images // 2, 60)
+        )
+
     part_2 = glow
     if by_hand:
-        state_2, gqkv_0 = lax.optimization_barrier((state_2, gqkv_0))
-        part_2 = links.fold(state_2)
-        state_2 += (links.move(part_2, links.second),)
-    gqkv_0 = attention_back(0, join(glow, part_2), images // 2, images - images // 2, 60, (gqkv_0,))
+        part_2 = add_up([keep_2[8:], state_2[1]]).astype(BF)
+        lower_2, send_1 = after((lower_2, send_1), part_2)
+        state_2 = keep_2, links.move(lower_2, links.cores), links.move(part_2, links.second)
+        state_1 = keep_1, links.move(send_1, links.cores)
+    gqkv_0 = attention_back(0, join(glow, part_2))
     if by_hand:
         state_1, gqkv_0 = lax.optimization_barrier((state_1, gqkv_0))
         state_1 += (links.move(links.fold(state_1), links.second),)
 
-    step_weight = lambda side: pl.BlockSpec((1, width, BLOCK), lambda step: (side, 0, step))
+    step_weight = lambda side: pl.BlockSpec((1, width, BLOCK), lambda step: (side, 0, jnp.minimum(step, 2)))
+    early_rows = pl.BlockSpec((rows, BLOCK), lambda step: (0, jnp.minimum(step, 2)))
+    late_rows = pl.BlockSpec((rows, BLOCK), lambda step: (0, jnp.maximum(step - 3, 0)))
     gh1, sums_0, keep_a, send_a = call(
         qkv_grad_kernel,
-        (place, h1_turned, gqkv_0, wq),
-        (wide_rows, struct((3, 8, BLOCK), F32)) + (shares(24, third),) * 2,
+        (place, h1_turned, gqkv_0, wq, att, glow),
+        (wide_rows, struct((3, 8, BLOCK), F32)) + (shares(24, third + wide),) * 2,
         (fixed(rows, width), fixed(3, 8, BLOCK)) + (step_shares(24, BLOCK),) * 2,
-        [smem, fixed(width, rows), step_rows(BLOCK), step_weight(0)],
+        [smem, fixed(width, rows), early_rows, step_weight(0), fixed(rows, width), late_rows],
         6 * rows * width * width,
         10,
         24,
-        grid=(3,),
+        grid=(5,),
         scratch=(buffer((width, BLOCK), F32),),
         name="qkv_grad",
     )
@@ -853,27 +899,30 @@
         part_2 = links.fold(state_2)
         state_2 += (links.move(part_2, links.near),)
 
-    gqkv_1 = attention_back(1, join(glow, gh1, part_2), 0, images, 20)
+    gqkv_1 = attention_back(1, join(glow, gh1, part_2))
     if by_hand:
         state_a, gqkv_1 = lax.optimization_barrier((state_a, gqkv_1))
         state_a += (links.move(links.fold(state_a), links.second),)
 
-    ginput, keep_c, send_c = call(
+    half_shares = pl.BlockSpec((8, 32, BLOCK), lambda step: (0, 0, step))
+    mlp_small = pl.BlockSpec((8, BLOCK), lambda step: (0, jnp.minimum(step, 1)))
+    ginput, keep_c, upper_c, lower_c = call(
         input_kernel,
-        (place, h1_turned, gqkv_1, wq, sums_0, rows_in, vec, gresid, gh1),
-        (low_rows,) + (shares(32, third),) * 2,
-        (fixed(rows, width),) + (step_shares(32, BLOCK),) * 2,
+        (place, h1_turned, gqkv_1, wq, sums_0, sums, fcg, rows_in, vec, glow, gh1),
+        (low_rows, shares(32, third)) + (struct((8, 32, third), BF),) * 2,
+        (fixed(rows, width), step_shares(32, BLOCK)) + (half_shares,) * 2,
         [
-            smem, fixed(width, rows), step_rows(BLOCK), step_weight(1), fixed(3, 8, BLOCK), fixed(rows, width), fixed(2, 16, BLOCK),
-            anywhere, anywhere,
+            smem, fixed(width, rows), step_rows(BLOCK), step_weight(1), fixed(3, 8, BLOCK), mlp_small,
+            pl.BlockSpec((steps, 8, BLOCK), lambda step: (0, 0, jnp.minimum(step, 1))), fixed(rows, width),
+            fixed(2, 16, BLOCK),
+            fixed(rows, width), anywhere,
         ],
         6 * rows * width * width,
         14,
         30,
         grid=(3,),
         scratch=(
-            buffer((width, BLOCK), F32), buffer((3, 8, BLOCK), F32), buffer((rows, width), F32),
-            buffer((rows, width), F32), flag((2,)),
+            buffer((width, BLOCK), F32), buffer((3, 8, BLOCK), F32), buffer((rows, width), F32), flag,
         ),
         name="input_grad",
     )
@@ -883,85 +932,96 @@
     if by_hand:
         fold, move = links.fold, links.move
 
-        def last_sum(kernel, state, heights, counts_out):
-            first = lambda part: pl.BlockSpec((1,) + part.shape[1:], lambda step: (0, 0, 0))
-            columns = 3 * width if kernel is last_heads_kernel else width
-            return pl.pallas_call(
-                kernel,
-                grid=(1,),
-                out_shape=tuple(struct((height, columns), F32) for height in heights)
-                + tuple(struct((count,), F32) for count in counts_out),
-                in_specs=[smem] + [first(part) for part in state],
-                out_specs=tuple(fixed(height, columns) for height in heights)
-                + tuple(pl.BlockSpec((count,), lambda step: (0,)) for count in counts_out),
-                compiler_params=pltpu.CompilerParams(vmem_limit_bytes=30 * MIB),
-                name="last_sum",
-            )(place, *state)
-
-        state_c = keep_c, move(send_c, links.cores)
+        state_c = keep_c, move(upper_c, links.cores)
+        rest_c = move(after(lower_c, keep_c), links.cores)
         state_1 = after(state_1, keep_c)
         part = fold(state_1)
         state_1 += (move(part, links.near),)
+        keep_c, got_c = after(state_c, part)
+        part = add_up([keep_c[8:], got_c]).astype(BF)
+        state_c = keep_c, rest_c, move(part, links.second)
+        state_2 = after(state_2, part)
+        part = fold(state_2)
+        state_2 += (move(part, links.first),)
+        state_a, out, ginput = after((state_a, out, ginput), part)
+        part = fold(state_a)
+        state_a += (move(part, links.first),)
+        out, ginput = cut(out), cut(ginput)
         part = fold(after(state_c, part))
-        state_c += (move(part, links.second),)
-        state_2, state_a = after((state_2, state_a), part)
-        parts = fold(state_2), fold(state_a)
-        state_2 += (move(parts[0], links.first),)
-        state_a += (move(parts[1], links.first),)
-        out, ginput = after((out, ginput), parts)
-        out, ginput = cut(out), cut(ginput)
-        part = fold(after(state_c, parts))
         state_c += (move(part, links.first),)
-        state_1, state_2, state_a, out, ginput = after((state_1, state_2, state_a, out, ginput), part)
-        parts = fold(state_2), fold(state_1), fold(state_a)
-        state_2 += (move(parts[0], links.far),)
-        state_1 += (move(parts[1], links.first),)
-        state_a += (move(parts[2], links.near),)
-        part = fold(after(state_c, parts))
+        state_1, out, ginput = after((state_1, out, ginput), part)
+        part = fold(state_1)
+        state_1 += (move(part, links.first),)
+        state_2 = after(state_2, part)
+        part = fold(state_2)
+        state_2 += (move(part, links.far),)
+        state_a = after(state_a, part)
+        part = fold(state_a)
+        state_a += (move(part, links.near),)
+        part = fold(after(state_c, part))
         state_c += (move(part, links.near),)
-        state_1, state_a = after((state_1, state_a), part)
-        parts = fold(state_1), fold(state_a)
-        state_1 += (move(parts[0], links.far),)
-        state_a += (move(parts[1], links.far),)
-        part = fold(after(state_c, parts))
+        state_1 = after(state_1, part)
+        part = fold(state_1)
+        state_1 += (move(part, links.far),)
+        state_a = after(state_a, part)
+        part = fold(state_a)
+        state_a += (move(part, links.far),)
+        part = fold(after(state_c, part))
         state_c += (move(part, links.far),)
         state_2 = after(state_2, part)
-        mine_2 = last_sum(last_second_kernel, state_2, (96, 24), (24, 24, 24, 24, 96))
+        mine_2 = add_up([part[0] for part in state_2])
         state_1 = after(state_1, mine_2)
         mine_1 = add_up([part[0] for part in state_1])
-        mine_c = last_sum(last_heads_kernel, state_a + state_c, (24,), (24, 24, 48))
-        fc2_grad, out_grad, ln2_gain_grad, ln2_bias_grad, fc2_bias_grad, out_bias_grad, fc1_bias_grad = mine_2
-        qkv_grad, ln1_gain_grad, ln1_bias_grad, qv_bias_grad = mine_c
+        own_slot = lambda part: pl.BlockSpec((1,) + part.shape[1:], lambda step: (0, 0, 0))
+        heights, counts_out = ((24, 3 * width), (24, width)), (24, 24, 48, 24, 24, 24, 96, 24)
+        (
+            qkv_grad, out_grad, ln1_gain_grad, ln1_bias_grad, qv_bias_grad,
+            ln2_gain_grad, ln2_bias_grad, fc2_bias_grad, fc1_bias_grad, out_bias_grad,
+        ) = pl.pallas_call(
+            last_kernel,
+            grid=(1,),
+            out_shape=tuple(struct(shape, F32) for shape in heights + tuple((count,) for count in counts_out)),
+            in_specs=[smem] + [own_slot(part) for part in state_a + state_c],
+            out_specs=tuple(fixed(*shape) for shape in heights)
+            + tuple(pl.BlockSpec((count,), lambda step: (0,)) for count in counts_out),
+            compiler_params=pltpu.CompilerParams(vmem_limit_bytes=30 * MIB),
+            name="last",
+        )(place, *state_a, *state_c)
         return (
             out, ginput, ln1_gain_grad, ln1_bias_grad, qkv_grad, qv_bias_grad, out_grad, out_bias_grad,
-            ln2_gain_grad, ln2_bias_grad, mine_1, fc1_bias_grad, fc2_grad, fc2_bias_grad,
+            ln2_gain_grad, ln2_bias_grad, mine_1, fc1_bias_grad, mine_2, fc2_bias_grad,
         )
 
     both_a, both_c, both_1, both_2 = (
         jnp.stack(pair, axis=1).astype(F32)
-        for pair in ((keep_a, send_a), (keep_c, send_c), (keep_1, send_1), (keep_2, send_2))
+        for pair in (
+            (keep_a, send_a),
+            (keep_c, jnp.concatenate([lower_c, upper_c])),
+            (keep_1, send_1),
+            (keep_2, jnp.concatenate([lower_2, upper_2])),
+        )
     )
     heads = jnp.stack(
-        [both.reshape(CHIPS, 2, 24, 3, BLOCK) for both in (both_a, both_c[:, :, :24])], axis=4
+        [both.reshape(CHIPS, 2, 24, 3, BLOCK) for both in (both_a[..., :third], both_c[:, :, :24])], axis=4
     )
 
     def vector(lines, count):
         columns = lines.shape[-1]
         return lines.reshape(32 * count // columns, -1, columns)[:, 0].reshape(-1)
 
-    small_c, small_2 = both_c[:, :, 24:, 2 * BLOCK :], both_2[:, :, 120:]
+    small_c, small_2 = both_c[:, :, 24:, 2 * BLOCK :], both_c[:, :, 24:, : 2 * BLOCK]
     totals = (
         vector(small_c[:, :, 0], 24),
         vector(small_c[:, :, 1], 24),
         heads.reshape(width, 3 * width),
         vector(small_c[:, :, 2], 48),
-        both_2[:, :, 96:120].reshape(width, width),
+        both_a[..., third:].reshape(width, width),
         vector(small_2[:, :, 4], 24),
         vector(small_2[:, :, 0], 24),
         vector(small_2[:, :, 1], 24),
         both_1.reshape(width, hidden_width),
         vector(small_2[:, :, 3], 96),
-        both_2[:, :, :96].reshape(hidden_width, width),
+        both_2.reshape(hidden_width, width),
         vector(small_2[:, :, 2], 24),
     )
     return (cut(out), cut(ginput)) + tuple(

time: 241 us -> 231 us (0.959)
  waiting for transfers between devices: 72 us -> 88.5 us
  other arithmetic: 20.1 us -> 9.56 us
  Pallas kernels: 89.7 us -> 82.3 us
  local copies, waits for them, and re-layouts: 16 us -> 11.8 us
  starting transfers between devices: 41.2 us -> 37.3 us
    pallas_call x5 -> x6, Pallas kernels: 64.8 us -> 42.6 us  [call(): pl.pallas_call(kernel, grid=grid, out_shape=out_shape, in_specs=in_specs,...]
    ppermute x42 -> x44, waiting for transfers between devices: 72 us -> 88.5 us  [move(): return lax.ppermute(value, AXES, pairs)]
    pallas_call x5 -> x2, Pallas kernels: 21.2 us -> 35.9 us  [the longest x1 34.5 us: shards(): pl.pallas_call(mlp_kernel, grid_spec=pltpu.PrefetchScalarGridSpec(num_sca...]
    convert_element_type x16 -> x14, other arithmetic: 13.5 us -> 2.05 us  [fold(): return add_up([part[left // 2:left] for part in state]).astype(BF)]
    unnamed x84 -> x80, local copies, waits for them, and re-layouts: 10.4 us -> 6.08 us
    ppermute x42 -> x44, starting transfers between devices: 41.2 us -> 37.3 us  [move(): return lax.ppermute(value, AXES, pairs)]
  transfers between devices with their start and end apart: 42 -> 44, of which waited for: 17 -> 21; matrix products, arithmetic and copies ran while one was open for 10% -> 6% of each run, Pallas kernels for 19% -> 18%
where the time goes in v3:
time: 231 us
  waiting for transfers between devices  88.5 us (38%)
  Pallas kernels  82.3 us (36%)
  starting transfers between devices  37.3 us (16%)
  local copies, waits for them, and re-layouts  11.8 us (5%)
  other arithmetic  9.56 us (4%)
    ppermute x44, waiting for transfers between devices, move(): return lax.ppermute(value, AXES, pairs)  88.5 us
    pallas_call x6, Pallas kernels, call(): pl.pallas_call(kernel, grid=grid, out_shape=out_shape, in_specs=in_specs,...  42.6 us
    ppermute x44, starting transfers between devices, move(): return lax.ppermute(value, AXES, pairs)  37.3 us
    pallas_call x1, Pallas kernels, shards(): pl.pallas_call(mlp_kernel, grid_spec=pltpu.PrefetchScalarGridSpec(num_sca...  34.5 us
    unnamed x80, local copies, waits for them, and re-layouts  6.08 us
  transfers between devices with their start and end apart: 44, of which 21 were waited for; matrix products, arithmetic and copies ran while one was open for 6% of the time, Pallas kernels for 18%

profile of v3, /device:TPU:0, one launch (start us, length us, event | category | flops | bytes accessed | tf_op | source)
XLA Modules:
  0.0 231.1 jit_solution(1979873081861493589)
XLA Ops:
  0.8 0.7 concatenate.20.place
  1.5 1.8 share.1
  3.7 0.7 iota_compare_fusion
  4.4 0.7 fusion.2
  5.8 2.0 pair.1
  7.8 4.8 %collective-permute-start.2 = (bf16[160,384]{1,0:T(8,128)(2,1)}, bf16[160,384]{1,0:T(8,128)(2,1)S(1)}, u32[]{:S(2)}, u32[]{:S(2)}) collective-permute-start(bf16[160,384]{1,0:T(8,128)(2,1)} %get-tuple-element.163), channel_id=1, source_target_pairs={{0,24},{1,25},{2,26},{3,27},{4,28},{5,29},{6,30},{7,31},{8,0},{9,1... | collective-permute-start | bytes 368648 | tf_op jit(solution)/shard_map/ppermute | solution.py:537
  12.5 1.5 collective-permute-start.3
  14.0 1.5 fusion
  15.6 0.9 collective-permute-done.2
  16.6 3.3 %collective-permute-done.1 = bf16[160,384]{1,0:T(8,128)(2,1)S(1)} collective-permute-done((bf16[160,384]{1,0:T(8,128)(2,1)}, bf16[160,384]{1,0:T(8,128)(2,1)S(1)}, u32[]{:S(2)}, u32[]{:S(2)}) %collective-permute-start.1) | collective-permute-done | bytes 122912 | tf_op jit(solution)/shard_map/ppermute | solution.py:537
  19.9 1.6 collective-permute-start.5
  21.5 0.7 pad_select_fusion
  22.2 1.1 copy.32
  24.0 1.2 collective-permute-start.4
  25.2 5.5 %collective-permute-done.4 = bf16[160,384]{1,0:T(8,128)(2,1)S(1)} collective-permute-done((bf16[160,384]{1,0:T(8,128)(2,1)S(1)}, bf16[160,384]{1,0:T(8,128)(2,1)S(1)}, u32[]{:S(2)}, u32[]{:S(2)}) %collective-permute-start.4) | collective-permute-done | bytes 122912 | tf_op jit(solution)/shard_map/ppermute | solution.py:537
  30.8 1.6 collective-permute-start.6
  32.5 2.0 collective-permute-start.7
  34.6 6.8 %collective-permute-done.8 = bf16[240,384]{1,0:T(8,128)(2,1)S(1)} collective-permute-done((bf16[240,384]{1,0:T(8,128)(2,1)S(1)}, bf16[240,384]{1,0:T(8,128)(2,1)S(1)}, u32[]{:S(2)}, u32[]{:S(2)}) %collective-permute-start.8) | collective-permute-done | bytes 184352 | tf_op jit(solution)/shard_map/ppermute | solution.py:537
  42.1 1.2 collective-permute-start.10
  43.4 15.0 %collective-permute-done.11 = bf16[4,192,384]{2,1,0:T(8,128)(2,1)S(1)} collective-permute-done((bf16[4,192,384]{2,1,0:T(8,128)(2,1)S(1)}, bf16[4,192,384]{2,1,0:T(8,128)(2,1)S(1)}, u32[]{:S(2)}, u32[]{:S(2)}) %collective-permute-start.11) | collective-permute-done | bytes 589856 | tf_op jit(solution)/shard_map/ppermute | solution.py:537
  58.3 2.0 collective-permute-done.10
  60.4 1.8 collective-permute-start.15
  62.9 7.1 %qkv.1 = (f32[2,16,384]{2,1,0:T(8,128)S(1)}, f32[4,1,768]{2,1,0:T(1,128)S(1)}, bf16[768,640]{1,0:T(8,128)(2,1)S(1)}, bf16[2,640,1152]{2,1,0:T(8,128)(2,1)S(1)}, bf16[2,768,1152]{2,1,0:T(8,128)(2,1)S(1)}) custom-call(s32[144]{0:T(256)S(1)} %copy-done.15, bf16[8,160,384]{2,1,0:T(8,128)(2,1)S(1)} %constant_dynamic-update-slice_fusion.own0, ...), custom_call_target="tpu_custom_call" | custom-call | flops 1 | bytes 1 | tf_op jit(solution)/shard_map/qkv/pallas_call | solution.py:744
  70.0 1.8 copy-done.3
  71.8 4.5 %collective-permute-done.14 = bf16[4,192,384]{2,1,0:T(8,128)(2,1)S(1)} collective-permute-done((bf16[4,192,384]{2,1,0:T(8,128)(2,1)S(1)}, bf16[4,192,384]{2,1,0:T(8,128)(2,1)S(1)}, u32[]{:S(2)}, u32[]{:S(2)}) %collective-permute-start.14) | collective-permute-done | bytes 589856 | tf_op jit(solution)/shard_map/ppermute | solution.py:537
  76.6 1.7 collective-permute-start.18
  78.8 6.3 %attention.1.att_far.att_ref = bf16[640,768]{1,0:T(8,128)(2,1)S(1)} custom-call(bf16[2,640,1152]{2,1,0:T(8,128)(2,1)S(1)} %get-tuple-element.180.qkv_ref.refs_1_, f32[4,160,160]{2,1,0:T(8,128)S(1)} %copy-done.11), custom_call_target="tpu_custom_call" | custom-call | flops 1 | bytes 1 | tf_op jit(solution)/shard_map/attention/pallas_call | solution.py:744
  85.2 11.0 %collective-permute-done.16 = bf16[4,192,384]{2,1,0:T(8,128)(2,1)S(1)} collective-permute-done((bf16[4,192,384]{2,1,0:T(8,128)(2,1)S(1)}, bf16[4,192,384]{2,1,0:T(8,128)(2,1)S(1)}, u32[]{:S(2)}, u32[]{:S(2)}) %collective-permute-start.16) | collective-permute-done | bytes 589856 | tf_op jit(solution)/shard_map/ppermute | solution.py:537
  97.2 6.1 %collective-permute-done.19.a3 = bf16[8,192,384]{2,1,0:T(8,128)(2,1)S(1)} collective-permute-done((bf16[8,192,384]{2,1,0:T(8,128)(2,1)S(1)}, bf16[8,192,384]{2,1,0:T(8,128)(2,1)S(1)}, u32[]{:S(2)}, u32[]{:S(2)}) %collective-permute-start.19) | collective-permute-done | bytes 1179680 | tf_op jit(solution)/shard_map/ppermute | solution.py:537
  103.3 1.2 copy-done.25
  104.8 0.8 copy-done.26
  105.6 34.5 %mlp.1 = (bf16[640,768]{1,0:T(8,128)(2,1)}, bf16[640,768]{1,0:T(8,128)(2,1)}, bf16[16,24,3072]{2,1,0:T(8,128)(2,1)}, bf16[16,24,3072]{2,1,0:T(8,128)(2,1)}, f32[...) custom-call(s32[144]{0:T(256)} %concatenate.20.place, ...), custom_call_target="tpu_custom_call" | custom-call | flops 1 | bytes 1 | tf_op jit(solution)/shard_map/mlp/pallas_call | solution.py:820
  140.3 3.0 %collective-permute-done.22 = bf16[8,96,768]{2,1,0:T(8,128)(2,1)S(1)} collective-permute-done((bf16[8,96,768]{2,1,0:T(8,128)(2,1)}, bf16[8,96,768]{2,1,0:T(8,128)(2,1)S(1)}, u32[]{:S(2)}, u32[]{:S(2)}) %collective-permute-start.22) | collective-permute-done | bytes 1179680 | tf_op jit(solution)/shard_map/ppermute | solution.py:537
  143.2 1.7 add_convert_fusion.1
  145.2 1.5 collective-permute-start.27
  146.8 6.7 %attention_back.2.gqkv_ref = bf16[640,1152]{1,0:T(8,128)(2,1)S(1)} custom-call(bf16[2,768,384]{2,1,0:T(8,128)(2,1)S(1)} %copy-done.8, bf16[2,640,1152]{2,1,0:T(8,128)(2,1)S(1)} %get-tuple-element.180.qkv_ref.refs_1_, f32[4,160,160]{2,1,0:T(8,128)S(1)} %copy-done.7, bf16[640,768]{1,0:T(8,128)(2,1)S(1)} %copy-done), custom_call_target="tpu_custom_call" | custom-call | flops 1 | bytes 1 | tf_op jit(solution)/shard_map/attention_back/pallas_call | solution.py:744
  153.6 7.3 %qkv_grad.1 = (f32[640,768]{1,0:T(8,128)S(1)}, f32[3,8,384]{2,1,0:T(8,128)S(1)}, bf16[16,24,1920]{2,1,0:T(8,128)(2,1)S(1)}, bf16[16,24,1920]{2,1,0:T(8,128)(2,1)S(1)}) custom-call(s32[144]{0:T(256)S(1)} %copy-done.16, bf16[768,640]{1,0:T(8,128)(2,1)S(1)} %copy-done.10, bf16[640,1152]{1,0:T(8,128)(2,1)S(1)} %attention_back.2.gqkv_ref, ...), custom_call_target="tpu_custom_call" | custom-call | flops 1 | bytes 1 | tf_op jit(solution)/shard_map/qkv_grad/pallas_call | solution.py:744
  162.9 6.5 %attention_back.3.gqkv_ref = bf16[640,1152]{1,0:T(8,128)(2,1)S(1)} custom-call(bf16[2,768,384]{2,1,0:T(8,128)(2,1)S(1)} %copy-done.8, bf16[2,640,1152]{2,1,0:T(8,128)(2,1)S(1)} %get-tuple-element.180.qkv_ref.refs_1_, f32[4,160,160]{2,1,0:T(8,128)S(1)} %copy-done.7, bf16[640,768]{1,0:T(8,128)(2,1)S(1)} %copy-done), custom_call_target="tpu_custom_call" | custom-call | flops 1 | bytes 1 | tf_op jit(solution)/shard_map/attention_back/pallas_call | solution.py:744
  169.5 8.7 %input_grad.1 = (bf16[640,768]{1,0:T(8,128)(2,1)S(1)}, bf16[16,32,1152]{2,1,0:T(8,128)(2,1)S(1)}, bf16[8,32,1152]{2,1,0:T(8,128)(2,1)S(1)}, bf16[8,32,1152]{2,1,0:T(8,128)(2,1)S(1)}) custom-call(s32[144]{0:T(256)S(1)} %copy-done.16, bf16[768,640]{1,0:T(8,128)(2,1)S(1)} %copy-done.10, bf16[640,1152]{1,0:T(8,128)(2,1)S(1)} %attention_back.3.gqkv_ref, ...), custom_call_target="tpu_custom_call" | custom-call | flops 1 | bytes 1 | tf_op jit(solution)/shard_map/input_grad/pallas_call | solution.py:744
  178.9 1.8 collective-permute-start.28
  181.0 1.3 collective-permute-start.29
  182.5 0.8 collective-permute-start.33
  183.5 1.4 collective-permute-start.35
  184.9 10.8 %collective-permute-done.29.refs_2_ = bf16[8,24,1920]{2,1,0:T(8,128)(2,1)S(1)} collective-permute-done((bf16[8,24,1920]{2,1,0:T(8,128)(2,1)S(1)}, bf16[8,24,1920]{2,1,0:T(8,128)(2,1)S(1)}, u32[]{:S(2)}, u32[]{:S(2)}) %collective-permute-start.29) | collective-permute-done | bytes 737312 | tf_op jit(solution)/shard_map/ppermute | solution.py:537
  195.8 1.7 copy.35
  197.5 1.7 copy.36
  199.2 1.3 collective-permute-start.34
  200.5 2.2 collective-permute-done.33.refs_8_
  202.8 1.4 collective-permute-start.38
  204.4 0.7 collective-permute-start.37
  205.2 1.1 collective-permute-start.43
  206.8 1.4 collective-permute-start.36
  208.1 1.7 collective-permute-done.38.refs_9_
  210.3 2.6 %collective-permute-done.37 = bf16[2,24,3072]{2,1,0:T(8,128)(2,1)S(1)} collective-permute-done((bf16[2,24,3072]{2,1,0:T(8,128)(2,1)S(1)}, bf16[2,24,3072]{2,1,0:T(8,128)(2,1)S(1)}, u32[]{:S(2)}, u32[]{:S(2)}) %collective-permute-start.37) | collective-permute-done | bytes 294944 | tf_op jit(solution)/shard_map/ppermute | solution.py:537
  213.1 1.1 collective-permute-start.42
  214.2 1.8 collective-permute-done.36.refs_4_
  216.0 1.3 collective-permute-start.39
  217.3 3.3 %collective-permute-done.40.refs_10_ = bf16[2,32,1152]{2,1,0:T(8,128)(2,1)S(1)} collective-permute-done((bf16[2,32,1152]{2,1,0:T(8,128)(2,1)S(1)}, bf16[2,32,1152]{2,1,0:T(8,128)(2,1)S(1)}, u32[]{:S(2)}, u32[]{:S(2)}) %collective-permute-start.40) | collective-permute-done | bytes 147488 | tf_op jit(solution)/shard_map/ppermute | solution.py:537
  220.8 0.8 add_bitcast_fusion.1
  221.6 5.2 %collective-permute-done.42 = bf16[1,24,3072]{2,1,0:T(8,128)(2,1)S(1)} collective-permute-done((bf16[1,24,3072]{2,1,0:T(8,128)(2,1)S(1)}, bf16[1,24,3072]{2,1,0:T(8,128)(2,1)S(1)}, u32[]{:S(2)}, u32[]{:S(2)}) %collective-permute-start.42) | collective-permute-done | bytes 147488 | tf_op jit(solution)/shard_map/ppermute | solution.py:537
  226.8 0.8 add_bitcast_fusion
  227.6 1.1 collective-permute-done.39.refs_5_
  228.7 0.8 collective-permute-done.41.refs_11_
  229.5 1.4 last.1
  (154 shorter events, 11.2 us)
Async XLA Ops:
  3.3 1.9 collective-permute-start
  5.8 15.7 %copy-start.30 = (bf16[4,153,768]{2,0,1:T(4,128)(2,1)S(1)}, bf16[4,153,768]{2,0,1:T(4,128)(2,1)}, u32[]{:S(2)}) copy-start(bf16[4,153,768]{2,0,1:T(4,128)(2,1)} %param.31) | copy-start | bytes 2820100
  7.8 12.1 %copy-start.32 = (bf16[192,384]{1,0:T(8,128)(2,1)S(1)}, bf16[192,384]{1,0:T(8,128)(2,1)}, u32[]{:S(2)}) copy-start(bf16[192,384]{1,0:T(8,128)(2,1)} %get-tuple-element.164) | copy-start | bytes 442372
  7.8 8.8 %collective-permute-start.2 = (bf16[160,384]{1,0:T(8,128)(2,1)}, bf16[160,384]{1,0:T(8,128)(2,1)S(1)}, u32[]{:S(2)}, u32[]{:S(2)}) collective-permute-start(bf16[160,384]{1,0:T(8,128)(2,1)} %get-tuple-element.163), channel_id=1, source_target_pairs={{0,24},{1,25},{2,26},{3,27},{4,28},{5,29},{6,30},{7,31},{8,0},{9,1... | collective-permute-start | bytes 368648 | tf_op jit(solution)/shard_map/ppermute | solution.py:537
  12.5 7.3 %collective-permute-start.1 = (bf16[160,384]{1,0:T(8,128)(2,1)}, bf16[160,384]{1,0:T(8,128)(2,1)S(1)}, u32[]{:S(2)}, u32[]{:S(2)}) collective-permute-start(bf16[160,384]{1,0:T(8,128)(2,1)} %get-tuple-element.163), channel_id=1, source_target_pairs={{0,8},{1,9},{2,10},{3,11},{4,12},{5,13},{6,14},{7,15},{8,16},{9,17... | collective-permute-start | bytes 368648 | tf_op jit(solution)/shard_map/ppermute | solution.py:537
  12.5 7.3 %collective-permute-start.3 = (bf16[192,384]{1,0:T(8,128)(2,1)}, bf16[192,384]{1,0:T(8,128)(2,1)S(1)}, u32[]{:S(2)}, u32[]{:S(2)}) collective-permute-start(bf16[192,384]{1,0:T(8,128)(2,1)} %get-tuple-element.164), channel_id=1, source_target_pairs={{0,4},{1,3},{2,6},{3,1},{4,0},{5,7},{6,2},{7,5},{8,12},{9,11},{10,... | collective-permute-start | bytes 442376 | tf_op jit(solution)/shard_map/ppermute | solution.py:537
  19.9 10.8 %collective-permute-start.5 = (bf16[2,192,384]{2,1,0:T(8,128)(2,1)S(1)}, bf16[2,192,384]{2,1,0:T(8,128)(2,1)S(1)}, u32[]{:S(2)}, u32[]{:S(2)}) collective-permute-start(bf16[2,192,384]{2,1,0:T(8,128)(2,1)S(1)} %pad_maximum_fusion.3), channel_id=1, source_target_pairs={{0,2},{1,5},{2,0},{3,7},{4,6},{5,1},{6,4},{7,3},{8,10},{9,13},{10,... | collective-permute-start | bytes 884744 | tf_op jit(solution)/shard_map/ppermute | solution.py:537
  23.9 38.9 %copy-start.1 = (bf16[4,160,768]{2,1,0:T(8,128)(2,1)}, bf16[4,160,768]{2,1,0:T(8,128)(2,1)S(1)}, u32[]{:S(2)}) copy-start(bf16[4,160,768]{2,1,0:T(8,128)(2,1)S(1)} %pad.11.clone) | copy-start | bytes 2949124
  24.0 8.5 %copy-start.34 = (bf16[240,384]{1,0:T(8,128)(2,1)S(1)}, bf16[240,384]{1,0:T(8,128)(2,1)}, u32[]{:S(2)}) copy-start(bf16[240,384]{1,0:T(8,128)(2,1)} %get-tuple-element.170) | copy-start | bytes 552964
  24.0 6.7 %collective-permute-start.4 = (bf16[160,384]{1,0:T(8,128)(2,1)S(1)}, bf16[160,384]{1,0:T(8,128)(2,1)S(1)}, u32[]{:S(2)}, u32[]{:S(2)}) collective-permute-start(bf16[160,384]{1,0:T(8,128)(2,1)S(1)} %collective-permute-done.1), channel_id=1, source_target_pairs={{0,8},{1,9},{2,10},{3,11},{4,12},{5,13},{6,14},{7,15},{8,16},{9,17... | collective-permute-start | bytes 368648 | tf_op jit(solution)/shard_map/ppermute | solution.py:537
  30.8 10.7 %collective-permute-start.6 = (bf16[4,160,384]{2,1,0:T(8,128)(2,1)S(1)}, bf16[4,160,384]{2,1,0:T(8,128)(2,1)S(1)}, u32[]{:S(2)}, u32[]{:S(2)}) collective-permute-start(bf16[4,160,384]{2,1,0:T(8,128)(2,1)S(1)} %pad_maximum_fusion.2), channel_id=1, source_target_pairs={{0,4},{1,3},{2,6},{3,1},{4,0},{5,7},{6,2},{7,5},{8,12},{9,11},{10,... | collective-permute-start | bytes 1474568 | tf_op jit(solution)/shard_map/ppermute | solution.py:537
  32.5 9.0 %collective-permute-start.8 = (bf16[240,384]{1,0:T(8,128)(2,1)S(1)}, bf16[240,384]{1,0:T(8,128)(2,1)S(1)}, u32[]{:S(2)}, u32[]{:S(2)}) collective-permute-start(bf16[240,384]{1,0:T(8,128)(2,1)S(1)} %copy-done.34), channel_id=1, source_target_pairs={{0,24},{1,25},{2,26},{3,27},{4,28},{5,29},{6,30},{7,31},{8,0},{9,1... | collective-permute-start | bytes 552968 | tf_op jit(solution)/shard_map/ppermute | solution.py:537
  32.5 8.9 %collective-permute-start.7 = (bf16[240,384]{1,0:T(8,128)(2,1)S(1)}, bf16[240,384]{1,0:T(8,128)(2,1)S(1)}, u32[]{:S(2)}, u32[]{:S(2)}) collective-permute-start(bf16[240,384]{1,0:T(8,128)(2,1)S(1)} %copy-done.34), channel_id=1, source_target_pairs={{0,8},{1,9},{2,10},{3,11},{4,12},{5,13},{6,14},{7,15},{8,16},{9,17... | collective-permute-start | bytes 552968 | tf_op jit(solution)/shard_map/ppermute | solution.py:537
  41.5 21.4 %copy-start.15 = (s32[144]{0:T(256)S(1)}, s32[144]{0:T(256)}, u32[]{:S(2)}) copy-start(s32[144]{0:T(256)} %concatenate.20.place) | copy-start | bytes 1732
  41.5 18.8 %collective-permute-start.9 = (bf16[8,160,384]{2,1,0:T(8,128)(2,1)S(1)}, bf16[8,160,384]{2,1,0:T(8,128)(2,1)S(1)}, u32[]{:S(2)}, u32[]{:S(2)}) collective-permute-start(bf16[8,160,384]{2,1,0:T(8,128)(2,1)S(1)} %constant_dynamic-update-slice_fusion.own0), channel_id=1, source_target_pairs={{0,2},{1,5},{2,0},{3,7},{4,6},{5,1},{6,4},{7,3},{8,10},{9,13},{10,... | collective-permute-start | bytes 2949128 | tf_op jit(solution)/shard_map/ppermute | solution.py:537
  42.1 16.3 %collective-permute-start.11 = (bf16[4,192,384]{2,1,0:T(8,128)(2,1)S(1)}, bf16[4,192,384]{2,1,0:T(8,128)(2,1)S(1)}, u32[]{:S(2)}, u32[]{:S(2)}) collective-permute-start(bf16[4,192,384]{2,1,0:T(8,128)(2,1)S(1)} %pad_maximum_fusion.1), channel_id=1, source_target_pairs={{0,8},{1,9},{2,10},{3,11},{4,12},{5,13},{6,14},{7,15},{8,16},{9,17... | collective-permute-start | bytes 1769480 | tf_op jit(solution)/shard_map/ppermute | solution.py:537
  42.1 18.2 %collective-permute-start.10 = (bf16[240,384]{1,0:T(8,128)(2,1)S(1)}, bf16[240,384]{1,0:T(8,128)(2,1)S(1)}, u32[]{:S(2)}, u32[]{:S(2)}) collective-permute-start(bf16[240,384]{1,0:T(8,128)(2,1)S(1)} %collective-permute-done.7), channel_id=1, source_target_pairs={{0,8},{1,9},{2,10},{3,11},{4,12},{5,13},{6,14},{7,15},{8,16},{9,17... | collective-permute-start | bytes 552968 | tf_op jit(solution)/shard_map/ppermute | solution.py:537
  43.4 19.0 %collective-permute-start.12 = (bf16[8,160,384]{2,1,0:T(8,128)(2,1)S(1)}, bf16[8,160,384]{2,1,0:T(8,128)(2,1)S(1)}, u32[]{:S(2)}, u32[]{:S(2)}) collective-permute-start(bf16[8,160,384]{2,1,0:T(8,128)(2,1)S(1)} %constant_dynamic-update-slice_fusion.own0), channel_id=1, source_target_pairs={{0,1},{1,0},{2,3},{3,2},{4,5},{5,4},{6,7},{7,6},{8,9},{9,8},{10,11... | collective-permute-start | bytes 2949128 | tf_op jit(solution)/shard_map/ppermute | solution.py:537
  60.3 2.6 %collective-permute-start.13 = (bf16[8,160,384]{2,1,0:T(8,128)(2,1)S(1)}, bf16[8,160,384]{2,1,0:T(8,128)(2,1)S(1)}, u32[]{:S(2)}, u32[]{:S(2)}) collective-permute-start(bf16[8,160,384]{2,1,0:T(8,128)(2,1)S(1)} %collective-permute-done.9.own1), channel_id=1, source_target_pairs={{0,1},{1,0},{2,3},{3,2},{4,5},{5,4},{6,7},{7,6},{8,9},{9,8},{10,11... | collective-permute-start | bytes 2949128 | tf_op jit(solution)/shard_map/ppermute | solution.py:537
  60.4 15.9 %collective-permute-start.15 = (bf16[4,240,384]{2,1,0:T(8,128)(2,1)S(1)}, bf16[4,240,384]{2,1,0:T(8,128)(2,1)S(1)}, u32[]{:S(2)}, u32[]{:S(2)}) collective-permute-start(bf16[4,240,384]{2,1,0:T(8,128)(2,1)S(1)} %pad_maximum_fusion), channel_id=1, source_target_pairs={{0,4},{1,3},{2,6},{3,1},{4,0},{5,7},{6,2},{7,5},{8,12},{9,11},{10,... | collective-permute-start | bytes 2211848 | tf_op jit(solution)/shard_map/ppermute | solution.py:537
  62.2 14.1 %collective-permute-start.14 = (bf16[4,192,384]{2,1,0:T(8,128)(2,1)S(1)}, bf16[4,192,384]{2,1,0:T(8,128)(2,1)S(1)}, u32[]{:S(2)}, u32[]{:S(2)}) collective-permute-start(bf16[4,192,384]{2,1,0:T(8,128)(2,1)S(1)} %pad_maximum_fusion.1), channel_id=1, source_target_pairs={{0,24},{1,25},{2,26},{3,27},{4,28},{5,29},{6,30},{7,31},{8,0},{9,1... | collective-permute-start | bytes 1769480 | tf_op jit(solution)/shard_map/ppermute | solution.py:537
  76.6 19.6 %copy-start.19 = (bf16[8,240,384]{2,1,0:T(8,128)(2,1)}, bf16[8,240,384]{2,1,0:T(8,128)(2,1)S(1)}, u32[]{:S(2)}) copy-start(bf16[8,240,384]{2,1,0:T(8,128)(2,1)S(1)} %constant_dynamic-update-slice_fusion.7.b0) | copy-start | bytes 4423684
  76.6 19.5 %collective-permute-start.18 = (bf16[8,240,384]{2,1,0:T(8,128)(2,1)S(1)}, bf16[8,240,384]{2,1,0:T(8,128)(2,1)S(1)}, u32[]{:S(2)}, u32[]{:S(2)}) collective-permute-start(bf16[8,240,384]{2,1,0:T(8,128)(2,1)S(1)} %constant_dynamic-update-slice_fusion.7.b0), channel_id=1, source_target_pairs={{0,2},{1,5},{2,0},{3,7},{4,6},{5,1},{6,4},{7,3},{8,10},{9,13},{10,... | collective-permute-start | bytes 4423688 | tf_op jit(solution)/shard_map/ppermute | solution.py:537
  78.5 6.6 %copy-start.21 = (bf16[8,192,384]{2,1,0:T(8,128)(2,1)}, bf16[8,192,384]{2,1,0:T(8,128)(2,1)S(1)}, u32[]{:S(2)}) copy-start(bf16[8,192,384]{2,1,0:T(8,128)(2,1)S(1)} %constant_dynamic-update-slice_fusion.5.a0) | copy-start | bytes 3538948
  78.5 17.6 %collective-permute-start.17 = (bf16[8,192,384]{2,1,0:T(8,128)(2,1)S(1)}, bf16[8,192,384]{2,1,0:T(8,128)(2,1)S(1)}, u32[]{:S(2)}, u32[]{:S(2)}) collective-permute-start(bf16[8,192,384]{2,1,0:T(8,128)(2,1)S(1)} %constant_dynamic-update-slice_fusion.5.a0), channel_id=1, source_target_pairs={{0,1},{1,0},{2,3},{3,2},{4,5},{5,4},{6,7},{7,6},{8,9},{9,8},{10,11... | collective-permute-start | bytes 3538952 | tf_op jit(solution)/shard_map/ppermute | solution.py:537
  78.6 17.5 %collective-permute-start.16 = (bf16[4,192,384]{2,1,0:T(8,128)(2,1)S(1)}, bf16[4,192,384]{2,1,0:T(8,128)(2,1)S(1)}, u32[]{:S(2)}, u32[]{:S(2)}) collective-permute-start(bf16[4,192,384]{2,1,0:T(8,128)(2,1)S(1)} %collective-permute-done.11), channel_id=1, source_target_pairs={{0,8},{1,9},{2,10},{3,11},{4,12},{5,13},{6,14},{7,15},{8,16},{9,17... | collective-permute-start | bytes 1769480 | tf_op jit(solution)/shard_map/ppermute | solution.py:537
  85.1 11.8 %copy-start.5 = (bf16[640,768]{1,0:T(8,128)(2,1)}, bf16[640,768]{1,0:T(8,128)(2,1)S(1)}, u32[]{:S(2)}) copy-start(bf16[640,768]{1,0:T(8,128)(2,1)S(1)} %attention.1.att_far.att_ref) | copy-start | bytes 2949124
  96.1 7.1 %copy-start.24 = (bf16[8,240,384]{2,1,0:T(8,128)(2,1)}, bf16[8,240,384]{2,1,0:T(8,128)(2,1)S(1)}, u32[]{:S(2)}) copy-start(bf16[8,240,384]{2,1,0:T(8,128)(2,1)S(1)} %collective-permute-done.18.b1) | copy-start | bytes 4423684
  96.2 7.1 %collective-permute-start.20 = (bf16[8,240,384]{2,1,0:T(8,128)(2,1)S(1)}, bf16[8,240,384]{2,1,0:T(8,128)(2,1)S(1)}, u32[]{:S(2)}, u32[]{:S(2)}) collective-permute-start(bf16[8,240,384]{2,1,0:T(8,128)(2,1)S(1)} %constant_dynamic-update-slice_fusion.7.b0), channel_id=1, source_target_pairs={{0,1},{1,0},{2,3},{3,2},{4,5},{5,4},{6,7},{7,6},{8,9},{9,8},{10,11... | collective-permute-start | bytes 4423688 | tf_op jit(solution)/shard_map/ppermute | solution.py:537
  96.2 7.1 %collective-permute-start.21 = (bf16[8,240,384]{2,1,0:T(8,128)(2,1)S(1)}, bf16[8,240,384]{2,1,0:T(8,128)(2,1)S(1)}, u32[]{:S(2)}, u32[]{:S(2)}) collective-permute-start(bf16[8,240,384]{2,1,0:T(8,128)(2,1)S(1)} %collective-permute-done.18.b1), channel_id=1, source_target_pairs={{0,1},{1,0},{2,3},{3,2},{4,5},{5,4},{6,7},{7,6},{8,9},{9,8},{10,11... | collective-permute-start | bytes 4423688 | tf_op jit(solution)/shard_map/ppermute | solution.py:537
  97.2 8.4 %copy-start.20 = (bf16[8,192,384]{2,1,0:T(8,128)(2,1)}, bf16[8,192,384]{2,1,0:T(8,128)(2,1)S(1)}, u32[]{:S(2)}) copy-start(bf16[8,192,384]{2,1,0:T(8,128)(2,1)S(1)} %constant_dynamic-update-slice_fusion.9.a1) | copy-start | bytes 3538948
  97.2 6.1 %collective-permute-start.19 = (bf16[8,192,384]{2,1,0:T(8,128)(2,1)S(1)}, bf16[8,192,384]{2,1,0:T(8,128)(2,1)S(1)}, u32[]{:S(2)}, u32[]{:S(2)}) collective-permute-start(bf16[8,192,384]{2,1,0:T(8,128)(2,1)S(1)} %constant_dynamic-update-slice_fusion.9.a1), channel_id=1, source_target_pairs={{0,1},{1,0},{2,3},{3,2},{4,5},{5,4},{6,7},{7,6},{8,9},{9,8},{10,11... | collective-permute-start | bytes 3538952 | tf_op jit(solution)/shard_map/ppermute | solution.py:537
  140.1 3.1 %collective-permute-start.22 = (bf16[8,96,768]{2,1,0:T(8,128)(2,1)}, bf16[8,96,768]{2,1,0:T(8,128)(2,1)S(1)}, u32[]{:S(2)}, u32[]{:S(2)}) collective-permute-start(bf16[8,96,768]{2,1,0:T(8,128)(2,1)} %get-tuple-element.201), channel_id=1, source_target_pairs={{0,1},{1,0},{2,3},{3,2},{4,5},{5,4},{6,7},{7,6},{8,9},{9,8},{10,11... | collective-permute-start | bytes 3538952 | tf_op jit(solution)/shard_map/ppermute | solution.py:537
  144.9 8.6 %collective-permute-start.23 = (bf16[16,24,3072]{2,1,0:T(8,128)(2,1)}, bf16[16,24,3072]{2,1,0:T(8,128)(2,1)S(1)}, u32[]{:S(2)}, u32[]{:S(2)}) collective-permute-start(bf16[16,24,3072]{2,1,0:T(8,128)(2,1)} %get-tuple-element.202), channel_id=1, source_target_pairs={{0,1},{1,0},{2,3},{3,2},{4,5},{5,4},{6,7},{7,6},{8,9},{9,8},{10,11... | collective-permute-start | bytes 7077896 | tf_op jit(solution)/shard_map/ppermute | solution.py:537
  145.2 17.2 %collective-permute-start.27 = (bf16[8,96,768]{2,1,0:T(8,128)(2,1)S(1)}, bf16[8,96,768]{2,1,0:T(8,128)(2,1)S(1)}, u32[]{:S(2)}, u32[]{:S(2)}) collective-permute-start(bf16[8,96,768]{2,1,0:T(8,128)(2,1)S(1)} %add_convert_fusion.1), channel_id=1, source_target_pairs={{0,2},{1,5},{2,0},{3,7},{4,6},{5,1},{6,4},{7,3},{8,10},{9,13},{10,... | collective-permute-start | bytes 3538952 | tf_op jit(solution)/shard_map/ppermute | solution.py:537
  146.6 15.7 %collective-permute-start.26 = (bf16[8,96,768]{2,1,0:T(8,128)(2,1)}, bf16[8,96,768]{2,1,0:T(8,128)(2,1)S(1)}, u32[]{:S(2)}, u32[]{:S(2)}) collective-permute-start(bf16[8,96,768]{2,1,0:T(8,128)(2,1)} %get-tuple-element.214), channel_id=1, source_target_pairs={{0,1},{1,0},{2,3},{3,2},{4,5},{5,4},{6,7},{7,6},{8,9},{9,8},{10,11... | collective-permute-start | bytes 3538952 | tf_op jit(solution)/shard_map/ppermute | solution.py:537
  146.8 6.8 %copy-start.4 = (bf16[2,768,1152]{2,1,0:T(8,128)(2,1)S(1)}, bf16[2,768,1152]{2,1,0:T(8,128)(2,1)}, u32[]{:S(2)}) copy-start(bf16[2,768,1152]{2,1,0:T(8,128)(2,1)} %copy-done.3) | copy-start | bytes 10616836
  146.8 6.8 %copy-start.6 = (bf16[640,768]{1,0:T(8,128)(2,1)S(1)}, bf16[640,768]{1,0:T(8,128)(2,1)}, u32[]{:S(2)}) copy-start(bf16[640,768]{1,0:T(8,128)(2,1)} %copy-done.5) | copy-start | bytes 2949124
  146.8 6.8 %copy-start.10 = (bf16[768,640]{1,0:T(8,128)(2,1)S(1)}, bf16[768,640]{1,0:T(8,128)(2,1)}, u32[]{:S(2)}) copy-start(bf16[768,640]{1,0:T(8,128)(2,1)} %copy-done.9) | copy-start | bytes 2949124
  146.8 6.8 %copy-start.16 = (s32[144]{0:T(256)S(1)}, s32[144]{0:T(256)}, u32[]{:S(2)}) copy-start(s32[144]{0:T(256)} %concatenate.20.place) | copy-start | bytes 1732
  153.6 7.7 %copy-start.22 = (bf16[16,24,3072]{2,1,0:T(8,128)(2,1)S(1)}, bf16[16,24,3072]{2,1,0:T(8,128)(2,1)}, u32[]{:S(2)}) copy-start(bf16[16,24,3072]{2,1,0:T(8,128)(2,1)} %get-tuple-element.298) | copy-start | bytes 7077892
  160.9 8.5 %collective-permute-start.25 = (bf16[16,24,1920]{2,1,0:T(8,128)(2,1)S(1)}, bf16[16,24,1920]{2,1,0:T(8,128)(2,1)S(1)}, u32[]{:S(2)}, u32[]{:S(2)}) collective-permute-start(bf16[16,24,1920]{2,1,0:T(8,128)(2,1)S(1)} %get-tuple-element.213), channel_id=1, source_target_pairs={{0,1},{1,0},{2,3},{3,2},{4,5},{5,4},{6,7},{7,6},{8,9},{9,8},{10,11... | collective-permute-start | bytes 4423688 | tf_op jit(solution)/shard_map/ppermute | solution.py:537
  161.7 16.5 %collective-permute-start.24 = (bf16[8,24,3072]{2,1,0:T(8,128)(2,1)S(1)}, bf16[8,24,3072]{2,1,0:T(8,128)(2,1)S(1)}, u32[]{:S(2)}, u32[]{:S(2)}) collective-permute-start(bf16[8,24,3072]{2,1,0:T(8,128)(2,1)S(1)} %add_convert_fusion), channel_id=1, source_target_pairs={{0,2},{1,5},{2,0},{3,7},{4,6},{5,1},{6,4},{7,3},{8,10},{9,13},{10,... | collective-permute-start | bytes 3538952 | tf_op jit(solution)/shard_map/ppermute | solution.py:537
  162.8 6.7 %copy-start.2 = (bf16[4,160,768]{2,1,0:T(8,128)(2,1)S(1)}, bf16[4,160,768]{2,1,0:T(8,128)(2,1)}, u32[]{:S(2)}) copy-start(bf16[4,160,768]{2,1,0:T(8,128)(2,1)} %copy-done.1) | copy-start | bytes 2949124
  162.8 6.7 %copy-start.13 = (f32[2,16,384]{2,1,0:T(8,128)S(1)}, f32[2,16,384]{2,1,0:T(8,128)}, u32[]{:S(2)}) copy-start(f32[2,16,384]{2,1,0:T(8,128)} %copy-done.12) | copy-start | bytes 147460
  162.8 6.7 %copy-start.14 = (f32[4,8,768]{2,1,0:T(8,128)S(1)}, f32[4,8,768]{2,1,0:T(8,128)}, u32[]{:S(2)}) copy-start(f32[4,8,768]{2,1,0:T(8,128)} %get-tuple-element.224.fcg_ref) | copy-start | bytes 294916
  162.8 6.7 %copy-start.17 = (f32[8,768]{1,0:T(8,128)S(1)}, f32[8,768]{1,0:T(8,128)}, u32[]{:S(2)}) copy-start(f32[8,768]{1,0:T(8,128)} %get-tuple-element.223.mlp_ref) | copy-start | bytes 73732
  162.8 20.5 %collective-permute-start.30 = (bf16[4,96,768]{2,1,0:T(8,128)(2,1)S(1)}, bf16[4,96,768]{2,1,0:T(8,128)(2,1)S(1)}, u32[]{:S(2)}, u32[]{:S(2)}) collective-permute-start(bf16[4,96,768]{2,1,0:T(8,128)(2,1)S(1)} %add_convert_fusion.5), channel_id=1, source_target_pairs={{0,8},{1,9},{2,10},{3,11},{4,12},{5,13},{6,14},{7,15},{8,0},{9,1},... | collective-permute-start | bytes 1769480 | tf_op jit(solution)/shard_map/ppermute | solution.py:537
  178.2 4.1 %collective-permute-start.31 = (bf16[8,32,1152]{2,1,0:T(8,128)(2,1)S(1)}, bf16[8,32,1152]{2,1,0:T(8,128)(2,1)S(1)}, u32[]{:S(2)}, u32[]{:S(2)}) collective-permute-start(bf16[8,32,1152]{2,1,0:T(8,128)(2,1)S(1)} %get-tuple-element.233), channel_id=1, source_target_pairs={{0,1},{1,0},{2,3},{3,2},{4,5},{5,4},{6,7},{7,6},{8,9},{9,8},{10,11... | collective-permute-start | bytes 1769480 | tf_op jit(solution)/shard_map/ppermute | solution.py:537
  178.9 25.4 %collective-permute-start.28 = (bf16[4,24,3072]{2,1,0:T(8,128)(2,1)S(1)}, bf16[4,24,3072]{2,1,0:T(8,128)(2,1)S(1)}, u32[]{:S(2)}, u32[]{:S(2)}) collective-permute-start(bf16[4,24,3072]{2,1,0:T(8,128)(2,1)S(1)} %add_convert_fusion.4), channel_id=1, source_target_pairs={{0,8},{1,9},{2,10},{3,11},{4,12},{5,13},{6,14},{7,15},{8,0},{9,1},... | collective-permute-start | bytes 1769480 | tf_op jit(solution)/shard_map/ppermute | solution.py:537
  180.7 19.8 %collective-permute-start.32 = (bf16[8,32,1152]{2,1,0:T(8,128)(2,1)S(1)}, bf16[8,32,1152]{2,1,0:T(8,128)(2,1)S(1)}, u32[]{:S(2)}, u32[]{:S(2)}) collective-permute-start(bf16[8,32,1152]{2,1,0:T(8,128)(2,1)S(1)} %get-tuple-element.243), channel_id=1, source_target_pairs={{0,1},{1,0},{2,3},{3,2},{4,5},{5,4},{6,7},{7,6},{8,9},{9,8},{10,11... | collective-permute-start | bytes 1769480 | tf_op jit(solution)/shard_map/ppermute | solution.py:537
  181.0 14.7 %collective-permute-start.29 = (bf16[8,24,1920]{2,1,0:T(8,128)(2,1)S(1)}, bf16[8,24,1920]{2,1,0:T(8,128)(2,1)S(1)}, u32[]{:S(2)}, u32[]{:S(2)}) collective-permute-start(bf16[8,24,1920]{2,1,0:T(8,128)(2,1)S(1)} %add_convert_fusion.2), channel_id=1, source_target_pairs={{0,2},{1,5},{2,0},{3,7},{4,6},{5,1},{6,4},{7,3},{8,10},{9,13},{10,... | collective-permute-start | bytes 2211848 | tf_op jit(solution)/shard_map/ppermute | solution.py:537
  182.5 13.3 %copy-start.29 = (bf16[640,768]{1,0:T(8,128)(2,1)S(1)}, bf16[640,768]{1,0:T(8,128)(2,1)}, u32[]{:S(2)}) copy-start(bf16[640,768]{1,0:T(8,128)(2,1)} %get-tuple-element.240) | copy-start | bytes 2949124
  182.5 20.2 %collective-permute-start.33 = (bf16[8,32,1152]{2,1,0:T(8,128)(2,1)S(1)}, bf16[8,32,1152]{2,1,0:T(8,128)(2,1)S(1)}, u32[]{:S(2)}, u32[]{:S(2)}) collective-permute-start(bf16[8,32,1152]{2,1,0:T(8,128)(2,1)S(1)} %add_convert_fusion.3), channel_id=1, source_target_pairs={{0,2},{1,5},{2,0},{3,7},{4,6},{5,1},{6,4},{7,3},{8,10},{9,13},{10,... | collective-permute-start | bytes 1769480 | tf_op jit(solution)/shard_map/ppermute | solution.py:537
  183.5 21.6 %collective-permute-start.35 = (bf16[2,96,768]{2,1,0:T(8,128)(2,1)S(1)}, bf16[2,96,768]{2,1,0:T(8,128)(2,1)S(1)}, u32[]{:S(2)}, u32[]{:S(2)}) collective-permute-start(bf16[2,96,768]{2,1,0:T(8,128)(2,1)S(1)} %add_convert_fusion.9), channel_id=1, source_target_pairs={{0,4},{1,3},{2,6},{3,1},{4,0},{5,7},{6,2},{7,5},{8,12},{9,11},{10,... | collective-permute-start | bytes 884744 | tf_op jit(solution)/shard_map/ppermute | solution.py:537
  199.2 7.5 %collective-permute-start.34 = (bf16[4,24,1920]{2,1,0:T(8,128)(2,1)S(1)}, bf16[4,24,1920]{2,1,0:T(8,128)(2,1)S(1)}, u32[]{:S(2)}, u32[]{:S(2)}) collective-permute-start(bf16[4,24,1920]{2,1,0:T(8,128)(2,1)S(1)} %add_convert_fusion.6), channel_id=1, source_target_pairs={{0,4},{1,3},{2,6},{3,1},{4,0},{5,7},{6,2},{7,5},{8,12},{9,11},{10,... | collective-permute-start | bytes 1105928 | tf_op jit(solution)/shard_map/ppermute | solution.py:537
  202.8 7.0 %collective-permute-start.38 = (bf16[4,32,1152]{2,1,0:T(8,128)(2,1)S(1)}, bf16[4,32,1152]{2,1,0:T(8,128)(2,1)S(1)}, u32[]{:S(2)}, u32[]{:S(2)}) collective-permute-start(bf16[4,32,1152]{2,1,0:T(8,128)(2,1)S(1)} %add_convert_fusion.8), channel_id=1, source_target_pairs={{0,4},{1,3},{2,6},{3,1},{4,0},{5,7},{6,2},{7,5},{8,12},{9,11},{10,... | collective-permute-start | bytes 884744 | tf_op jit(solution)/shard_map/ppermute | solution.py:537
  204.4 8.6 %collective-permute-start.37 = (bf16[2,24,3072]{2,1,0:T(8,128)(2,1)S(1)}, bf16[2,24,3072]{2,1,0:T(8,128)(2,1)S(1)}, u32[]{:S(2)}, u32[]{:S(2)}) collective-permute-start(bf16[2,24,3072]{2,1,0:T(8,128)(2,1)S(1)} %add_convert_fusion.7), channel_id=1, source_target_pairs={{0,4},{1,3},{2,6},{3,1},{4,0},{5,7},{6,2},{7,5},{8,12},{9,11},{10,... | collective-permute-start | bytes 884744 | tf_op jit(solution)/shard_map/ppermute | solution.py:537
  205.2 15.5 %collective-permute-start.43 = (bf16[1,96,768]{2,1,0:T(8,128)(2,1)S(1)}, bf16[1,96,768]{2,1,0:T(8,128)(2,1)S(1)}, u32[]{:S(2)}, u32[]{:S(2)}) collective-permute-start(bf16[1,96,768]{2,1,0:T(8,128)(2,1)S(1)} %add_convert_fusion.13), channel_id=1, source_target_pairs={{0,16},{1,17},{2,18},{3,19},{4,20},{5,21},{6,22},{7,23},{8,24},{9,... | collective-permute-start | bytes 442376 | tf_op jit(solution)/shard_map/ppermute | solution.py:537
  206.8 9.2 %collective-permute-start.36 = (bf16[2,24,1920]{2,1,0:T(8,128)(2,1)S(1)}, bf16[2,24,1920]{2,1,0:T(8,128)(2,1)S(1)}, u32[]{:S(2)}, u32[]{:S(2)}) collective-permute-start(bf16[2,24,1920]{2,1,0:T(8,128)(2,1)S(1)} %add_convert_fusion.10), channel_id=1, source_target_pairs={{0,8},{1,9},{2,10},{3,11},{4,12},{5,13},{6,14},{7,15},{8,0},{9,1},... | collective-permute-start | bytes 552968 | tf_op jit(solution)/shard_map/ppermute | solution.py:537
  209.9 10.7 %collective-permute-start.40 = (bf16[2,32,1152]{2,1,0:T(8,128)(2,1)S(1)}, bf16[2,32,1152]{2,1,0:T(8,128)(2,1)S(1)}, u32[]{:S(2)}, u32[]{:S(2)}) collective-permute-start(bf16[2,32,1152]{2,1,0:T(8,128)(2,1)S(1)} %add_convert_fusion.12), channel_id=1, source_target_pairs={{0,8},{1,9},{2,10},{3,11},{4,12},{5,13},{6,14},{7,15},{8,0},{9,1},... | collective-permute-start | bytes 442376 | tf_op jit(solution)/shard_map/ppermute | solution.py:537
  213.1 13.7 %collective-permute-start.42 = (bf16[1,24,3072]{2,1,0:T(8,128)(2,1)S(1)}, bf16[1,24,3072]{2,1,0:T(8,128)(2,1)S(1)}, u32[]{:S(2)}, u32[]{:S(2)}) collective-permute-start(bf16[1,24,3072]{2,1,0:T(8,128)(2,1)S(1)} %add_convert_fusion.11), channel_id=1, source_target_pairs={{0,16},{1,17},{2,18},{3,19},{4,20},{5,21},{6,22},{7,23},{8,24},{9,... | collective-permute-start | bytes 442376 | tf_op jit(solution)/shard_map/ppermute | solution.py:537
  216.0 12.6 %collective-permute-start.39 = (bf16[1,24,1920]{2,1,0:T(8,128)(2,1)S(1)}, bf16[1,24,1920]{2,1,0:T(8,128)(2,1)S(1)}, u32[]{:S(2)}, u32[]{:S(2)}) collective-permute-start(bf16[1,24,1920]{2,1,0:T(8,128)(2,1)S(1)} %add_convert_fusion.14), channel_id=1, source_target_pairs={{0,16},{1,17},{2,18},{3,19},{4,20},{5,21},{6,22},{7,23},{8,24},{9,... | collective-permute-start | bytes 276488 | tf_op jit(solution)/shard_map/ppermute | solution.py:537
  220.7 8.8 %collective-permute-start.41 = (bf16[1,32,1152]{2,1,0:T(8,128)(2,1)S(1)}, bf16[1,32,1152]{2,1,0:T(8,128)(2,1)S(1)}, u32[]{:S(2)}, u32[]{:S(2)}) collective-permute-start(bf16[1,32,1152]{2,1,0:T(8,128)(2,1)S(1)} %add_convert_fusion.15), channel_id=1, source_target_pairs={{0,16},{1,17},{2,18},{3,19},{4,20},{5,21},{6,22},{7,23},{8,24},{9,... | collective-permute-start | bytes 221192 | tf_op jit(solution)/shard_map/ppermute | solution.py:537
  (16 other events, 39.1 us)

commit v4 on v3

--- a/solution.py
+++ b/solution.py
@@ -147,7 +147,7 @@
 
 def qkv_kernel(
     place, own0, own1, other0, other1, rows_ref,
-    vec_ref, fcb_ref, h1_turned, qkv_ref, wq_out,
+    vec_ref, fcb_ref, h1_turned, qkv_ref, wq_out0, wq_out1,
     wq, h1, qvb, small, sems,
 ):
     sources = (own0, own1, other0, other1)
@@ -176,13 +176,17 @@
         h1_turned[...] = low.T
 
     wait_all(wq.at[side], sems.at[side])
-    keeping = pltpu.make_async_copy(wq.at[side], wq_out.at[side], sems.at[3])
-    keeping.start()
+    for half, target in enumerate((wq_out0, wq_out1)):
+
+        @pl.when(side == half)
+        def _(half=half, target=target):
+            pltpu.make_async_copy(wq.at[half], target, sems.at[3]).start()
+
     bias = jnp.concatenate(
         [qvb[side, 6:7, :], jnp.zeros((1, BLOCK), F32), qvb[2 + side, 6:7, :]], axis=1
     )
     qkv_ref[0] = (dot(h1[...], wq[side]) + bias).astype(BF)
-    keeping.wait()
+    wait_all(wq_out0, sems.at[3])
 
 
 def two_heads(pair_rows, low_half):
@@ -228,7 +232,7 @@
         work(target[1], slot)
 
 
-def give_rows(place, tables, total, keep_ref, send_ref, extra=None):
+def give_rows(place, tables, total, keep_ref, send_ref, extra=None, lanes=slice(None)):
     for chip in range(CHIPS):
         below = None if extra is None else extra(chip)
         for which, target in enumerate((keep_ref, send_ref)):
@@ -238,7 +242,7 @@
                 share = jnp.concatenate([share, below], axis=0)
 
             def put(ref, slot, share=share):
-                ref[slot] = share.astype(BF)
+                ref[slot, :, lanes] = share.astype(BF)
 
             at_slot(target, place[tables[which] + chip], put)
 
@@ -417,67 +421,40 @@
 
 
 def qkv_grad_kernel(
-    place, h1_turned, gqkv_ref, wq_ref, att_ref, glow_ref, gh1_ref, sums_ref, keep_ref, send_ref, product
+    place, h1_turned, gqkv_ref, wq_ref, att_ref, glow_ref, gh1_ref, sums_ref, keep_ref, upper_ref, lower_ref,
+    product, product_out,
 ):
-    part = pl.program_id(0)
-
-    @pl.when(part < 3)
-    def _():
-        product[...] = dot(h1_turned[...], gqkv_ref[...])
-        gradient = dot(gqkv_ref[...], wq_ref[0], 1, 1)
-        gh1_ref[...] = jnp.where(part == 0, gradient, gh1_ref[...] + gradient)
-        sums_ref[jnp.minimum(part, 2)] = stack_rows([None, None, sum_rows(gqkv_ref[...])])
-
-    @pl.when(part >= 3)
-    def _():
-        product[...] = dot(att_ref[...], glow_ref[...], 0, 0)
-
-    give_rows(place, SMALL, product, keep_ref, send_ref)
+    third, wide = gqkv_ref.shape[1], glow_ref.shape[1]
+    product[...] = dot(h1_turned[...], gqkv_ref[...])
+    product_out[...] = dot(att_ref[...], glow_ref[...], 0, 0)
+    gh1_ref[...] = dot(gqkv_ref[...], wq_ref[...], 1, 1)
+    sums_ref[...] = sum_rows(gqkv_ref[...])
+    send = upper_ref, lower_ref
+    give_rows(place, SMALL, product, keep_ref, send, lanes=slice(0, third))
+    give_rows(place, SMALL, product_out, keep_ref, send, lanes=slice(third, third + wide))
 
 
 def input_kernel(
-    place, h1_turned, gqkv_ref, wq_ref, before_ref, mlp_ref, fcg_ref, rows_ref, vec_ref, glow_ref, gh1,
-    ginput_ref, keep_ref, upper_ref, lower_ref,
-    product, sums, total, sems_in,
+    place, h1_turned, gqkv_ref, wq_ref, before_ref, mlp_ref, fcg_ref, rows_ref, vec_ref, glow_ref, gh1_ref,
+    ginput_ref, keep_ref, upper_ref, lower_ref, product,
 ):
-    part = pl.program_id(0)
-    load = pltpu.make_async_copy(gh1, total, sems_in)
-
-    @pl.when(part == 0)
-    def _():
-        load.start()
-
     product[...] = dot(h1_turned[...], gqkv_ref[...])
-    gradient = dot(gqkv_ref[...], wq_ref[0], 1, 1)
-
-    @pl.when(part == 0)
-    def _():
-        load.wait()
-
-    total[...] += gradient
-    sums[part] = stack_rows([None, None, sum_rows(gqkv_ref[...])])
-
-    send_ref = upper_ref, lower_ref
-
-    @pl.when(part < 2)
-    def _():
-        give_rows(place, SMALL, product, keep_ref, send_ref, lambda chip: mlp_ref[...] + fcg_ref[chip // 4])
-
-    @pl.when(part == 2)
-    def _():
-        gradient = total[...]
-        normed, scale = normed_rows(rows_ref[...].astype(F32))
-        ginput_ref[...] = (
-            glow_ref[...].astype(F32) + norm_back(gradient * row_of(vec_ref, 0), normed, scale)
-        ).astype(BF)
-        gain, shift = sum_rows(gradient * normed), sum_rows(gradient)
-
-        def below(chip):
-            lanes = slice(BLOCK * (chip // 8), BLOCK * (chip // 8 + 1))
-            biases = (before_ref[0], sums[0], before_ref[2], sums[2])[chip // 4]
-            return stack_rows([gain[:, lanes], shift[:, lanes]]) + biases
-
-        give_rows(place, SMALL, product, keep_ref, send_ref, below)
+    sums = sum_rows(gqkv_ref[...])
+    gradient = gh1_ref[...] + dot(gqkv_ref[...], wq_ref[...], 1, 1)
+    normed, scale = normed_rows(rows_ref[...].astype(F32))
+    ginput_ref[...] = (
+        glow_ref[...].astype(F32) + norm_back(gradient * row_of(vec_ref, 0), normed, scale)
+    ).astype(BF)
+    gain, shift = sum_rows(gradient * normed), sum_rows(gradient)
+    first, last = slice(0, BLOCK), slice(2 * BLOCK, 3 * BLOCK)
+    biases = before_ref[:, first], sums[:, first], before_ref[:, last], sums[:, last]
+
+    def below(chip):
+        lanes = slice(BLOCK * (chip // 8), BLOCK * (chip // 8 + 1))
+        own = stack_rows([gain[:, lanes], shift[:, lanes], biases[chip // 4]])
+        return jnp.concatenate([mlp_ref[...] + fcg_ref[chip // 4], own], axis=1)
+
+    give_rows(place, SMALL, product, keep_ref, (upper_ref, lower_ref), below)
 
 
 def add_up(parts):
@@ -769,16 +746,16 @@
     def join(value, *others):
         return after(value, *others) if by_hand else value
 
-    vec, fcb, h1_turned, qkv, wq = call(
+    vec, fcb, h1_turned, qkv, wq_0, wq_1 = call(
         qkv_kernel,
         (place, *gathered_a, rows_in),
         (
             struct((2, 16, BLOCK), F32), struct((steps, 1, wide), F32), struct((width, rows), BF),
-            struct((2, rows, third), BF), struct((2, width, third), BF),
+            struct((2, rows, third), BF), struct((width, third), BF), struct((width, third), BF),
         ),
         (
             fixed(2, 16, BLOCK), fixed(steps, 1, wide), fixed(width, rows),
-            pl.BlockSpec((1, rows, third), lambda step: (step, 0, 0)), anywhere,
+            pl.BlockSpec((1, rows, third), lambda step: (step, 0, 0)), anywhere, anywhere,
         ),
         [smem] + [anywhere] * 4 + [fixed(rows, width)],
         2 * rows * width * 3 * width,
@@ -876,56 +853,44 @@
         state_1, gqkv_0 = lax.optimization_barrier((state_1, gqkv_0))
         state_1 += (links.move(links.fold(state_1), links.second),)
 
-    step_weight = lambda side: pl.BlockSpec((1, width, BLOCK), lambda step: (side, 0, jnp.minimum(step, 2)))
-    early_rows = pl.BlockSpec((rows, BLOCK), lambda step: (0, jnp.minimum(step, 2)))
-    late_rows = pl.BlockSpec((rows, BLOCK), lambda step: (0, jnp.maximum(step - 3, 0)))
-    gh1, sums_0, keep_a, send_a = call(
+    def grad_call(kernel, operands, out_shape, scratch, name):
+        return pl.pallas_call(
+            kernel,
+            out_shape=out_shape,
+            in_specs=[smem] + [vmem] * (len(operands) - 1),
+            out_specs=(vmem,) * len(out_shape),
+            scratch_shapes=list(scratch),
+            compiler_params=pltpu.CompilerParams(vmem_limit_bytes=28 * MIB),
+            cost_estimate=pl.CostEstimate(flops=1, bytes_accessed=1, transcendentals=0),
+            name=name,
+        )(*operands)
+
+    half_shares = lambda height, columns: (struct((8, height, columns), BF),) * 2
+    gh1, sums_0, keep_a, upper_a, lower_a = grad_call(
         qkv_grad_kernel,
-        (place, h1_turned, gqkv_0, wq, att, glow),
-        (wide_rows, struct((3, 8, BLOCK), F32)) + (shares(24, third + wide),) * 2,
-        (fixed(rows, width), fixed(3, 8, BLOCK)) + (step_shares(24, BLOCK),) * 2,
-        [smem, fixed(width, rows), early_rows, step_weight(0), fixed(rows, width), late_rows],
-        6 * rows * width * width,
-        10,
-        24,
-        grid=(5,),
-        scratch=(buffer((width, BLOCK), F32),),
-        name="qkv_grad",
-    )
-    part_2 = gh1
+        (place, h1_turned, gqkv_0, wq_0, att, glow),
+        (wide_rows, struct((1, third), F32), shares(24, third + wide)) + half_shares(24, third + wide),
+        (buffer((width, third), F32), buffer((width, wide), F32)),
+        "qkv_grad",
+    )
+    parts = gh1
     if by_hand:
-        state_a = keep_a, links.move(send_a, links.cores)
-        state_2, gh1 = lax.optimization_barrier((state_2, gh1))
-        part_2 = links.fold(state_2)
-        state_2 += (links.move(part_2, links.near),)
-
-    gqkv_1 = attention_back(1, join(glow, gh1, part_2))
-    if by_hand:
-        state_a, gqkv_1 = lax.optimization_barrier((state_a, gqkv_1))
-        state_a += (links.move(links.fold(state_a), links.second),)
-
-    half_shares = pl.BlockSpec((8, 32, BLOCK), lambda step: (0, 0, step))
-    mlp_small = pl.BlockSpec((8, BLOCK), lambda step: (0, jnp.minimum(step, 1)))
-    ginput, keep_c, upper_c, lower_c = call(
+        got_a = links.move(upper_a, links.cores)
+        state_2, got_a, gh1 = lax.optimization_barrier((state_2, got_a, gh1))
+        parts = links.fold(state_2), add_up([keep_a[8:], got_a]).astype(BF)
+        state_2 += (links.move(parts[0], links.near),)
+        lower_a = after(lower_a, parts)
+        state_a = keep_a, links.move(lower_a, links.cores), links.move(parts[1], links.second)
+
+    gqkv_1 = attention_back(1, join(glow, gh1, parts))
+    ginput, keep_c, upper_c, lower_c = grad_call(
         input_kernel,
-        (place, h1_turned, gqkv_1, wq, sums_0, sums, fcg, rows_in, vec, glow, gh1),
-        (low_rows, shares(32, third)) + (struct((8, 32, third), BF),) * 2,
-        (fixed(rows, width), step_shares(32, BLOCK)) + (half_shares,) * 2,
-        [
-            smem, fixed(width, rows), step_rows(BLOCK), step_weight(1), fixed(3, 8, BLOCK), mlp_small,
-            pl.BlockSpec((steps, 8, BLOCK), lambda step: (0, 0, jnp.minimum(step, 1))), fixed(rows, width),
-            fixed(2, 16, BLOCK),
-            fixed(rows, width), anywhere,
-        ],
-        6 * rows * width * width,
-        14,
-        30,
-        grid=(3,),
-        scratch=(
-            buffer((width, BLOCK), F32), buffer((3, 8, BLOCK), F32), buffer((rows, width), F32), flag,
-        ),
-        name="input_grad",
-    )
+        (place, h1_turned, gqkv_1, wq_1, sums_0, sums, fcg, rows_in, vec, glow, gh1),
+        (low_rows, shares(32, third)) + half_shares(32, third),
+        (buffer((width, third), F32),),
+        "input_grad",
+    )
+
     def cut(value):
         return value.reshape(images, padded, width)[:, :length]
 
@@ -940,14 +905,13 @@
         keep_c, got_c = after(state_c, part)
         part = add_up([keep_c[8:], got_c]).astype(BF)
         state_c = keep_c, rest_c, move(part, links.second)
-        state_2 = after(state_2, part)
-        part = fold(state_2)
-        state_2 += (move(part, links.first),)
-        state_a, out, ginput = after((state_a, out, ginput), part)
-        part = fold(state_a)
-        state_a += (move(part, links.first),)
+        state_2, state_a, out, ginput = after((state_2, state_a, out, ginput), part)
         out, ginput = cut(out), cut(ginput)
-        part = fold(after(state_c, part))
+        state_2, state_a, out, ginput = after((state_2, state_a, out, ginput))
+        parts = fold(state_2), fold(state_a)
+        state_2 += (move(parts[0], links.first),)
+        state_a += (move(parts[1], links.first),)
+        part = fold(after(state_c, parts))
         state_c += (move(part, links.first),)
         state_1, out, ginput = after((state_1, out, ginput), part)
         part = fold(state_1)
@@ -995,7 +959,7 @@
     both_a, both_c, both_1, both_2 = (
         jnp.stack(pair, axis=1).astype(F32)
         for pair in (
-            (keep_a, send_a),
+            (keep_a, jnp.concatenate([lower_a, upper_a])),
             (keep_c, jnp.concatenate([lower_c, upper_c])),
             (keep_1, send_1),
             (keep_2, jnp.concatenate([lower_2, upper_2])),

time: 231 us -> 223 us (0.965)
  Pallas kernels: 82.3 us -> 76.9 us
  starting transfers between devices: 37.3 us -> 34.7 us
    pallas_call x6 -> x4, Pallas kernels: 42.6 us -> 26.6 us  [call(): pl.pallas_call(kernel, grid=grid, out_shape=out_shape, in_specs=in_specs,...]
    pallas_call x0 -> x2, Pallas kernels: none -> 10.5 us  [grad_call(): pl.pallas_call(kernel, out_shape=out_shape, in_specs=[smem] + [vmem] * (l...]
    ppermute x44 -> x45, starting transfers between devices: 37.3 us -> 34.7 us  [move(): return lax.ppermute(value, AXES, pairs)]
    unnamed x80 -> x84, local copies, waits for them, and re-layouts: 6.08 us -> 5.32 us
    ppermute x44 -> x45, waiting for transfers between devices: 88.5 us -> 89.1 us  [move(): return lax.ppermute(value, AXES, pairs)]
  transfers between devices with their start and end apart: 44 -> 45, of which waited for: 21 -> 24; matrix products, arithmetic and copies ran while one was open for 6% -> 6% of each run, Pallas kernels for 18% -> 17%
where the time goes in v4:
time: 223 us
  waiting for transfers between devices  89.1 us (40%)
  Pallas kernels  76.9 us (34%)
  starting transfers between devices  34.7 us (16%)
  local copies, waits for them, and re-layouts  11 us (5%)
  other arithmetic  9.56 us (4%)
    ppermute x45, waiting for transfers between devices, move(): return lax.ppermute(value, AXES, pairs)  89.1 us
    ppermute x45, starting transfers between devices, move(): return lax.ppermute(value, AXES, pairs)  34.7 us
    pallas_call x1, Pallas kernels, shards(): pl.pallas_call(mlp_kernel, grid_spec=pltpu.PrefetchScalarGridSpec(num_sca...  34.6 us
    pallas_call x4, Pallas kernels, call(): pl.pallas_call(kernel, grid=grid, out_shape=out_shape, in_specs=in_specs,...  26.6 us
    pallas_call x2, Pallas kernels, grad_call(): pl.pallas_call(kernel, out_shape=out_shape, in_specs=[smem] + [vmem] * (l...  10.5 us
    unnamed x84, local copies, waits for them, and re-layouts  5.32 us
  transfers between devices with their start and end apart: 45, of which 24 were waited for; matrix products, arithmetic and copies ran while one was open for 6% of the time, Pallas kernels for 17%

profile of v4, /device:TPU:0, one launch (start us, length us, event | category | flops | bytes accessed | tf_op | source)
XLA Modules:
  0.0 222.9 jit_solution(16403636806910637198)
XLA Ops:
  1.4 1.8 share.1
  3.7 0.7 iota_compare_fusion
  4.4 0.7 fusion.2
  5.1 0.7 copy-done.37
  5.8 2.0 pair.1
  7.7 4.8 %collective-permute-start.2 = (bf16[160,384]{1,0:T(8,128)(2,1)}, bf16[160,384]{1,0:T(8,128)(2,1)S(1)}, u32[]{:S(2)}, u32[]{:S(2)}) collective-permute-start(bf16[160,384]{1,0:T(8,128)(2,1)} %get-tuple-element.173), channel_id=1, source_target_pairs={{0,24},{1,25},{2,26},{3,27},{4,28},{5,29},{6,30},{7,31},{8,0},{9,1... | collective-permute-start | bytes 368648 | tf_op jit(solution)/shard_map/ppermute | solution.py:514
  12.5 1.5 collective-permute-start.3
  14.0 1.5 fusion
  15.6 0.9 collective-permute-done.2
  16.5 3.3 %collective-permute-done.1 = bf16[160,384]{1,0:T(8,128)(2,1)S(1)} collective-permute-done((bf16[160,384]{1,0:T(8,128)(2,1)}, bf16[160,384]{1,0:T(8,128)(2,1)S(1)}, u32[]{:S(2)}, u32[]{:S(2)}) %collective-permute-start.1) | collective-permute-done | bytes 122912 | tf_op jit(solution)/shard_map/ppermute | solution.py:514
  19.8 1.6 collective-permute-start.5
  21.4 0.7 pad_select_fusion
  22.2 1.1 copy.32
  23.9 1.2 collective-permute-start.4
  25.1 5.5 %collective-permute-done.4 = bf16[160,384]{1,0:T(8,128)(2,1)S(1)} collective-permute-done((bf16[160,384]{1,0:T(8,128)(2,1)S(1)}, bf16[160,384]{1,0:T(8,128)(2,1)S(1)}, u32[]{:S(2)}, u32[]{:S(2)}) %collective-permute-start.4) | collective-permute-done | bytes 122912 | tf_op jit(solution)/shard_map/ppermute | solution.py:514
  30.7 1.6 collective-permute-start.6
  32.5 2.0 collective-permute-start.7
  34.5 6.8 %collective-permute-done.8 = bf16[240,384]{1,0:T(8,128)(2,1)S(1)} collective-permute-done((bf16[240,384]{1,0:T(8,128)(2,1)S(1)}, bf16[240,384]{1,0:T(8,128)(2,1)S(1)}, u32[]{:S(2)}, u32[]{:S(2)}) %collective-permute-start.8) | collective-permute-done | bytes 184352 | tf_op jit(solution)/shard_map/ppermute | solution.py:514
  42.1 1.2 collective-permute-start.10
  43.3 15.0 %collective-permute-done.11 = bf16[4,192,384]{2,1,0:T(8,128)(2,1)S(1)} collective-permute-done((bf16[4,192,384]{2,1,0:T(8,128)(2,1)S(1)}, bf16[4,192,384]{2,1,0:T(8,128)(2,1)S(1)}, u32[]{:S(2)}, u32[]{:S(2)}) %collective-permute-start.11) | collective-permute-done | bytes 589856 | tf_op jit(solution)/shard_map/ppermute | solution.py:514
  58.3 2.0 collective-permute-done.10
  60.4 1.8 collective-permute-start.15
  62.8 7.1 %qkv.1 = (f32[2,16,384]{2,1,0:T(8,128)S(1)}, f32[4,1,768]{2,1,0:T(1,128)S(1)}, bf16[768,640]{1,0:T(8,128)(2,1)S(1)}, bf16[2,640,1152]{2,1,0:T(8,128)(2,1)S(1)}, ...) custom-call(s32[144]{0:T(256)S(1)} %copy-done.17, ...), custom_call_target="tpu_custom_call" | custom-call | flops 1 | bytes 1 | tf_op jit(solution)/shard_map/qkv/pallas_call | solution.py:721
  69.9 1.2 copy-done.12
  71.1 5.1 %collective-permute-done.14 = bf16[4,192,384]{2,1,0:T(8,128)(2,1)S(1)} collective-permute-done((bf16[4,192,384]{2,1,0:T(8,128)(2,1)S(1)}, bf16[4,192,384]{2,1,0:T(8,128)(2,1)S(1)}, u32[]{:S(2)}, u32[]{:S(2)}) %collective-permute-start.14) | collective-permute-done | bytes 589856 | tf_op jit(solution)/shard_map/ppermute | solution.py:514
  76.5 1.7 collective-permute-start.18
  78.8 6.3 %attention.1.att_far.att_ref = bf16[640,768]{1,0:T(8,128)(2,1)S(1)} custom-call(bf16[2,640,1152]{2,1,0:T(8,128)(2,1)S(1)} %get-tuple-element.190.qkv_ref.refs_1_, f32[4,160,160]{2,1,0:T(8,128)S(1)} %copy-done.9), custom_call_target="tpu_custom_call" | custom-call | flops 1 | bytes 1 | tf_op jit(solution)/shard_map/attention/pallas_call | solution.py:721
  85.1 11.0 %collective-permute-done.16 = bf16[4,192,384]{2,1,0:T(8,128)(2,1)S(1)} collective-permute-done((bf16[4,192,384]{2,1,0:T(8,128)(2,1)S(1)}, bf16[4,192,384]{2,1,0:T(8,128)(2,1)S(1)}, u32[]{:S(2)}, u32[]{:S(2)}) %collective-permute-start.16) | collective-permute-done | bytes 589856 | tf_op jit(solution)/shard_map/ppermute | solution.py:514
  97.1 6.1 %collective-permute-done.19.a3 = bf16[8,192,384]{2,1,0:T(8,128)(2,1)S(1)} collective-permute-done((bf16[8,192,384]{2,1,0:T(8,128)(2,1)S(1)}, bf16[8,192,384]{2,1,0:T(8,128)(2,1)S(1)}, u32[]{:S(2)}, u32[]{:S(2)}) %collective-permute-start.19) | collective-permute-done | bytes 1179680 | tf_op jit(solution)/shard_map/ppermute | solution.py:514
  103.3 1.1 copy-done.27
  104.7 0.8 copy-done.28
  105.5 34.6 %mlp.1 = (bf16[640,768]{1,0:T(8,128)(2,1)}, bf16[640,768]{1,0:T(8,128)(2,1)}, bf16[16,24,3072]{2,1,0:T(8,128)(2,1)}, bf16[16,24,3072]{2,1,0:T(8,128)(2,1)}, f32[...) custom-call(s32[144]{0:T(256)} %concatenate.20.place, ...), custom_call_target="tpu_custom_call" | custom-call | flops 1 | bytes 1 | tf_op jit(solution)/shard_map/mlp/pallas_call | solution.py:797
  140.3 3.0 %collective-permute-done.22 = bf16[8,96,768]{2,1,0:T(8,128)(2,1)S(1)} collective-permute-done((bf16[8,96,768]{2,1,0:T(8,128)(2,1)}, bf16[8,96,768]{2,1,0:T(8,128)(2,1)S(1)}, u32[]{:S(2)}, u32[]{:S(2)}) %collective-permute-start.22) | collective-permute-done | bytes 1179680 | tf_op jit(solution)/shard_map/ppermute | solution.py:514
  143.3 1.7 add_convert_fusion.1
  145.6 1.5 collective-permute-start.26
  147.1 6.7 %attention_back.2.gqkv_ref = bf16[640,1152]{1,0:T(8,128)(2,1)S(1)} custom-call(bf16[2,768,384]{2,1,0:T(8,128)(2,1)S(1)} %copy-done.6, bf16[2,640,1152]{2,1,0:T(8,128)(2,1)S(1)} %get-tuple-element.190.qkv_ref.refs_1_, f32[4,160,160]{2,1,0:T(8,128)S(1)} %copy-done.5, bf16[640,768]{1,0:T(8,128)(2,1)S(1)} %copy-done), custom_call_target="tpu_custom_call" | custom-call | flops 1 | bytes 1 | tf_op jit(solution)/shard_map/attention_back/pallas_call | solution.py:721
  153.9 5.3 %qkv_grad.1 = (f32[640,768]{1,0:T(8,128)S(1)}, f32[1,1152]{1,0:T(1,128)S(1)}, bf16[16,24,1920]{2,1,0:T(8,128)(2,1)S(1)}, bf16[8,24,1920]{2,1,0:T(8,128)(2,1)S(1)}, bf16[8,24,1920]{2,1,0:T(8,128)(2,1)S(1)}) custom-call(s32[144]{0:T(256)S(1)} %copy-done.18, bf16[768,640]{1,0:T(8,128)(2,1)S(1)} %copy-done.8, bf16[640,1152]{1,0:T(8,128)(2,1)S(1)} %attention_back.2.gqkv_ref, ...), custom_call_target="tpu_custom_call" | custom-call | flops 1 | bytes 1 | tf_op jit(solution)/shard_map/qkv_grad/pallas_call | solution.py:857
  160.3 1.4 collective-permute-done.26
  162.3 1.6 collective-permute-start.31
  163.9 6.5 %attention_back.3.gqkv_ref = bf16[640,1152]{1,0:T(8,128)(2,1)S(1)} custom-call(bf16[2,768,384]{2,1,0:T(8,128)(2,1)S(1)} %copy-done.6, bf16[2,640,1152]{2,1,0:T(8,128)(2,1)S(1)} %get-tuple-element.190.qkv_ref.refs_1_, f32[4,160,160]{2,1,0:T(8,128)S(1)} %copy-done.5, bf16[640,768]{1,0:T(8,128)(2,1)S(1)} %copy-done), custom_call_target="tpu_custom_call" | custom-call | flops 1 | bytes 1 | tf_op jit(solution)/shard_map/attention_back/pallas_call | solution.py:721
  170.4 5.2 %input_grad.1 = (bf16[640,768]{1,0:T(8,128)(2,1)S(1)}, bf16[16,32,1152]{2,1,0:T(8,128)(2,1)S(1)}, bf16[8,32,1152]{2,1,0:T(8,128)(2,1)S(1)}, bf16[8,32,1152]{2,1,0:T(8,128)(2,1)S(1)}) custom-call(s32[144]{0:T(256)S(1)} %copy-done.18, bf16[768,640]{1,0:T(8,128)(2,1)S(1)} %copy-done.8, bf16[640,1152]{1,0:T(8,128)(2,1)S(1)} %attention_back.3.gqkv_ref, ...), custom_call_target="tpu_custom_call" | custom-call | flops 1 | bytes 1 | tf_op jit(solution)/shard_map/input_grad/pallas_call | solution.py:857
  176.5 2.0 collective-permute-done.32
  178.5 2.0 collective-permute-start.28
  181.3 2.6 %collective-permute-done.31.refs_2_ = bf16[8,24,1920]{2,1,0:T(8,128)(2,1)S(1)} collective-permute-done((bf16[8,24,1920]{2,1,0:T(8,128)(2,1)S(1)}, bf16[8,24,1920]{2,1,0:T(8,128)(2,1)S(1)}, u32[]{:S(2)}, u32[]{:S(2)}) %collective-permute-start.31) | collective-permute-done | bytes 737312 | tf_op jit(solution)/shard_map/ppermute | solution.py:514
  183.9 1.7 copy.35
  185.6 1.7 copy.36
  188.2 1.5 collective-permute-start.35
  189.7 1.8 collective-permute-done.34.refs_8_
  191.6 0.6 collective-permute-start.39
  192.3 1.9 collective-permute-done.28
  194.3 0.6 collective-permute-start.38
  195.0 2.1 collective-permute-start.44
  197.1 1.0 collective-permute-done.35.refs_3_
  198.3 3.0 %collective-permute-done.39.refs_9_ = bf16[4,32,1152]{2,1,0:T(8,128)(2,1)S(1)} collective-permute-done((bf16[4,32,1152]{2,1,0:T(8,128)(2,1)S(1)}, bf16[4,32,1152]{2,1,0:T(8,128)(2,1)S(1)}, u32[]{:S(2)}, u32[]{:S(2)}) %collective-permute-start.39) | collective-permute-done | bytes 294944 | tf_op jit(solution)/shard_map/ppermute | solution.py:514
  201.5 3.0 %collective-permute-done.38 = bf16[2,24,3072]{2,1,0:T(8,128)(2,1)S(1)} collective-permute-done((bf16[2,24,3072]{2,1,0:T(8,128)(2,1)S(1)}, bf16[2,24,3072]{2,1,0:T(8,128)(2,1)S(1)}, u32[]{:S(2)}, u32[]{:S(2)}) %collective-permute-start.38) | collective-permute-done | bytes 294944 | tf_op jit(solution)/shard_map/ppermute | solution.py:514
  205.0 2.2 collective-permute-done.37.refs_4_
  207.3 1.2 collective-permute-start.40
  208.4 3.0 %collective-permute-done.41.refs_10_ = bf16[2,32,1152]{2,1,0:T(8,128)(2,1)S(1)} collective-permute-done((bf16[2,32,1152]{2,1,0:T(8,128)(2,1)S(1)}, bf16[2,32,1152]{2,1,0:T(8,128)(2,1)S(1)}, u32[]{:S(2)}, u32[]{:S(2)}) %collective-permute-start.41) | collective-permute-done | bytes 147488 | tf_op jit(solution)/shard_map/ppermute | solution.py:514
  211.6 0.8 add_bitcast_fusion.1
  212.4 6.0 %collective-permute-done.43 = bf16[1,24,3072]{2,1,0:T(8,128)(2,1)S(1)} collective-permute-done((bf16[1,24,3072]{2,1,0:T(8,128)(2,1)S(1)}, bf16[1,24,3072]{2,1,0:T(8,128)(2,1)S(1)}, u32[]{:S(2)}, u32[]{:S(2)}) %collective-permute-start.43) | collective-permute-done | bytes 147488 | tf_op jit(solution)/shard_map/ppermute | solution.py:514
  218.4 0.8 add_bitcast_fusion
  219.3 1.1 collective-permute-done.40.refs_5_
  220.4 0.8 collective-permute-done.42.refs_11_
  221.3 1.4 last.1
  (160 shorter events, 12.0 us)
Async XLA Ops:
  3.2 1.9 collective-permute-start
  5.8 15.7 %copy-start.32 = (bf16[4,153,768]{2,0,1:T(4,128)(2,1)S(1)}, bf16[4,153,768]{2,0,1:T(4,128)(2,1)}, u32[]{:S(2)}) copy-start(bf16[4,153,768]{2,0,1:T(4,128)(2,1)} %param.31) | copy-start | bytes 2820100
  7.7 12.1 %copy-start.34 = (bf16[192,384]{1,0:T(8,128)(2,1)S(1)}, bf16[192,384]{1,0:T(8,128)(2,1)}, u32[]{:S(2)}) copy-start(bf16[192,384]{1,0:T(8,128)(2,1)} %get-tuple-element.174) | copy-start | bytes 442372
  7.7 8.8 %collective-permute-start.2 = (bf16[160,384]{1,0:T(8,128)(2,1)}, bf16[160,384]{1,0:T(8,128)(2,1)S(1)}, u32[]{:S(2)}, u32[]{:S(2)}) collective-permute-start(bf16[160,384]{1,0:T(8,128)(2,1)} %get-tuple-element.173), channel_id=1, source_target_pairs={{0,24},{1,25},{2,26},{3,27},{4,28},{5,29},{6,30},{7,31},{8,0},{9,1... | collective-permute-start | bytes 368648 | tf_op jit(solution)/shard_map/ppermute | solution.py:514
  12.5 7.3 %collective-permute-start.1 = (bf16[160,384]{1,0:T(8,128)(2,1)}, bf16[160,384]{1,0:T(8,128)(2,1)S(1)}, u32[]{:S(2)}, u32[]{:S(2)}) collective-permute-start(bf16[160,384]{1,0:T(8,128)(2,1)} %get-tuple-element.173), channel_id=1, source_target_pairs={{0,8},{1,9},{2,10},{3,11},{4,12},{5,13},{6,14},{7,15},{8,16},{9,17... | collective-permute-start | bytes 368648 | tf_op jit(solution)/shard_map/ppermute | solution.py:514
  12.5 7.3 %collective-permute-start.3 = (bf16[192,384]{1,0:T(8,128)(2,1)}, bf16[192,384]{1,0:T(8,128)(2,1)S(1)}, u32[]{:S(2)}, u32[]{:S(2)}) collective-permute-start(bf16[192,384]{1,0:T(8,128)(2,1)} %get-tuple-element.174), channel_id=1, source_target_pairs={{0,4},{1,3},{2,6},{3,1},{4,0},{5,7},{6,2},{7,5},{8,12},{9,11},{10,... | collective-permute-start | bytes 442376 | tf_op jit(solution)/shard_map/ppermute | solution.py:514
  19.8 10.8 %collective-permute-start.5 = (bf16[2,192,384]{2,1,0:T(8,128)(2,1)S(1)}, bf16[2,192,384]{2,1,0:T(8,128)(2,1)S(1)}, u32[]{:S(2)}, u32[]{:S(2)}) collective-permute-start(bf16[2,192,384]{2,1,0:T(8,128)(2,1)S(1)} %pad_maximum_fusion.3), channel_id=1, source_target_pairs={{0,2},{1,5},{2,0},{3,7},{4,6},{5,1},{6,4},{7,3},{8,10},{9,13},{10,... | collective-permute-start | bytes 884744 | tf_op jit(solution)/shard_map/ppermute | solution.py:514
  23.9 38.9 %copy-start.1 = (bf16[4,160,768]{2,1,0:T(8,128)(2,1)}, bf16[4,160,768]{2,1,0:T(8,128)(2,1)S(1)}, u32[]{:S(2)}) copy-start(bf16[4,160,768]{2,1,0:T(8,128)(2,1)S(1)} %pad.11.clone) | copy-start | bytes 2949124
  23.9 8.5 %copy-start.36 = (bf16[240,384]{1,0:T(8,128)(2,1)S(1)}, bf16[240,384]{1,0:T(8,128)(2,1)}, u32[]{:S(2)}) copy-start(bf16[240,384]{1,0:T(8,128)(2,1)} %get-tuple-element.180) | copy-start | bytes 552964
  23.9 6.7 %collective-permute-start.4 = (bf16[160,384]{1,0:T(8,128)(2,1)S(1)}, bf16[160,384]{1,0:T(8,128)(2,1)S(1)}, u32[]{:S(2)}, u32[]{:S(2)}) collective-permute-start(bf16[160,384]{1,0:T(8,128)(2,1)S(1)} %collective-permute-done.1), channel_id=1, source_target_pairs={{0,8},{1,9},{2,10},{3,11},{4,12},{5,13},{6,14},{7,15},{8,16},{9,17... | collective-permute-start | bytes 368648 | tf_op jit(solution)/shard_map/ppermute | solution.py:514
  30.7 10.7 %collective-permute-start.6 = (bf16[4,160,384]{2,1,0:T(8,128)(2,1)S(1)}, bf16[4,160,384]{2,1,0:T(8,128)(2,1)S(1)}, u32[]{:S(2)}, u32[]{:S(2)}) collective-permute-start(bf16[4,160,384]{2,1,0:T(8,128)(2,1)S(1)} %pad_maximum_fusion.2), channel_id=1, source_target_pairs={{0,4},{1,3},{2,6},{3,1},{4,0},{5,7},{6,2},{7,5},{8,12},{9,11},{10,... | collective-permute-start | bytes 1474568 | tf_op jit(solution)/shard_map/ppermute | solution.py:514
  32.4 9.0 %collective-permute-start.8 = (bf16[240,384]{1,0:T(8,128)(2,1)S(1)}, bf16[240,384]{1,0:T(8,128)(2,1)S(1)}, u32[]{:S(2)}, u32[]{:S(2)}) collective-permute-start(bf16[240,384]{1,0:T(8,128)(2,1)S(1)} %copy-done.36), channel_id=1, source_target_pairs={{0,24},{1,25},{2,26},{3,27},{4,28},{5,29},{6,30},{7,31},{8,0},{9,1... | collective-permute-start | bytes 552968 | tf_op jit(solution)/shard_map/ppermute | solution.py:514
  32.5 8.9 %collective-permute-start.7 = (bf16[240,384]{1,0:T(8,128)(2,1)S(1)}, bf16[240,384]{1,0:T(8,128)(2,1)S(1)}, u32[]{:S(2)}, u32[]{:S(2)}) collective-permute-start(bf16[240,384]{1,0:T(8,128)(2,1)S(1)} %copy-done.36), channel_id=1, source_target_pairs={{0,8},{1,9},{2,10},{3,11},{4,12},{5,13},{6,14},{7,15},{8,16},{9,17... | collective-permute-start | bytes 552968 | tf_op jit(solution)/shard_map/ppermute | solution.py:514
  41.5 21.4 %copy-start.17 = (s32[144]{0:T(256)S(1)}, s32[144]{0:T(256)}, u32[]{:S(2)}) copy-start(s32[144]{0:T(256)} %concatenate.20.place) | copy-start | bytes 1732
  41.5 18.8 %collective-permute-start.9 = (bf16[8,160,384]{2,1,0:T(8,128)(2,1)S(1)}, bf16[8,160,384]{2,1,0:T(8,128)(2,1)S(1)}, u32[]{:S(2)}, u32[]{:S(2)}) collective-permute-start(bf16[8,160,384]{2,1,0:T(8,128)(2,1)S(1)} %constant_dynamic-update-slice_fusion.own0), channel_id=1, source_target_pairs={{0,2},{1,5},{2,0},{3,7},{4,6},{5,1},{6,4},{7,3},{8,10},{9,13},{10,... | collective-permute-start | bytes 2949128 | tf_op jit(solution)/shard_map/ppermute | solution.py:514
  42.0 16.3 %collective-permute-start.11 = (bf16[4,192,384]{2,1,0:T(8,128)(2,1)S(1)}, bf16[4,192,384]{2,1,0:T(8,128)(2,1)S(1)}, u32[]{:S(2)}, u32[]{:S(2)}) collective-permute-start(bf16[4,192,384]{2,1,0:T(8,128)(2,1)S(1)} %pad_maximum_fusion.1), channel_id=1, source_target_pairs={{0,8},{1,9},{2,10},{3,11},{4,12},{5,13},{6,14},{7,15},{8,16},{9,17... | collective-permute-start | bytes 1769480 | tf_op jit(solution)/shard_map/ppermute | solution.py:514
  42.1 18.2 %collective-permute-start.10 = (bf16[240,384]{1,0:T(8,128)(2,1)S(1)}, bf16[240,384]{1,0:T(8,128)(2,1)S(1)}, u32[]{:S(2)}, u32[]{:S(2)}) collective-permute-start(bf16[240,384]{1,0:T(8,128)(2,1)S(1)} %collective-permute-done.7), channel_id=1, source_target_pairs={{0,8},{1,9},{2,10},{3,11},{4,12},{5,13},{6,14},{7,15},{8,16},{9,17... | collective-permute-start | bytes 552968 | tf_op jit(solution)/shard_map/ppermute | solution.py:514
  43.3 19.0 %collective-permute-start.12 = (bf16[8,160,384]{2,1,0:T(8,128)(2,1)S(1)}, bf16[8,160,384]{2,1,0:T(8,128)(2,1)S(1)}, u32[]{:S(2)}, u32[]{:S(2)}) collective-permute-start(bf16[8,160,384]{2,1,0:T(8,128)(2,1)S(1)} %constant_dynamic-update-slice_fusion.own0), channel_id=1, source_target_pairs={{0,1},{1,0},{2,3},{3,2},{4,5},{5,4},{6,7},{7,6},{8,9},{9,8},{10,11... | collective-permute-start | bytes 2949128 | tf_op jit(solution)/shard_map/ppermute | solution.py:514
  60.2 2.6 %collective-permute-start.13 = (bf16[8,160,384]{2,1,0:T(8,128)(2,1)S(1)}, bf16[8,160,384]{2,1,0:T(8,128)(2,1)S(1)}, u32[]{:S(2)}, u32[]{:S(2)}) collective-permute-start(bf16[8,160,384]{2,1,0:T(8,128)(2,1)S(1)} %collective-permute-done.9.own1), channel_id=1, source_target_pairs={{0,1},{1,0},{2,3},{3,2},{4,5},{5,4},{6,7},{7,6},{8,9},{9,8},{10,11... | collective-permute-start | bytes 2949128 | tf_op jit(solution)/shard_map/ppermute | solution.py:514
  60.4 15.9 %collective-permute-start.15 = (bf16[4,240,384]{2,1,0:T(8,128)(2,1)S(1)}, bf16[4,240,384]{2,1,0:T(8,128)(2,1)S(1)}, u32[]{:S(2)}, u32[]{:S(2)}) collective-permute-start(bf16[4,240,384]{2,1,0:T(8,128)(2,1)S(1)} %pad_maximum_fusion), channel_id=1, source_target_pairs={{0,4},{1,3},{2,6},{3,1},{4,0},{5,7},{6,2},{7,5},{8,12},{9,11},{10,... | collective-permute-start | bytes 2211848 | tf_op jit(solution)/shard_map/ppermute | solution.py:514
  62.2 14.1 %collective-permute-start.14 = (bf16[4,192,384]{2,1,0:T(8,128)(2,1)S(1)}, bf16[4,192,384]{2,1,0:T(8,128)(2,1)S(1)}, u32[]{:S(2)}, u32[]{:S(2)}) collective-permute-start(bf16[4,192,384]{2,1,0:T(8,128)(2,1)S(1)} %pad_maximum_fusion.1), channel_id=1, source_target_pairs={{0,24},{1,25},{2,26},{3,27},{4,28},{5,29},{6,30},{7,31},{8,0},{9,1... | collective-permute-start | bytes 1769480 | tf_op jit(solution)/shard_map/ppermute | solution.py:514
  76.5 19.6 %copy-start.21 = (bf16[8,240,384]{2,1,0:T(8,128)(2,1)}, bf16[8,240,384]{2,1,0:T(8,128)(2,1)S(1)}, u32[]{:S(2)}) copy-start(bf16[8,240,384]{2,1,0:T(8,128)(2,1)S(1)} %constant_dynamic-update-slice_fusion.7.b0) | copy-start | bytes 4423684
  76.5 19.5 %collective-permute-start.18 = (bf16[8,240,384]{2,1,0:T(8,128)(2,1)S(1)}, bf16[8,240,384]{2,1,0:T(8,128)(2,1)S(1)}, u32[]{:S(2)}, u32[]{:S(2)}) collective-permute-start(bf16[8,240,384]{2,1,0:T(8,128)(2,1)S(1)} %constant_dynamic-update-slice_fusion.7.b0), channel_id=1, source_target_pairs={{0,2},{1,5},{2,0},{3,7},{4,6},{5,1},{6,4},{7,3},{8,10},{9,13},{10,... | collective-permute-start | bytes 4423688 | tf_op jit(solution)/shard_map/ppermute | solution.py:514
  78.4 6.6 %copy-start.23 = (bf16[8,192,384]{2,1,0:T(8,128)(2,1)}, bf16[8,192,384]{2,1,0:T(8,128)(2,1)S(1)}, u32[]{:S(2)}) copy-start(bf16[8,192,384]{2,1,0:T(8,128)(2,1)S(1)} %constant_dynamic-update-slice_fusion.5.a0) | copy-start | bytes 3538948
  78.5 17.6 %collective-permute-start.17 = (bf16[8,192,384]{2,1,0:T(8,128)(2,1)S(1)}, bf16[8,192,384]{2,1,0:T(8,128)(2,1)S(1)}, u32[]{:S(2)}, u32[]{:S(2)}) collective-permute-start(bf16[8,192,384]{2,1,0:T(8,128)(2,1)S(1)} %constant_dynamic-update-slice_fusion.5.a0), channel_id=1, source_target_pairs={{0,1},{1,0},{2,3},{3,2},{4,5},{5,4},{6,7},{7,6},{8,9},{9,8},{10,11... | collective-permute-start | bytes 3538952 | tf_op jit(solution)/shard_map/ppermute | solution.py:514
  78.5 17.5 %collective-permute-start.16 = (bf16[4,192,384]{2,1,0:T(8,128)(2,1)S(1)}, bf16[4,192,384]{2,1,0:T(8,128)(2,1)S(1)}, u32[]{:S(2)}, u32[]{:S(2)}) collective-permute-start(bf16[4,192,384]{2,1,0:T(8,128)(2,1)S(1)} %collective-permute-done.11), channel_id=1, source_target_pairs={{0,8},{1,9},{2,10},{3,11},{4,12},{5,13},{6,14},{7,15},{8,16},{9,17... | collective-permute-start | bytes 1769480 | tf_op jit(solution)/shard_map/ppermute | solution.py:514
  85.1 11.8 %copy-start.3 = (bf16[640,768]{1,0:T(8,128)(2,1)}, bf16[640,768]{1,0:T(8,128)(2,1)S(1)}, u32[]{:S(2)}) copy-start(bf16[640,768]{1,0:T(8,128)(2,1)S(1)} %attention.1.att_far.att_ref) | copy-start | bytes 2949124
  96.1 7.1 %copy-start.26 = (bf16[8,240,384]{2,1,0:T(8,128)(2,1)}, bf16[8,240,384]{2,1,0:T(8,128)(2,1)S(1)}, u32[]{:S(2)}) copy-start(bf16[8,240,384]{2,1,0:T(8,128)(2,1)S(1)} %collective-permute-done.18.b1) | copy-start | bytes 4423684
  96.1 7.1 %collective-permute-start.20 = (bf16[8,240,384]{2,1,0:T(8,128)(2,1)S(1)}, bf16[8,240,384]{2,1,0:T(8,128)(2,1)S(1)}, u32[]{:S(2)}, u32[]{:S(2)}) collective-permute-start(bf16[8,240,384]{2,1,0:T(8,128)(2,1)S(1)} %constant_dynamic-update-slice_fusion.7.b0), channel_id=1, source_target_pairs={{0,1},{1,0},{2,3},{3,2},{4,5},{5,4},{6,7},{7,6},{8,9},{9,8},{10,11... | collective-permute-start | bytes 4423688 | tf_op jit(solution)/shard_map/ppermute | solution.py:514
  96.2 7.1 %collective-permute-start.21 = (bf16[8,240,384]{2,1,0:T(8,128)(2,1)S(1)}, bf16[8,240,384]{2,1,0:T(8,128)(2,1)S(1)}, u32[]{:S(2)}, u32[]{:S(2)}) collective-permute-start(bf16[8,240,384]{2,1,0:T(8,128)(2,1)S(1)} %collective-permute-done.18.b1), channel_id=1, source_target_pairs={{0,1},{1,0},{2,3},{3,2},{4,5},{5,4},{6,7},{7,6},{8,9},{9,8},{10,11... | collective-permute-start | bytes 4423688 | tf_op jit(solution)/shard_map/ppermute | solution.py:514
  97.1 8.4 %copy-start.22 = (bf16[8,192,384]{2,1,0:T(8,128)(2,1)}, bf16[8,192,384]{2,1,0:T(8,128)(2,1)S(1)}, u32[]{:S(2)}) copy-start(bf16[8,192,384]{2,1,0:T(8,128)(2,1)S(1)} %constant_dynamic-update-slice_fusion.9.a1) | copy-start | bytes 3538948
  97.1 6.1 %collective-permute-start.19 = (bf16[8,192,384]{2,1,0:T(8,128)(2,1)S(1)}, bf16[8,192,384]{2,1,0:T(8,128)(2,1)S(1)}, u32[]{:S(2)}, u32[]{:S(2)}) collective-permute-start(bf16[8,192,384]{2,1,0:T(8,128)(2,1)S(1)} %constant_dynamic-update-slice_fusion.9.a1), channel_id=1, source_target_pairs={{0,1},{1,0},{2,3},{3,2},{4,5},{5,4},{6,7},{7,6},{8,9},{9,8},{10,11... | collective-permute-start | bytes 3538952 | tf_op jit(solution)/shard_map/ppermute | solution.py:514
  140.1 3.1 %collective-permute-start.22 = (bf16[8,96,768]{2,1,0:T(8,128)(2,1)}, bf16[8,96,768]{2,1,0:T(8,128)(2,1)S(1)}, u32[]{:S(2)}, u32[]{:S(2)}) collective-permute-start(bf16[8,96,768]{2,1,0:T(8,128)(2,1)} %get-tuple-element.211), channel_id=1, source_target_pairs={{0,1},{1,0},{2,3},{3,2},{4,5},{5,4},{6,7},{7,6},{8,9},{9,8},{10,11... | collective-permute-start | bytes 3538952 | tf_op jit(solution)/shard_map/ppermute | solution.py:514
  145.0 8.9 %collective-permute-start.23 = (bf16[16,24,3072]{2,1,0:T(8,128)(2,1)}, bf16[16,24,3072]{2,1,0:T(8,128)(2,1)S(1)}, u32[]{:S(2)}, u32[]{:S(2)}) collective-permute-start(bf16[16,24,3072]{2,1,0:T(8,128)(2,1)} %get-tuple-element.212), channel_id=1, source_target_pairs={{0,1},{1,0},{2,3},{3,2},{4,5},{5,4},{6,7},{7,6},{8,9},{9,8},{10,11... | collective-permute-start | bytes 7077896 | tf_op jit(solution)/shard_map/ppermute | solution.py:514
  145.2 15.1 %collective-permute-start.25 = (bf16[8,96,768]{2,1,0:T(8,128)(2,1)}, bf16[8,96,768]{2,1,0:T(8,128)(2,1)S(1)}, u32[]{:S(2)}, u32[]{:S(2)}) collective-permute-start(bf16[8,96,768]{2,1,0:T(8,128)(2,1)} %get-tuple-element.220), channel_id=1, source_target_pairs={{0,1},{1,0},{2,3},{3,2},{4,5},{5,4},{6,7},{7,6},{8,9},{9,8},{10,11... | collective-permute-start | bytes 3538952 | tf_op jit(solution)/shard_map/ppermute | solution.py:514
  145.6 16.2 %collective-permute-start.26 = (bf16[8,96,768]{2,1,0:T(8,128)(2,1)S(1)}, bf16[8,96,768]{2,1,0:T(8,128)(2,1)S(1)}, u32[]{:S(2)}, u32[]{:S(2)}) collective-permute-start(bf16[8,96,768]{2,1,0:T(8,128)(2,1)S(1)} %add_convert_fusion.1), channel_id=1, source_target_pairs={{0,2},{1,5},{2,0},{3,7},{4,6},{5,1},{6,4},{7,3},{8,10},{9,13},{10,... | collective-permute-start | bytes 3538952 | tf_op jit(solution)/shard_map/ppermute | solution.py:514
  147.1 6.8 %copy-start.4 = (bf16[640,768]{1,0:T(8,128)(2,1)S(1)}, bf16[640,768]{1,0:T(8,128)(2,1)}, u32[]{:S(2)}) copy-start(bf16[640,768]{1,0:T(8,128)(2,1)} %copy-done.3) | copy-start | bytes 2949124
  147.1 6.8 %copy-start.8 = (bf16[768,640]{1,0:T(8,128)(2,1)S(1)}, bf16[768,640]{1,0:T(8,128)(2,1)}, u32[]{:S(2)}) copy-start(bf16[768,640]{1,0:T(8,128)(2,1)} %copy-done.7) | copy-start | bytes 2949124
  147.1 6.8 %copy-start.13 = (bf16[768,1152]{1,0:T(8,128)(2,1)S(1)}, bf16[768,1152]{1,0:T(8,128)(2,1)}, u32[]{:S(2)}) copy-start(bf16[768,1152]{1,0:T(8,128)(2,1)} %copy-done.12) | copy-start | bytes 5308420
  147.1 6.8 %copy-start.18 = (s32[144]{0:T(256)S(1)}, s32[144]{0:T(256)}, u32[]{:S(2)}) copy-start(s32[144]{0:T(256)} %concatenate.20.place) | copy-start | bytes 1732
  159.2 2.5 %collective-permute-start.27 = (bf16[8,24,1920]{2,1,0:T(8,128)(2,1)S(1)}, bf16[8,24,1920]{2,1,0:T(8,128)(2,1)S(1)}, u32[]{:S(2)}, u32[]{:S(2)}) collective-permute-start(bf16[8,24,1920]{2,1,0:T(8,128)(2,1)S(1)} %get-tuple-element.223), channel_id=1, source_target_pairs={{0,1},{1,0},{2,3},{3,2},{4,5},{5,4},{6,7},{7,6},{8,9},{9,8},{10,11... | collective-permute-start | bytes 2211848 | tf_op jit(solution)/shard_map/ppermute | solution.py:514
  159.7 16.4 %collective-permute-start.24 = (bf16[8,24,3072]{2,1,0:T(8,128)(2,1)S(1)}, bf16[8,24,3072]{2,1,0:T(8,128)(2,1)S(1)}, u32[]{:S(2)}, u32[]{:S(2)}) collective-permute-start(bf16[8,24,3072]{2,1,0:T(8,128)(2,1)S(1)} %add_convert_fusion), channel_id=1, source_target_pairs={{0,2},{1,5},{2,0},{3,7},{4,6},{5,1},{6,4},{7,3},{8,10},{9,13},{10,... | collective-permute-start | bytes 3538952 | tf_op jit(solution)/shard_map/ppermute | solution.py:514
  162.0 18.7 %collective-permute-start.29 = (bf16[4,96,768]{2,1,0:T(8,128)(2,1)S(1)}, bf16[4,96,768]{2,1,0:T(8,128)(2,1)S(1)}, u32[]{:S(2)}, u32[]{:S(2)}) collective-permute-start(bf16[4,96,768]{2,1,0:T(8,128)(2,1)S(1)} %add_convert_fusion.5), channel_id=1, source_target_pairs={{0,8},{1,9},{2,10},{3,11},{4,12},{5,13},{6,14},{7,15},{8,0},{9,1},... | collective-permute-start | bytes 1769480 | tf_op jit(solution)/shard_map/ppermute | solution.py:514
  162.3 8.1 %copy-start.2 = (bf16[4,160,768]{2,1,0:T(8,128)(2,1)S(1)}, bf16[4,160,768]{2,1,0:T(8,128)(2,1)}, u32[]{:S(2)}) copy-start(bf16[4,160,768]{2,1,0:T(8,128)(2,1)} %copy-done.1) | copy-start | bytes 2949124
  162.3 8.1 %copy-start.15 = (f32[2,16,384]{2,1,0:T(8,128)S(1)}, f32[2,16,384]{2,1,0:T(8,128)}, u32[]{:S(2)}) copy-start(f32[2,16,384]{2,1,0:T(8,128)} %copy-done.14) | copy-start | bytes 147460
  162.3 8.1 %copy-start.16 = (f32[4,8,768]{2,1,0:T(8,128)S(1)}, f32[4,8,768]{2,1,0:T(8,128)}, u32[]{:S(2)}) copy-start(f32[4,8,768]{2,1,0:T(8,128)} %get-tuple-element.235.fcg_ref) | copy-start | bytes 294916
  162.3 8.1 %copy-start.19 = (f32[8,768]{1,0:T(8,128)S(1)}, f32[8,768]{1,0:T(8,128)}, u32[]{:S(2)}) copy-start(f32[8,768]{1,0:T(8,128)} %get-tuple-element.234.mlp_ref) | copy-start | bytes 73732
  162.3 21.6 %collective-permute-start.31 = (bf16[8,24,1920]{2,1,0:T(8,128)(2,1)S(1)}, bf16[8,24,1920]{2,1,0:T(8,128)(2,1)S(1)}, u32[]{:S(2)}, u32[]{:S(2)}) collective-permute-start(bf16[8,24,1920]{2,1,0:T(8,128)(2,1)S(1)} %add_convert_fusion.2), channel_id=1, source_target_pairs={{0,2},{1,5},{2,0},{3,7},{4,6},{5,1},{6,4},{7,3},{8,10},{9,13},{10,... | collective-permute-start | bytes 2211848 | tf_op jit(solution)/shard_map/ppermute | solution.py:514
  175.6 14.1 %collective-permute-start.33 = (bf16[8,32,1152]{2,1,0:T(8,128)(2,1)S(1)}, bf16[8,32,1152]{2,1,0:T(8,128)(2,1)S(1)}, u32[]{:S(2)}, u32[]{:S(2)}) collective-permute-start(bf16[8,32,1152]{2,1,0:T(8,128)(2,1)S(1)} %get-tuple-element.259), channel_id=1, source_target_pairs={{0,1},{1,0},{2,3},{3,2},{4,5},{5,4},{6,7},{7,6},{8,9},{9,8},{10,11... | collective-permute-start | bytes 1769480 | tf_op jit(solution)/shard_map/ppermute | solution.py:514
  175.7 2.8 %collective-permute-start.32 = (bf16[8,32,1152]{2,1,0:T(8,128)(2,1)S(1)}, bf16[8,32,1152]{2,1,0:T(8,128)(2,1)S(1)}, u32[]{:S(2)}, u32[]{:S(2)}) collective-permute-start(bf16[8,32,1152]{2,1,0:T(8,128)(2,1)S(1)} %get-tuple-element.244), channel_id=1, source_target_pairs={{0,1},{1,0},{2,3},{3,2},{4,5},{5,4},{6,7},{7,6},{8,9},{9,8},{10,11... | collective-permute-start | bytes 1769480 | tf_op jit(solution)/shard_map/ppermute | solution.py:514
  176.2 5.1 %collective-permute-start.30 = (bf16[8,24,1920]{2,1,0:T(8,128)(2,1)S(1)}, bf16[8,24,1920]{2,1,0:T(8,128)(2,1)S(1)}, u32[]{:S(2)}, u32[]{:S(2)}) collective-permute-start(bf16[8,24,1920]{2,1,0:T(8,128)(2,1)S(1)} %get-tuple-element.241), channel_id=1, source_target_pairs={{0,1},{1,0},{2,3},{3,2},{4,5},{5,4},{6,7},{7,6},{8,9},{9,8},{10,11... | collective-permute-start | bytes 2211848 | tf_op jit(solution)/shard_map/ppermute | solution.py:514
  176.5 7.5 %copy-start.31 = (bf16[640,768]{1,0:T(8,128)(2,1)S(1)}, bf16[640,768]{1,0:T(8,128)(2,1)}, u32[]{:S(2)}) copy-start(bf16[640,768]{1,0:T(8,128)(2,1)} %get-tuple-element.254) | copy-start | bytes 2949124
  178.5 15.6 %collective-permute-start.28 = (bf16[4,24,3072]{2,1,0:T(8,128)(2,1)S(1)}, bf16[4,24,3072]{2,1,0:T(8,128)(2,1)S(1)}, u32[]{:S(2)}, u32[]{:S(2)}) collective-permute-start(bf16[4,24,3072]{2,1,0:T(8,128)(2,1)S(1)} %add_convert_fusion.4), channel_id=1, source_target_pairs={{0,8},{1,9},{2,10},{3,11},{4,12},{5,13},{6,14},{7,15},{8,0},{9,1},... | collective-permute-start | bytes 1769480 | tf_op jit(solution)/shard_map/ppermute | solution.py:514
  180.7 10.8 %collective-permute-start.34 = (bf16[8,32,1152]{2,1,0:T(8,128)(2,1)S(1)}, bf16[8,32,1152]{2,1,0:T(8,128)(2,1)S(1)}, u32[]{:S(2)}, u32[]{:S(2)}) collective-permute-start(bf16[8,32,1152]{2,1,0:T(8,128)(2,1)S(1)} %add_convert_fusion.3), channel_id=1, source_target_pairs={{0,2},{1,5},{2,0},{3,7},{4,6},{5,1},{6,4},{7,3},{8,10},{9,13},{10,... | collective-permute-start | bytes 1769480 | tf_op jit(solution)/shard_map/ppermute | solution.py:514
  187.4 7.5 %collective-permute-start.36 = (bf16[2,96,768]{2,1,0:T(8,128)(2,1)S(1)}, bf16[2,96,768]{2,1,0:T(8,128)(2,1)S(1)}, u32[]{:S(2)}, u32[]{:S(2)}) collective-permute-start(bf16[2,96,768]{2,1,0:T(8,128)(2,1)S(1)} %add_convert_fusion.9), channel_id=1, source_target_pairs={{0,4},{1,3},{2,6},{3,1},{4,0},{5,7},{6,2},{7,5},{8,12},{9,11},{10,... | collective-permute-start | bytes 884744 | tf_op jit(solution)/shard_map/ppermute | solution.py:514
  188.2 10.0 %collective-permute-start.35 = (bf16[4,24,1920]{2,1,0:T(8,128)(2,1)S(1)}, bf16[4,24,1920]{2,1,0:T(8,128)(2,1)S(1)}, u32[]{:S(2)}, u32[]{:S(2)}) collective-permute-start(bf16[4,24,1920]{2,1,0:T(8,128)(2,1)S(1)} %add_convert_fusion.6), channel_id=1, source_target_pairs={{0,4},{1,3},{2,6},{3,1},{4,0},{5,7},{6,2},{7,5},{8,12},{9,11},{10,... | collective-permute-start | bytes 1105928 | tf_op jit(solution)/shard_map/ppermute | solution.py:514
  191.6 9.7 %collective-permute-start.39 = (bf16[4,32,1152]{2,1,0:T(8,128)(2,1)S(1)}, bf16[4,32,1152]{2,1,0:T(8,128)(2,1)S(1)}, u32[]{:S(2)}, u32[]{:S(2)}) collective-permute-start(bf16[4,32,1152]{2,1,0:T(8,128)(2,1)S(1)} %add_convert_fusion.8), channel_id=1, source_target_pairs={{0,4},{1,3},{2,6},{3,1},{4,0},{5,7},{6,2},{7,5},{8,12},{9,11},{10,... | collective-permute-start | bytes 884744 | tf_op jit(solution)/shard_map/ppermute | solution.py:514
  194.3 10.2 %collective-permute-start.38 = (bf16[2,24,3072]{2,1,0:T(8,128)(2,1)S(1)}, bf16[2,24,3072]{2,1,0:T(8,128)(2,1)S(1)}, u32[]{:S(2)}, u32[]{:S(2)}) collective-permute-start(bf16[2,24,3072]{2,1,0:T(8,128)(2,1)S(1)} %add_convert_fusion.7), channel_id=1, source_target_pairs={{0,4},{1,3},{2,6},{3,1},{4,0},{5,7},{6,2},{7,5},{8,12},{9,11},{10,... | collective-permute-start | bytes 884744 | tf_op jit(solution)/shard_map/ppermute | solution.py:514
  195.0 16.5 %collective-permute-start.44 = (bf16[1,96,768]{2,1,0:T(8,128)(2,1)S(1)}, bf16[1,96,768]{2,1,0:T(8,128)(2,1)S(1)}, u32[]{:S(2)}, u32[]{:S(2)}) collective-permute-start(bf16[1,96,768]{2,1,0:T(8,128)(2,1)S(1)} %add_convert_fusion.13), channel_id=1, source_target_pairs={{0,16},{1,17},{2,18},{3,19},{4,20},{5,21},{6,22},{7,23},{8,24},{9,... | collective-permute-start | bytes 442376 | tf_op jit(solution)/shard_map/ppermute | solution.py:514
  198.2 9.0 %collective-permute-start.37 = (bf16[2,24,1920]{2,1,0:T(8,128)(2,1)S(1)}, bf16[2,24,1920]{2,1,0:T(8,128)(2,1)S(1)}, u32[]{:S(2)}, u32[]{:S(2)}) collective-permute-start(bf16[2,24,1920]{2,1,0:T(8,128)(2,1)S(1)} %add_convert_fusion.10), channel_id=1, source_target_pairs={{0,8},{1,9},{2,10},{3,11},{4,12},{5,13},{6,14},{7,15},{8,0},{9,1},... | collective-permute-start | bytes 552968 | tf_op jit(solution)/shard_map/ppermute | solution.py:514
  201.4 10.1 %collective-permute-start.41 = (bf16[2,32,1152]{2,1,0:T(8,128)(2,1)S(1)}, bf16[2,32,1152]{2,1,0:T(8,128)(2,1)S(1)}, u32[]{:S(2)}, u32[]{:S(2)}) collective-permute-start(bf16[2,32,1152]{2,1,0:T(8,128)(2,1)S(1)} %add_convert_fusion.12), channel_id=1, source_target_pairs={{0,8},{1,9},{2,10},{3,11},{4,12},{5,13},{6,14},{7,15},{8,0},{9,1},... | collective-permute-start | bytes 442376 | tf_op jit(solution)/shard_map/ppermute | solution.py:514
  204.5 13.9 %collective-permute-start.43 = (bf16[1,24,3072]{2,1,0:T(8,128)(2,1)S(1)}, bf16[1,24,3072]{2,1,0:T(8,128)(2,1)S(1)}, u32[]{:S(2)}, u32[]{:S(2)}) collective-permute-start(bf16[1,24,3072]{2,1,0:T(8,128)(2,1)S(1)} %add_convert_fusion.11), channel_id=1, source_target_pairs={{0,16},{1,17},{2,18},{3,19},{4,20},{5,21},{6,22},{7,23},{8,24},{9,... | collective-permute-start | bytes 442376 | tf_op jit(solution)/shard_map/ppermute | solution.py:514
  207.3 13.1 %collective-permute-start.40 = (bf16[1,24,1920]{2,1,0:T(8,128)(2,1)S(1)}, bf16[1,24,1920]{2,1,0:T(8,128)(2,1)S(1)}, u32[]{:S(2)}, u32[]{:S(2)}) collective-permute-start(bf16[1,24,1920]{2,1,0:T(8,128)(2,1)S(1)} %add_convert_fusion.14), channel_id=1, source_target_pairs={{0,16},{1,17},{2,18},{3,19},{4,20},{5,21},{6,22},{7,23},{8,24},{9,... | collective-permute-start | bytes 276488 | tf_op jit(solution)/shard_map/ppermute | solution.py:514
  211.5 9.7 %collective-permute-start.42 = (bf16[1,32,1152]{2,1,0:T(8,128)(2,1)S(1)}, bf16[1,32,1152]{2,1,0:T(8,128)(2,1)S(1)}, u32[]{:S(2)}, u32[]{:S(2)}) collective-permute-start(bf16[1,32,1152]{2,1,0:T(8,128)(2,1)S(1)} %add_convert_fusion.15), channel_id=1, source_target_pairs={{0,16},{1,17},{2,18},{3,19},{4,20},{5,21},{6,22},{7,23},{8,24},{9,... | collective-permute-start | bytes 221192 | tf_op jit(solution)/shard_map/ppermute | solution.py:514
  (19 other events, 59.2 us)
